TPU v7x, 512 devices: a whole 4x4x16 slice. The times are simulated.
512 devices in a mesh: rep: 16 (over x, z_hi, core), tab: 32 (over y, z_lo).
Axes of the slice: x: 4, y: 4, z: 16 (z_hi: 2, z_lo: 8; z = z_hi * 8 + z_lo), core: 2. Of those that a mesh axis runs over, the one named last changes fastest.
Arguments:
- bottom_out: bfloat16 [65536, 128], P(('rep', 'tab')), may hold values from -1.5 to 1.5
- pooled: bfloat16 [65536, 32, 128], P(('rep', 'tab')), may hold values from -1.5 to 1.5
- top_grad: bfloat16 [65536, 512], P(('rep', 'tab')), may hold values from -6 to 6
- top_weight: bfloat16 [656, 512], replicated, may hold values from -0.25 to 0.25
- core_first: bfloat16 [32, 128, 256], P('tab'), may hold values from -4 to 4
- core_mid: bfloat16 [32, 16, 64, 256], P('tab'), may hold values from -0.75 to 0.75
- core_last: bfloat16 [32, 128, 512], P('tab'), may hold values from -0.75 to 0.75
- digit_first: int32 [32, 65536], P('tab', 'rep'), may hold values from 0 to 127
- digit_last: int32 [32, 65536], P('tab', 'rep'), may hold values from 0 to 127
- grouped: int32 [32, 16, 4096], P('tab', 'rep'), may hold values from 0 to 4095, each once within a row
Outputs:
- grad_first: float32 [32, 128, 256], P('tab', 'rep')
- grad_mid: float32 [32, 16, 64, 256], P('tab', 'rep')
- grad_last: float32 [32, 128, 512], P('tab', 'rep')
- grad_top: bfloat16 [656, 512], replicated
- grad_bottom: bfloat16 [65536, 128], P(('rep', 'tab'))
Inputs may be any that keep to these rules, and one draw needn't show every extreme that they name: `grouped`: for each table and rep group, a permutation of the 4096 positions of that group's samples; the sample at position p has second digit p // 256, so every second digit has exactly 256 samples in each rep group.
All inputs are finite; a program needn't handle non-finite values.
Results may differ from a plain program's by a relative error of at most 0.017.
Values may be sent and summed in bfloat16 or wider, within the bound.
No kernel may reach another device: no remote copies, remote signals or barrier semaphores. Data moves between devices by JAX's collectives and lax.ppermute only.
A program may use at most 64 MiB of HBM per device.

v0:
```python
import jax
import jax.numpy as jnp
import numpy as np
from jax import lax
from jax.sharding import PartitionSpec as P

D1 = 4
D2 = 4
D3 = 8
R = 64
I1 = 128
I2 = 16
I3 = 128


def core_partials(received, order, first_digit, third_digit, core_one, core_two, core_three):
    samples = received.shape[0]
    group = samples // I2
    slots_one = jnp.arange(I1, dtype=jnp.int32)[:, None]
    slots_three = jnp.arange(I3, dtype=jnp.int32)[:, None]

    def step(carry, inputs):
        acc_one, acc_three = carry
        index, mid_core = inputs
        picked = lax.dynamic_slice_in_dim(order, index * group, group)
        grad_block = received[picked].reshape(group, D1, D2, D3)
        first = first_digit[picked]
        third = third_digit[picked]
        left_core = core_one[first].reshape(group * D1, R)
        right_core = core_three[third].reshape(group, D3, R)
        inner = jnp.einsum(
            "nabc,ncs->nabs", grad_block, right_core, preferred_element_type=jnp.float32
        ).astype(jnp.bfloat16)
        inner = inner.reshape(group * D1, D2 * R)
        grad_two = lax.dot_general(
            left_core, inner, (((0,), (0,)), ((), ())), preferred_element_type=jnp.float32
        )
        back_first = lax.dot_general(
            inner, mid_core, (((1,), (1,)), ((), ())), preferred_element_type=jnp.float32
        )
        back_first = back_first.astype(jnp.bfloat16).reshape(group, D1 * R)
        chained = jnp.dot(left_core, mid_core, preferred_element_type=jnp.float32).astype(
            jnp.bfloat16
        )
        chained = chained.reshape(group, D1, D2, R)
        back_last = jnp.einsum(
            "nabc,nabs->ncs", grad_block, chained, preferred_element_type=jnp.float32
        )
        back_last = back_last.astype(jnp.bfloat16).reshape(group, D3 * R)
        onehot_one = (first[None, :] == slots_one).astype(jnp.bfloat16)
        onehot_three = (third[None, :] == slots_three).astype(jnp.bfloat16)
        acc_one = acc_one + jnp.dot(onehot_one, back_first, preferred_element_type=jnp.float32)
        acc_three = acc_three + jnp.dot(onehot_three, back_last, preferred_element_type=jnp.float32)
        return ((acc_one, acc_three), grad_two)

    start = (jnp.zeros((I1, D1 * R), jnp.float32), jnp.zeros((I3, D3 * R), jnp.float32))
    (acc_one, acc_three), grad_two = lax.scan(
        step, start, (jnp.arange(I2, dtype=jnp.int32), core_two)
    )
    return (acc_one, grad_two, acc_three)


def on_device(
    bottom_out,
    pooled,
    top_grad,
    top_weight,
    core_first,
    core_mid,
    core_last,
    digit_first,
    digit_last,
    grouped,
):
    samples = bottom_out.shape[0]
    tables = pooled.shape[1]
    count = tables + 1
    width = bottom_out.shape[1]
    lower_rows, lower_cols = np.tril_indices(count, -1)
    batch_all = samples * lax.axis_size("rep") * lax.axis_size("tab")
    scale = jnp.float32(1.0 / np.sqrt(batch_all))
    features = jnp.concatenate([bottom_out[:, None, :], pooled], axis=1)
    gram = jnp.einsum("bid,bjd->bij", features, features, preferred_element_type=jnp.float32)
    pairs = gram[:, lower_rows, lower_cols]
    inputs = jnp.concatenate([bottom_out.astype(jnp.float32), pairs], axis=1).astype(jnp.bfloat16)
    grad_inputs = lax.dot_general(
        top_grad, top_weight, (((1,), (1,)), ((), ())), preferred_element_type=jnp.float32
    )
    sym = jnp.zeros((samples, count, count), jnp.float32)
    sym = sym.at[:, lower_rows, lower_cols].set(grad_inputs[:, width:])
    sym = sym + jnp.swapaxes(sym, 1, 2)
    grad_features = jnp.einsum(
        "bij,bjd->bid", sym, features.astype(jnp.float32), precision=lax.Precision.HIGHEST
    )
    grad_bottom = (grad_inputs[:, :width] + grad_features[:, 0]).astype(jnp.bfloat16)
    grad_rows = grad_features[:, 1:].astype(jnp.bfloat16)
    received = lax.all_to_all(grad_rows, "tab", split_axis=1, concat_axis=0, tiled=True)
    received = received.reshape(received.shape[0], width)
    acc_one, grad_two, acc_three = core_partials(
        received,
        grouped[0, 0],
        digit_first[0],
        digit_last[0],
        core_first[0],
        core_mid[0],
        core_last[0],
    )
    grad_one, grad_two, grad_three = (
        lax.psum_scatter(
            (scale * acc_one).astype(jnp.bfloat16), "rep", scatter_dimension=0, tiled=True
        ).astype(jnp.float32),
        lax.psum_scatter(
            (scale * grad_two).astype(jnp.bfloat16), "rep", scatter_dimension=0, tiled=True
        ).astype(jnp.float32),
        lax.psum_scatter(
            (scale * acc_three).astype(jnp.bfloat16), "rep", scatter_dimension=0, tiled=True
        ).astype(jnp.float32),
    )
    dense_term = scale * lax.dot_general(
        inputs, top_grad, (((0,), (0,)), ((), ())), preferred_element_type=jnp.float32
    )
    grad_top = lax.psum(dense_term, ("rep", "tab")).astype(jnp.bfloat16)
    return (grad_one[None], grad_two[None], grad_three[None], grad_top, grad_bottom)


def solution(mesh):
    return jax.shard_map(
        on_device,
        mesh=mesh,
        in_specs=(
            P(("rep", "tab"), None),
            P(("rep", "tab"), None, None),
            P(("rep", "tab"), None),
            P(),
            P("tab", None, None),
            P("tab", None, None, None),
            P("tab", None, None),
            P("tab", "rep"),
            P("tab", "rep"),
            P("tab", "rep", None),
        ),
        out_specs=(
            P("tab", "rep", None),
            P("tab", "rep", None, None),
            P("tab", "rep", None),
            P(),
            P(("rep", "tab"), None),
        ),
        check_vma=False,
    )
```

profile of v0, /device:TPU:1, one launch (start us, length us, event | category | flops | bytes accessed | tf_op | source)
XLA Modules:
  0.0 735.3 jit_solution(11646684961836317187)
XLA Ops:
  10.3 28.0 %scatter_fusion = f32[128,33,33]{0,2,1:T(8,128)S(1)} fusion(f32[128,33,33]{0,2,1:T(8,128)S(1)} %broadcast_in_dim.69, s32[528]{0:T(1024)S(1)} %copy-done.5, f32[528,128]{1,0:T(8,128)S(1)} %slice_bitcast_fusion), kind=kCustom, calls=%fused_computation.6 | custom fusion | bytes 815232 | tf_op jit(solution)/shard_map/scatter | solution.py:90
  39.2 2.2 copy.49
  41.5 3.9 fusion.13
  48.6 16.2 %all-to-all-start = ((bf16[128,32,128]{2,0,1:T(8,128)(2,1)}), bf16[128,32,128]{2,0,1:T(8,128)(2,1)}, u32[]{:S(2)}, u32[]{:S(2)}) async-start(bf16[128,32,128]{2,0,1:T(8,128)(2,1)} %copy.50), calls=%async_computation | async-start | bytes 2097152 | tf_op jit(solution)/shard_map/all_to_all | solution.py:97
  68.0 2.6 fusion.12
  70.6 1.7 copy.51
  72.3 7.0 gather_fusion.5
  80.8 34.4 %all-to-all-done = bf16[128,32,128]{2,0,1:T(8,128)(2,1)} async-done(((bf16[128,32,128]{2,0,1:T(8,128)(2,1)}), bf16[128,32,128]{2,0,1:T(8,128)(2,1)}, u32[]{:S(2)}, u32[]{:S(2)}) %all-to-all-start) | async-done | bytes 1048608 | tf_op jit(solution)/shard_map/all_to_all | solution.py:97
  115.2 332.7 %while.17 = (s32[]{:T(128)}, f32[128,256]{1,0:T(8,128)}, f32[128,512]{1,0:T(8,128)}, f32[16,64,256]{2,1,0:T(8,128)}, s32[16]{0:T(128)S(1)}, /*index=5*/s32[4096]...) while((s32[]{:T(128)}, f32[128,256]{1,0:T(8,128)}, ...), condition=%wide.region_2.3_spmd.clone.clone, body=%wide.region_1.2_spmd.clone.clone.sunk | while | flops 160371968 | bytes 11699990 | solution.py:57
  120.6 2.1 gather_fusion
  125.0 1.7 gather_fusion.3
  140.5 2.1 gather_fusion
  154.1 1.9 convolution_add_fusion.5
  161.3 2.1 gather_fusion
  165.7 1.7 gather_fusion.3
  174.9 1.9 convolution_add_fusion.5
  182.2 2.1 gather_fusion
  195.8 1.9 convolution_add_fusion.5
  203.0 2.1 gather_fusion
  216.6 1.9 convolution_add_fusion.5
  223.9 2.1 gather_fusion
  228.3 1.7 gather_fusion.3
  237.5 1.9 convolution_add_fusion.5
  244.8 2.1 gather_fusion
  258.3 1.9 convolution_add_fusion.5
  265.6 2.1 gather_fusion
  279.2 1.9 convolution_add_fusion.5
  286.5 2.1 gather_fusion
  290.8 1.7 gather_fusion.3
  300.0 1.9 convolution_add_fusion.5
  307.3 2.1 gather_fusion
  320.9 1.9 convolution_add_fusion.5
  328.2 2.1 gather_fusion
  341.7 1.9 convolution_add_fusion.5
  349.0 2.1 gather_fusion
  362.6 1.9 convolution_add_fusion.5
  369.9 2.1 gather_fusion
  383.4 1.9 convolution_add_fusion.5
  390.7 2.1 gather_fusion
  404.3 1.9 convolution_add_fusion.5
  411.6 2.1 gather_fusion
  425.1 1.9 convolution_add_fusion.5
  432.4 2.1 gather_fusion
  446.0 1.9 convolution_add_fusion.5
  451.3 2.1 multiply_convert_fusion
  453.4 108.9 %all-reduce.1 = bf16[656,512]{1,0:T(8,128)(2,1)} all-reduce(f32[656,512]{1,0:T(8,128)S(1)} %copy-done.6), channel_id=1, replica_groups=mesh['rep'=16,'tab'=32] {'rep','tab'}, use_global_device_ids=true, to_apply=%region_6.7 | all-reduce | flops 335872 | bytes 2015232 | tf_op jit(solution)/shard_map/psum | solution.py:122
  563.6 66.0 %reduce-scatter.8.cloned.1.call-done = bf16[8,512]{1,0:T(8,128)(2,1)} async-done(((bf16[128,512]{1,0:T(8,128)(2,1)}), bf16[8,512]{1,0:T(8,128)(2,1)}) %reduce-scatter.8.cloned.1.call-update) | async-done | bytes 8208 | tf_op jit(solution)/shard_map/reduce_scatter | solution.py:115
  630.9 96.5 %reduce-scatter.6.cloned.1.call-done = bf16[1,64,256]{2,1,0:T(8,128)(2,1)} async-done(((bf16[16,64,256]{2,1,0:T(8,128)(2,1)}), bf16[1,64,256]{2,1,0:T(8,128)(2,1)}) %reduce-scatter.6.cloned.1.call-update) | async-done | bytes 32784 | tf_op jit(solution)/shard_map/reduce_scatter | solution.py:112
  (544 shorter events, 269.8 us)
Async XLA Ops:
  7.2 1.1 copy-start
  7.2 3.1 copy-start.5
  9.5 0.7 copy-start.10
  39.2 2.2 copy-start.12
  45.4 1.5 copy-start.7
  48.6 66.6 %all-to-all-start = ((bf16[128,32,128]{2,0,1:T(8,128)(2,1)}), bf16[128,32,128]{2,0,1:T(8,128)(2,1)}, u32[]{:S(2)}, u32[]{:S(2)}) async-start(bf16[128,32,128]{2,0,1:T(8,128)(2,1)} %copy.50), calls=%async_computation | async-start | bytes 2097152 | tf_op jit(solution)/shard_map/all_to_all | solution.py:97
  64.8 497.5 %reduce-scatter.4.cloned.1.call-start = ((), (), s32[]{:S(2)}) async-start(), calls=%async_computation.4 | async-start | bytes 69632 | tf_op jit(solution)/shard_map/reduce_scatter | solution.py:109
  70.5 8.8 %copy-start.11 = (bf16[128,512]{1,0:T(8,128)(2,1)S(1)}, bf16[128,512]{1,0:T(8,128)(2,1)}, u32[]{:S(2)}) copy-start(bf16[128,512]{1,0:T(8,128)(2,1)} %param.20) | copy-start | bytes 393220
  72.3 42.9 %copy-start.1 = (s32[1,4096]{1,0:T(1,128)S(1)}, s32[1,4096]{1,0:T(1,128)}, u32[]{:S(2)}) copy-start(s32[1,4096]{1,0:T(1,128)} %param.25) | copy-start | bytes 49156
  72.3 42.9 %copy-start.2 = (s32[1,4096]{1,0:T(1,128)S(1)}, s32[1,4096]{1,0:T(1,128)}, u32[]{:S(2)}) copy-start(s32[1,4096]{1,0:T(1,128)} %param.26) | copy-start | bytes 49156
  72.3 42.9 %copy-start.3 = (bf16[1,128,512]{2,1,0:T(8,128)(2,1)S(1)}, bf16[1,128,512]{2,1,0:T(8,128)(2,1)}, u32[]{:S(2)}) copy-start(bf16[1,128,512]{2,1,0:T(8,128)(2,1)} %param.24) | copy-start | bytes 393220
  72.3 42.9 %copy-start.4 = (bf16[1,128,256]{2,1,0:T(8,128)(2,1)S(1)}, bf16[1,128,256]{2,1,0:T(8,128)(2,1)}, u32[]{:S(2)}) copy-start(bf16[1,128,256]{2,1,0:T(8,128)(2,1)} %param.22) | copy-start | bytes 196612
  127.9 2.5 copy-start.8
  130.6 0.7 copy-start.9
  147.8 2.5 copy-start.8
  150.5 0.7 copy-start.9
  168.6 2.5 copy-start.8
  171.3 0.7 copy-start.9
  189.5 2.5 copy-start.8
  192.2 0.7 copy-start.9
  210.3 2.5 copy-start.8
  213.0 0.7 copy-start.9
  231.2 2.5 copy-start.8
  233.9 0.7 copy-start.9
  252.0 2.5 copy-start.8
  254.7 0.7 copy-start.9
  272.9 2.5 copy-start.8
  275.6 0.7 copy-start.9
  293.7 2.5 copy-start.8
  296.4 0.7 copy-start.9
  314.6 2.5 copy-start.8
  317.3 0.7 copy-start.9
  335.4 2.5 copy-start.8
  338.1 0.7 copy-start.9
  356.3 2.5 copy-start.8
  359.0 0.7 copy-start.9
  377.1 2.5 copy-start.8
  379.8 0.7 copy-start.9
  398.0 2.5 copy-start.8
  400.7 0.7 copy-start.9
  418.8 2.5 copy-start.8
  421.5 0.7 copy-start.9
  439.7 2.5 copy-start.8
  442.4 0.7 copy-start.9
  449.4 4.0 copy-start.6
  449.4 180.2 %reduce-scatter.8.cloned.1.call-start = ((), (), s32[]{:S(2)}) async-start(), calls=%async_computation.6 | async-start | bytes 139264 | tf_op jit(solution)/shard_map/reduce_scatter | solution.py:115
  451.2 276.2 %reduce-scatter.6.cloned.1.call-start = ((), (), s32[]{:S(2)}) async-start(), calls=%async_computation.5 | async-start | bytes 557056 | tf_op jit(solution)/shard_map/reduce_scatter | solution.py:112
Sparse Core Ops, SparseCore 0:
  449.6 88.1 reduce-scatter.3
  542.3 87.2 reduce-scatter.7
  634.9 92.3 reduce-scatter.5
where the time goes:
time: 740 us; the launch traced here: 735 us
  local copies, waits for them, and re-layouts  245 us (33%)
  waiting for transfers between devices  197 us (27%)
  matrix products  116 us (16%)
  blocking collectives  109 us (15%)
  other arithmetic  23.9 us (3%)
  starting transfers between devices  16.5 us (2%)
  between operations  14 us (2%)
  loops' own time  13.3 us (2%)
    psum x1, blocking collectives, on_device(): grad_top = lax.psum(dense_term, ('rep', 'tab')).astype(jnp.bfloat16)  109 us
    reduce_scatter x1, waiting for transfers between devices, on_device(): lax.psum_scatter((scale * grad_two).astype(jnp.bfloat16), 'rep', scatter_...  96.5 us
    reduce_scatter x1, waiting for transfers between devices, on_device(): lax.psum_scatter((scale * acc_three).astype(jnp.bfloat16), 'rep', scatter...  66 us
    gather x32, local copies, waits for them, and re-layouts, step(): grad_block = received[picked].reshape(group, D1, D2, D3)  35.1 us
    all_to_all x1, waiting for transfers between devices, on_device(): lax.all_to_all(grad_rows, 'tab', split_axis=1, concat_axis=0, tiled=True)  34.4 us
    dot_general x16, matrix products, step(): jnp.dot(onehot_three, back_last, preferred_element_type=jnp.float32)  29.4 us
    scatter x1, local copies, waits for them, and re-layouts, on_device(): sym = sym.at[:, lower_rows, lower_cols].set(grad_inputs[:, width:])  28 us
    gather x16, local copies, waits for them, and re-layouts, step(): first = first_digit[picked]  27.6 us
  transfers between devices with their start and end apart: 4, of which 3 were waited for; matrix products, arithmetic and copies ran while one was open for 3% of the time, Pallas kernels for 0%

commit v1 on v0

v1 whole, which is shorter than its diff:
```python
import jax
import jax.numpy as jnp
import numpy as np
from jax import lax
from jax.experimental import pallas as pl
from jax.experimental.pallas import tpu as pltpu
from jax.sharding import PartitionSpec as P

D1 = 4
D2 = 4
D3 = 8
R = 64
I1 = 128
I2 = 16
I3 = 128
LANES = 128
SUB = 8
BF = jnp.bfloat16
F32 = jnp.float32
NT = (((1,), (1,)), ((), ()))
TN = (((0,), (0,)), ((), ()))
NN = (((1,), (0,)), ((), ()))


def pair(i, j):
    low, high = min(i, j), max(i, j)
    return high * (high - 1) // 2 + low


def dense_kernel(count, bottom_ref, pooled_ref, grad_ref, weight_ref, rows_ref, gbottom_ref, feat_ref, wide, feat, gi, out):
    samples, width = bottom_ref.shape
    tables = count - 1
    gi[...] = lax.dot_general(weight_ref[...], grad_ref[...], NT, preferred_element_type=F32)
    wide[...] = pooled_ref[...].astype(F32)
    feat[0] = bottom_ref[...].astype(F32).T
    for t in range(tables):
        feat[1 + t] = wide[pl.ds(t, samples, stride=tables), :].T
    feat_ref[...] = feat[...].astype(BF)

    def chunk(step, carry):
        at = pl.ds(pl.multiple_of(step * SUB, SUB), SUB)
        parts = [feat[j, at, :] for j in range(count)]
        for i in range(count):
            total = None
            for j in range(count):
                if j != i:
                    row = gi[pl.ds(width + pair(i, j), 1), :]
                    term = jnp.broadcast_to(row, (SUB, samples)) * parts[j]
                    total = term if total is None else total + term
            out[i, at, :] = total
        return carry

    lax.fori_loop(0, width // SUB, chunk, 0)
    gbottom_ref[...] = (out[0] + gi[pl.ds(0, width), :]).T.astype(BF)
    for t in range(tables):
        rows_ref[t] = out[1 + t].T.astype(BF)


def gram_kernel(count, scale, feat_ref, grad_ref, top_ref, feat, pairs):
    width, samples = feat_ref.shape[1:]
    feat[...] = feat_ref[...].astype(F32)
    for i0 in range(0, count, 4):
        for j0 in range(0, count, 8):
            todo = [(i, j) for i in range(i0, min(i0 + 4, count)) for j in range(j0, min(j0 + 8, count)) if j < i]
            if not todo:
                continue
            used = sorted({i for one in todo for i in one})

            def chunk(step, totals, todo=todo, used=used):
                at = pl.ds(pl.multiple_of(step * SUB, SUB), SUB)
                parts = {i: feat[i, at, :] for i in used}
                return tuple(total + parts[i] * parts[j] for total, (i, j) in zip(totals, todo))

            zero = jnp.zeros((SUB, samples), F32)
            totals = lax.fori_loop(0, width // SUB, chunk, (zero,) * len(todo), unroll=2)
            for total, (i, j) in zip(totals, todo):
                pairs[pl.ds(pair(i, j), 1), :] = jnp.sum(total, axis=0, keepdims=True)
    top_ref[:width] = scale * lax.dot_general(feat_ref[0], grad_ref[...], NN, preferred_element_type=F32)
    top_ref[width:] = scale * lax.dot_general(pairs[...].astype(BF), grad_ref[...], NN, preferred_element_type=F32)


def digits_kernel(order_ref, first_ref, last_ref, sorted_ref):
    order = order_ref[...]
    both = first_ref[...] * I3 + last_ref[...]
    row, lane = order // LANES, order % LANES
    total = jnp.zeros(order.shape, jnp.int32)
    for r in range(order.shape[0]):
        spread = jnp.broadcast_to(both[r : r + 1], order.shape)
        total = jnp.where(row == r, jnp.take_along_axis(spread, lane, axis=1), total)
    sorted_ref[...] = total


def onehot(digit, slots):
    lanes = digit.shape[1]
    return jnp.where(lax.broadcasted_iota(jnp.int32, (slots, lanes), 0) == digit, 1.0, 0.0).astype(BF)


def digits_of(sorted_ref, group):
    rows = group // LANES
    at = sorted_ref[pl.ds(pl.program_id(0) * rows, rows), :]
    at = jnp.concatenate([at[r : r + 1] for r in range(rows)], axis=1)
    return at // I3, at % I3


def before_kernel(sorted_ref, one_ref, mid_ref, three_ref, left_ref, right_ref, chained_ref):
    group = left_ref.shape[1]
    first, third = digits_of(sorted_ref, group)
    left = lax.dot_general(one_ref[...], onehot(first, I1), NN, preferred_element_type=F32).astype(BF)
    left_ref[...] = left
    right_ref[...] = lax.dot_general(three_ref[...], onehot(third, I3), NN, preferred_element_type=F32).astype(BF)
    for a in range(D1):
        chained = lax.dot_general(mid_ref[0], left[a * R : (a + 1) * R], TN, preferred_element_type=F32)
        chained_ref[a * D2 * R : (a + 1) * D2 * R] = chained.astype(BF)


def after_kernel(scale, order_ref, sorted_ref, received_ref, left_ref, right_ref, chained_ref, mid_ref, one_ref, two_ref, three_ref, wide, picked, gt, inner, back, acc_one, acc_three, right_wide, chained_wide):
    k = pl.program_id(0)
    groups = pl.num_programs(0)
    group = left_ref.shape[1]
    steps = (R // SUB) * (group // LANES)
    share = group // steps

    def fetch(slot, base, begin, number):
        for n in range(number):
            picked[slot, pl.ds(begin + n, 1), :] = wide[pl.ds(order_ref[base + begin + n], 1), :]

    @pl.when(k == 0)
    def _():
        wide[...] = received_ref[...].astype(F32)
        acc_one[...] = jnp.zeros_like(acc_one)
        acc_three[...] = jnp.zeros_like(acc_three)

        def one(step, carry):
            fetch(0, 0, step * share, share)
            return carry

        lax.fori_loop(0, steps, one, 0)

    slot = k % 2
    later = jnp.minimum(k + 1, groups - 1) * group
    gt[...] = picked[slot].T
    right_wide[...] = right_ref[...].astype(F32)
    chained_wide[...] = chained_ref[...].astype(F32)

    def chunk(step, carry):
        fetch(1 - slot, later, step * share, share)
        half = step // (R // SUB)
        lanes = pl.ds(pl.multiple_of(half * LANES, LANES), LANES)
        low = (step % (R // SUB)) * SUB
        rights = [right_wide[pl.ds(pl.multiple_of(c * R + low, SUB), SUB), lanes] for c in range(D3)]
        totals = [None] * D3
        for j in range(D1 * D2):
            at = pl.ds(pl.multiple_of(j * R + low, SUB), SUB)
            link = chained_wide[at, lanes]
            total = None
            for c in range(D3):
                g = jnp.broadcast_to(gt[pl.ds(j * D3 + c, 1), lanes], (SUB, LANES))
                term = g * rights[c]
                total = term if total is None else total + term
                term = g * link
                totals[c] = term if totals[c] is None else totals[c] + term
            inner[at, lanes] = total
        for c in range(D3):
            back[pl.ds(pl.multiple_of(c * R + low, SUB), SUB), lanes] = totals[c]
        return carry

    lax.fori_loop(0, steps, chunk, 0)
    first, third = digits_of(sorted_ref, group)
    inner_all = inner[...].astype(BF)
    two = None
    firsts = []
    for a in range(D1):
        part = inner_all[a * D2 * R : (a + 1) * D2 * R]
        term = lax.dot_general(left_ref[a * R : (a + 1) * R], part, NT, preferred_element_type=F32)
        two = term if two is None else two + term
        firsts.append(lax.dot_general(mid_ref[0], part, NN, preferred_element_type=F32).astype(BF))
    two_ref[0] = (scale * two).astype(BF)
    back_first = jnp.concatenate(firsts, axis=0)
    acc_one[...] += lax.dot_general(onehot(first, I1), back_first, NT, preferred_element_type=F32)
    acc_three[...] += lax.dot_general(onehot(third, I3), back[...].astype(BF), NT, preferred_element_type=F32)

    @pl.when(k == groups - 1)
    def _():
        one_ref[...] = (scale * acc_one[...]).astype(BF)
        three_ref[...] = (scale * acc_three[...]).astype(BF)


def whole(shape):
    return pl.BlockSpec(shape, lambda *a: (0,) * len(shape))


def dense(bottom_out, pooled, top_grad, top_weight):
    samples, width = bottom_out.shape
    tables = pooled.shape[1]
    count = tables + 1
    return pl.pallas_call(
        lambda *refs: dense_kernel(count, *refs),
        out_shape=(
            jax.ShapeDtypeStruct((tables, samples, width), BF),
            jax.ShapeDtypeStruct((samples, width), BF),
            jax.ShapeDtypeStruct((count, width, samples), BF),
        ),
        scratch_shapes=[
            pltpu.VMEM((samples * tables, width), F32),
            pltpu.VMEM((count, width, samples), F32),
            pltpu.VMEM((top_weight.shape[0], samples), F32),
            pltpu.VMEM((count, width, samples), F32),
        ],
        compiler_params=pltpu.CompilerParams(vmem_limit_bytes=48 << 20),
        name="dense",
    )(bottom_out, pooled.reshape(samples * tables, width), top_grad, top_weight)


def gram(feat, top_grad, scale):
    count, width, samples = feat.shape
    pairs = count * (count - 1) // 2
    return pl.pallas_call(
        lambda *refs: gram_kernel(count, scale, *refs),
        out_shape=jax.ShapeDtypeStruct((width + pairs, top_grad.shape[1]), F32),
        scratch_shapes=[pltpu.VMEM((count, width, samples), F32), pltpu.VMEM((pairs, samples), F32)],
        compiler_params=pltpu.CompilerParams(vmem_limit_bytes=48 << 20),
        name="gram",
    )(feat, top_grad)


def before(order, first, last, core_one, core_two, core_three):
    total = order.shape[0]
    group = total // I2
    table = (total // LANES, LANES)
    sorted_digits = pl.pallas_call(
        digits_kernel, out_shape=jax.ShapeDtypeStruct(table, jnp.int32), name="digits"
    )(order.reshape(table), first.reshape(table), last.reshape(table))
    links = pl.pallas_call(
        before_kernel,
        grid=(I2,),
        in_specs=[
            whole(table),
            whole((D1 * R, I1)),
            pl.BlockSpec((1, R, D2 * R), lambda k: (k, 0, 0)),
            whole((D3 * R, I3)),
        ],
        out_specs=(
            pl.BlockSpec((D1 * R, group), lambda k: (0, k)),
            pl.BlockSpec((D3 * R, group), lambda k: (0, k)),
            pl.BlockSpec((D1 * D2 * R, group), lambda k: (0, k)),
        ),
        out_shape=(
            jax.ShapeDtypeStruct((D1 * R, total), BF),
            jax.ShapeDtypeStruct((D3 * R, total), BF),
            jax.ShapeDtypeStruct((D1 * D2 * R, total), BF),
        ),
        compiler_params=pltpu.CompilerParams(vmem_limit_bytes=48 << 20),
        name="before",
    )(sorted_digits, core_one.T, core_two, core_three.T)
    return sorted_digits, links


def after(received, order, sorted_digits, links, core_two, scale):
    total, width = received.shape
    group = total // I2
    left, right, chained = links
    return pl.pallas_call(
        lambda *refs: after_kernel(scale, *refs),
        grid_spec=pltpu.PrefetchScalarGridSpec(
            num_scalar_prefetch=1,
            grid=(I2,),
            in_specs=[
                whole(sorted_digits.shape),
                whole((total, width)),
                pl.BlockSpec((D1 * R, group), lambda k, o: (0, k)),
                pl.BlockSpec((D3 * R, group), lambda k, o: (0, k)),
                pl.BlockSpec((D1 * D2 * R, group), lambda k, o: (0, k)),
                pl.BlockSpec((1, R, D2 * R), lambda k, o: (k, 0, 0)),
            ],
            out_specs=(
                whole((I1, D1 * R)),
                pl.BlockSpec((1, R, D2 * R), lambda k, o: (k, 0, 0)),
                whole((I3, D3 * R)),
            ),
            scratch_shapes=[
                pltpu.VMEM((total, width), F32),
                pltpu.VMEM((2, group, width), F32),
                pltpu.VMEM((width, group), F32),
                pltpu.VMEM((D1 * D2 * R, group), F32),
                pltpu.VMEM((D3 * R, group), F32),
                pltpu.VMEM((I1, D1 * R), F32),
                pltpu.VMEM((I3, D3 * R), F32),
                pltpu.VMEM((D3 * R, group), F32),
                pltpu.VMEM((D1 * D2 * R, group), F32),
            ],
        ),
        out_shape=(
            jax.ShapeDtypeStruct((I1, D1 * R), BF),
            jax.ShapeDtypeStruct((I2, R, D2 * R), BF),
            jax.ShapeDtypeStruct((I3, D3 * R), BF),
        ),
        compiler_params=pltpu.CompilerParams(vmem_limit_bytes=48 << 20),
        name="after",
    )(order, sorted_digits, received, left, right, chained, core_two)


def scatter_sum(array):
    return lax.psum_scatter(array, "rep", scatter_dimension=0, tiled=True)


def on_device(
    bottom_out,
    pooled,
    top_grad,
    top_weight,
    core_first,
    core_mid,
    core_last,
    digit_first,
    digit_last,
    grouped,
):
    samples, width = bottom_out.shape
    reps = lax.axis_size("rep")
    batch_all = samples * reps * lax.axis_size("tab")
    scale = float(np.float32(1.0 / np.sqrt(batch_all)))
    grad_rows, grad_bottom, feat = dense(bottom_out, pooled, top_grad, top_weight)
    received = lax.all_to_all(grad_rows, "tab", split_axis=0, concat_axis=0, tiled=True)
    dense_term = gram(feat, top_grad, scale)
    grad_top = lax.psum(dense_term, ("rep", "tab")).astype(BF)
    order = grouped[0, 0]
    sorted_digits, links = before(
        order, digit_first[0], digit_last[0], core_first[0], core_mid[0], core_last[0]
    )
    one, two, three = after(
        received.reshape(-1, width), order, sorted_digits, links, core_mid[0], scale
    )
    parts = jnp.concatenate(
        [one.reshape(reps, -1, LANES), two.reshape(reps, -1, LANES), three.reshape(reps, -1, LANES)],
        axis=1,
    )
    share = scatter_sum(parts.reshape(-1, LANES)).astype(F32)
    size_one = I1 * D1 * R // reps // LANES
    size_two = I2 * R * D2 * R // reps // LANES
    grad_one = share[:size_one].reshape(1, I1 // reps, D1 * R)
    grad_two = share[size_one : size_one + size_two].reshape(1, I2 // reps, R, D2 * R)
    grad_three = share[size_one + size_two :].reshape(1, I3 // reps, D3 * R)
    return (grad_one, grad_two, grad_three, grad_top, grad_bottom)


def solution(mesh):
    return jax.shard_map(
        on_device,
        mesh=mesh,
        in_specs=(
            P(("rep", "tab"), None),
            P(("rep", "tab"), None, None),
            P(("rep", "tab"), None),
            P(),
            P("tab", None, None),
            P("tab", None, None, None),
            P("tab", None, None),
            P("tab", "rep"),
            P("tab", "rep"),
            P("tab", "rep", None),
        ),
        out_specs=(
            P("tab", "rep", None),
            P("tab", "rep", None, None),
            P("tab", "rep", None),
            P(),
            P(("rep", "tab"), None),
        ),
        check_vma=False,
    )
```

time: 740 us -> 262 us (0.35)
  local copies, waits for them, and re-layouts: 245 us -> 13.9 us
  waiting for transfers between devices: 197 us -> 34 us
  matrix products: 116 us -> 0 us
  Pallas kernels: 0 us -> 66.6 us
  other arithmetic: 23.9 us -> 0.92 us
  loops' own time: 13.3 us -> 0 us
    reduce_scatter x3 -> x1, waiting for transfers between devices: 162 us -> 0.01 us  [scatter_sum(): return lax.psum_scatter(array, 'rep', scatter_dimension=0, tiled=True)]
    gather x113 -> x0, local copies, waits for them, and re-layouts: 136 us -> none  [the longest x32 35.1 us: step(): grad_block = received[picked].reshape(group, D1, D2, D3)]
    dot_general x116 -> x0, matrix products: 116 us -> none  [the longest x16 29.4 us: step(): jnp.dot(onehot_three, back_last, preferred_element_type=jnp.float32)]
    pallas_call x0 -> x5, Pallas kernels: none -> 66.6 us  [the longest x1 39.3 us: after(): pl.pallas_call(lambda *refs: after_kernel(scale, *refs), grid_spec=pltpu....]
    reshape x96 -> x6, local copies, waits for them, and re-layouts: 42.5 us -> 2.15 us  [the longest x1 0.65 us: on_device(): share[size_one:size_one + size_two].reshape(1, I2 // reps, R, D2 * R)]
    scatter x1 -> x0, local copies, waits for them, and re-layouts: 28 us -> none  [on_device(): sym = sym.at[:, lower_rows, lower_cols].set(grad_inputs[:, width:])]
    another operation x1 -> x0, loops' own time: 13.3 us -> none  [core_partials(): lax.scan(step, start, (jnp.arange(I2, dtype=jnp.int32), core_two))]
    select_n x48 -> x0, other arithmetic: 12.4 us -> none  [the longest x16 12.3 us: step(): first = first_digit[picked]]
  transfers between devices with their start and end apart: 4 -> 2, of which waited for: 3 -> 1; matrix products, arithmetic and copies ran while one was open for 3% -> 0% of each run, Pallas kernels for 0% -> 7%
where the time goes in v1:
time: 262 us; the launch traced here: 261 us
  blocking collectives  115 us (44%)
  Pallas kernels  66.6 us (25%)
  waiting for transfers between devices  34 us (13%)
  starting transfers between devices  16.3 us (6%)
  between operations  14.1 us (5%)
  local copies, waits for them, and re-layouts  13.9 us (5%)
    psum x1, blocking collectives, on_device(): grad_top = lax.psum(dense_term, ('rep', 'tab')).astype(BF)  115 us
    pallas_call x1, Pallas kernels, after(): pl.pallas_call(lambda *refs: after_kernel(scale, *refs), grid_spec=pltpu....  39.3 us
    all_to_all x1, waiting for transfers between devices, on_device(): lax.all_to_all(grad_rows, 'tab', split_axis=0, concat_axis=0, tiled=True)  34 us
    all_to_all x1, starting transfers between devices, on_device(): lax.all_to_all(grad_rows, 'tab', split_axis=0, concat_axis=0, tiled=True)  16.2 us
    pallas_call x1, Pallas kernels, before(): pl.pallas_call(before_kernel, grid=(I2,), in_specs=[whole(table), whole((...  12.2 us
    unnamed x30, local copies, waits for them, and re-layouts  9.57 us
    pallas_call x1, Pallas kernels, dense(): pl.pallas_call(lambda *refs: dense_kernel(count, *refs), out_shape=(jax.S...  8.17 us
  transfers between devices with their start and end apart: 2, of which 1 were waited for; matrix products, arithmetic and copies ran while one was open for 0% of the time, Pallas kernels for 7%

profile of v1, /device:TPU:1, one launch (start us, length us, event | category | flops | bytes accessed | tf_op | source)
XLA Modules:
  0.0 261.1 jit_solution(7589968046469943637)
XLA Ops:
  7.2 0.0 copy-start.3
  7.2 1.2 copy-done.3
  8.4 0.0 copy-start.5
  8.4 1.1 copy-done.5
  9.5 0.9 copy-done.6
  10.4 0.0 copy-start.11
  10.4 0.8 copy-done.11
  11.1 8.2 %dense.1 = (bf16[32,128,128]{2,1,0:T(8,128)(2,1)S(1)}, bf16[128,128]{1,0:T(8,128)(2,1)}, bf16[33,128,128]{2,1,0:T(8,128)(2,1)S(1)}) custom-call(bf16[128,128]{1,0:T(8,128)(2,1)S(1)} %copy-done.11, bf16[4096,128]{1,0:T(8,128)(2,1)S(1)} %bitcast.17, bf16[128,512]{1,0:T(8,128)(2,1)S(1)} %copy-done.6, bf16[656,512]{1,0:T(8,128)(2,1)S(1)} %copy-done.5), custom_call_target="tpu_custom_call" | custom-call | tf_op jit(solution)/shard_map/dense/pallas_call | solution.py:196
  19.3 0.0 copy-start.4
  19.3 1.0 copy-done.4
  20.3 0.0 copy-start.13
  20.3 0.0 copy-start.12
  20.3 0.0 copy-start.10
  20.3 16.2 %all-to-all-start = ((bf16[32,128,128]{2,1,0:T(8,128)(2,1)}), bf16[32,128,128]{2,1,0:T(8,128)(2,1)S(1)}, u32[]{:S(2)}, u32[]{:S(2)}) async-start(bf16[32,128,128]{2,1,0:T(8,128)(2,1)} %copy-done.4), calls=%async_computation | async-start | bytes 2097152 | tf_op jit(solution)/shard_map/all_to_all | solution.py:323
  36.6 0.0 reduce-scatter.2.cloned.1.call-start
  36.6 0.0 copy-done.13
  36.6 0.1 copy.15
  36.7 0.0 copy-done.12
  36.7 0.1 copy.16
  36.9 1.8 digits.1.sorted_ref.refs_1_
  38.7 0.0 copy-done
  38.7 0.0 copy-start.8
  38.7 0.7 copy-done.8
  39.4 12.2 %before.1 = (bf16[256,4096]{1,0:T(8,128)(2,1)S(1)}, bf16[512,4096]{1,0:T(8,128)(2,1)}, bf16[1024,4096]{1,0:T(8,128)(2,1)}) custom-call(s32[32,128]{1,0:T(8,128)S(1)} %copy-done.8, bf16[256,128]{1,0:T(8,128)(2,1)S(1)} %bitcast.19, bf16[16,64,256]{2,1,0:T(8,128)(2,1)S(1)} %bitcast.15, bf16[512,128]{1,0:T(8,128)(2,1)S(1)} %bitcast.18), custom_call_target="tpu_custom_call" | custom-call | tf_op jit(solution)/shard_map/before/pallas_call | solution.py:233
  51.6 0.0 copy-start.1
  51.6 1.3 copy-done.1
  52.9 34.0 %all-to-all-done = bf16[32,128,128]{2,1,0:T(8,128)(2,1)S(1)} async-done(((bf16[32,128,128]{2,1,0:T(8,128)(2,1)}), bf16[32,128,128]{2,1,0:T(8,128)(2,1)S(1)}, u32[]{:S(2)}, u32[]{:S(2)}) %all-to-all-start) | async-done | bytes 1048608 | tf_op jit(solution)/shard_map/all_to_all | solution.py:323
  86.9 0.0 copy-done.10
  86.9 0.0 copy-start.2
  87.0 1.6 copy-done.2
  88.5 0.0 copy-start.9
  88.5 0.7 copy-done.9
  89.3 39.3 %after.1 = (bf16[128,256]{1,0:T(8,128)(2,1)S(1)}, bf16[16,64,256]{2,1,0:T(8,128)(2,1)S(1)}, bf16[128,512]{1,0:T(8,128)(2,1)S(1)}) custom-call(s32[4096]{0:T(1024)S(1)} %bitcast.21, s32[32,128]{1,0:T(8,128)S(1)} %copy-done.9, bf16[4096,128]{1,0:T(8,128)(2,1)S(1)} %bitcast.14, bf16[256,4096]{1,0:T(8,128)(2,1)S(1)} %copy-done.2, ...), custom_call_target="tpu_custom_call" | custom-call | tf_op jit(solution)/shard_map/after/pallas_call | solution.py:262
  128.6 0.1 reshape.41
  128.7 0.0 copy-start.7
  128.7 0.2 reshape.40
  128.9 0.9 pad_maximum_fusion
  129.9 0.0 reduce-scatter.2.cloned.1.call-update
  129.9 0.0 copy-done.7
  129.9 5.1 %gram.1 = f32[656,512]{1,0:T(8,128)S(1)} custom-call(bf16[33,128,128]{2,1,0:T(8,128)(2,1)S(1)} %get-tuple-element.21.refs_0_, bf16[128,512]{1,0:T(8,128)(2,1)S(1)} %copy-done.7), custom_call_target="tpu_custom_call" | custom-call | tf_op jit(solution)/shard_map/gram/pallas_call | solution.py:217
  135.0 115.3 %all-reduce.1 = bf16[656,512]{1,0:T(8,128)(2,1)} all-reduce(f32[656,512]{1,0:T(8,128)S(1)} %gram.1), channel_id=1, replica_groups=mesh['rep'=16,'tab'=32] {'rep','tab'}, use_global_device_ids=true, to_apply=%region_1.0 | all-reduce | flops 335872 | bytes 2015232 | tf_op jit(solution)/shard_map/psum | solution.py:325
  250.3 0.0 reduce-scatter.2.cloned.1.call-done
  250.3 0.7 slice.12
  251.0 0.6 reshape.43
  251.6 0.8 slice.13
  252.3 0.6 reshape.44
  253.0 0.7 slice.14
  253.7 0.6 reshape.45
  (3 shorter events, 0.0 us)
Async XLA Ops:
  7.2 1.2 copy-start.3
  8.4 1.1 copy-start.5
  9.5 0.9 copy-start.6
  10.4 0.8 copy-start.11
  19.3 1.0 copy-start.4
  20.3 16.3 %copy-start.13 = (bf16[1,128,256]{2,1,0:T(8,128)(2,1)S(1)}, bf16[1,128,256]{2,1,0:T(8,128)(2,1)}, u32[]{:S(2)}) copy-start(bf16[1,128,256]{2,1,0:T(8,128)(2,1)} %param.14) | copy-start | bytes 196612
  20.3 16.4 %copy-start.12 = (bf16[1,128,512]{2,1,0:T(8,128)(2,1)S(1)}, bf16[1,128,512]{2,1,0:T(8,128)(2,1)}, u32[]{:S(2)}) copy-start(bf16[1,128,512]{2,1,0:T(8,128)(2,1)} %param.16) | copy-start | bytes 393220
  20.3 18.4 %copy-start = (bf16[1,16,64,256]{3,2,1,0:T(8,128)(2,1)S(1)}, bf16[1,16,64,256]{3,2,1,0:T(8,128)(2,1)}, u32[]{:S(2)}) copy-start(bf16[1,16,64,256]{3,2,1,0:T(8,128)(2,1)} %param.15) | copy-start | bytes 1572868
  20.3 66.6 %copy-start.10 = (s32[1,1,4096]{2,1,0:T(1,128)S(1)}, s32[1,1,4096]{2,1,0:T(1,128)}, u32[]{:S(2)}) copy-start(s32[1,1,4096]{2,1,0:T(1,128)} %param.19) | copy-start | bytes 49156
  20.3 66.6 %all-to-all-start = ((bf16[32,128,128]{2,1,0:T(8,128)(2,1)}), bf16[32,128,128]{2,1,0:T(8,128)(2,1)S(1)}, u32[]{:S(2)}, u32[]{:S(2)}) async-start(bf16[32,128,128]{2,1,0:T(8,128)(2,1)} %copy-done.4), calls=%async_computation | async-start | bytes 2097152 | tf_op jit(solution)/shard_map/all_to_all | solution.py:323
  36.6 213.7 %reduce-scatter.2.cloned.1.call-start = ((), (), s32[]{:S(2)}) async-start(), calls=%async_computation.2 | async-start | bytes 765952 | tf_op jit(solution)/shard_map/reduce_scatter | solution.py:303
  38.7 0.7 copy-start.8
  51.6 1.3 copy-start.1
  86.9 1.6 copy-start.2
  88.5 0.7 copy-start.9
  128.7 1.2 copy-start.7
Sparse Core Ops, SparseCore 0:
  130.0 98.0 reduce-scatter.1

commit v2 on v1

--- a/solution.py
+++ b/solution.py
@@ -56,7 +56,7 @@
         rows_ref[t] = out[1 + t].T.astype(BF)
 
 
-def gram_kernel(count, scale, feat_ref, grad_ref, top_ref, feat, pairs):
+def gram_kernel(count, scale, at_ref, feat_ref, grad_ref, keep_ref, send_ref, feat, pairs, top):
     width, samples = feat_ref.shape[1:]
     feat[...] = feat_ref[...].astype(F32)
     for i0 in range(0, count, 4):
@@ -75,8 +75,55 @@
             totals = lax.fori_loop(0, width // SUB, chunk, (zero,) * len(todo), unroll=2)
             for total, (i, j) in zip(totals, todo):
                 pairs[pl.ds(pair(i, j), 1), :] = jnp.sum(total, axis=0, keepdims=True)
-    top_ref[:width] = scale * lax.dot_general(feat_ref[0], grad_ref[...], NN, preferred_element_type=F32)
-    top_ref[width:] = scale * lax.dot_general(pairs[...].astype(BF), grad_ref[...], NN, preferred_element_type=F32)
+    top[:width] = scale * lax.dot_general(feat_ref[0], grad_ref[...], NN, preferred_element_type=F32)
+    top[width:] = scale * lax.dot_general(pairs[...].astype(BF), grad_ref[...], NN, preferred_element_type=F32)
+    blocks, padded, lanes = keep_ref.shape
+    rows = top.shape[0] // 2
+    fill = jnp.zeros((padded - rows, lanes), F32)
+    x, core = at_ref[0], at_ref[1]
+    for b in range(blocks):
+        column = pl.ds(pl.multiple_of((x + b) % blocks * lanes, lanes), lanes)
+        halves = [jnp.concatenate([top[c * rows : (c + 1) * rows, column], fill], axis=0) for c in range(2)]
+        keep_ref[b] = jnp.where(core == 0, halves[0], halves[1]).astype(BF)
+        send_ref[b] = jnp.where(core == 0, halves[1], halves[0]).astype(BF)
+
+
+def join_core_kernel(keep_ref, came_ref, *outs):
+    for b, out in enumerate(outs):
+        out[...] = (keep_ref[b].astype(F32) + came_ref[b].astype(F32)).astype(BF)
+
+
+def total_of(refs):
+    total = refs[0][...].astype(F32)
+    for ref in refs[1:]:
+        total += ref[...].astype(F32)
+    return total
+
+
+def join_x_kernel(at_ref, a, b, c, d, o0, o1, o2, o3, total):
+    total[...] = total_of((a, b, c, d))
+    rows = o0.shape[0]
+    for n, out in enumerate((o0, o1, o2, o3)):
+        begin = pl.multiple_of((at_ref[2] + n) % 4 * rows, rows)
+        out[...] = total[pl.ds(begin, rows), :].astype(BF)
+
+
+def join_y_kernel(a, b, c, d, out):
+    total = total_of((a, b, c, d))
+    fill = jnp.zeros((out.shape[0] - total.shape[0], total.shape[1]), F32)
+    out[...] = jnp.concatenate([total, fill], axis=0).astype(BF)
+
+
+def assemble_kernel(at_ref, a, b, c, d, other_ref, out, wide):
+    x, core = at_ref[0], at_ref[1]
+    rows = out.shape[0] // 2
+    for n, mine in enumerate((a, b, c, d)):
+        own, other = mine[...].astype(F32), other_ref[n].astype(F32)
+        low = jnp.where(core == 0, own, other)[:rows]
+        high = jnp.where(core == 0, other, own)[:rows]
+        column = pl.ds(pl.multiple_of((x + 4 - n) % 4 * LANES, LANES), LANES)
+        wide[:, column] = jnp.concatenate([low, high], axis=0)
+    out[...] = wide[...].astype(BF)
 
 
 def digits_kernel(order_ref, first_ref, last_ref, sorted_ref):
@@ -95,16 +142,16 @@
     return jnp.where(lax.broadcasted_iota(jnp.int32, (slots, lanes), 0) == digit, 1.0, 0.0).astype(BF)
 
 
-def digits_of(sorted_ref, group):
+def digits_of(sorted_ref, group, k):
     rows = group // LANES
-    at = sorted_ref[pl.ds(pl.program_id(0) * rows, rows), :]
+    at = sorted_ref[pl.ds(k * rows, rows), :]
     at = jnp.concatenate([at[r : r + 1] for r in range(rows)], axis=1)
     return at // I3, at % I3
 
 
 def before_kernel(sorted_ref, one_ref, mid_ref, three_ref, left_ref, right_ref, chained_ref):
     group = left_ref.shape[1]
-    first, third = digits_of(sorted_ref, group)
+    first, third = digits_of(sorted_ref, group, pl.program_id(0))
     left = lax.dot_general(one_ref[...], onehot(first, I1), NN, preferred_element_type=F32).astype(BF)
     left_ref[...] = left
     right_ref[...] = lax.dot_general(three_ref[...], onehot(third, I3), NN, preferred_element_type=F32).astype(BF)
@@ -113,7 +160,19 @@
         chained_ref[a * D2 * R : (a + 1) * D2 * R] = chained.astype(BF)
 
 
-def after_kernel(scale, order_ref, sorted_ref, received_ref, left_ref, right_ref, chained_ref, mid_ref, one_ref, two_ref, three_ref, wide, picked, gt, inner, back, acc_one, acc_three, right_wide, chained_wide):
+def place(r):
+    return r % 2 * 8 + r // 4 * 2 + r // 2 % 2
+
+
+def after_kernel(
+    scale, start, reps, order_ref, sorted_ref, received_ref, left_ref, right_ref, chained_ref, mid_ref, *refs
+):
+    last = reps > 0
+    if start:
+        old_one_ref, old_three_ref, unused = refs[:3]
+        refs = refs[3:]
+    two_ref, *ends = refs[: 2 if last else 3]
+    wide, picked, gt, inner, back, acc_one, acc_three, right_wide, chained_wide = refs[2 if last else 3 :]
     k = pl.program_id(0)
     groups = pl.num_programs(0)
     group = left_ref.shape[1]
@@ -127,17 +186,17 @@
     @pl.when(k == 0)
     def _():
         wide[...] = received_ref[...].astype(F32)
-        acc_one[...] = jnp.zeros_like(acc_one)
-        acc_three[...] = jnp.zeros_like(acc_three)
+        acc_one[...] = old_one_ref[...] if start else jnp.zeros_like(acc_one)
+        acc_three[...] = old_three_ref[...] if start else jnp.zeros_like(acc_three)
 
         def one(step, carry):
-            fetch(0, 0, step * share, share)
+            fetch(0, start * group, step * share, share)
             return carry
 
         lax.fori_loop(0, steps, one, 0)
 
     slot = k % 2
-    later = jnp.minimum(k + 1, groups - 1) * group
+    later = (start + jnp.minimum(k + 1, groups - 1)) * group
     gt[...] = picked[slot].T
     right_wide[...] = right_ref[...].astype(F32)
     chained_wide[...] = chained_ref[...].astype(F32)
@@ -165,7 +224,7 @@
         return carry
 
     lax.fori_loop(0, steps, chunk, 0)
-    first, third = digits_of(sorted_ref, group)
+    first, third = digits_of(sorted_ref, group, start + k)
     inner_all = inner[...].astype(BF)
     two = None
     firsts = []
@@ -174,15 +233,31 @@
         term = lax.dot_general(left_ref[a * R : (a + 1) * R], part, NT, preferred_element_type=F32)
         two = term if two is None else two + term
         firsts.append(lax.dot_general(mid_ref[0], part, NN, preferred_element_type=F32).astype(BF))
-    two_ref[0] = (scale * two).astype(BF)
+    two = (scale * two).astype(BF)
+    for b in range(D2 * R // LANES):
+        two_ref[0, b * R : (b + 1) * R] = two[:, b * LANES : (b + 1) * LANES]
     back_first = jnp.concatenate(firsts, axis=0)
     acc_one[...] += lax.dot_general(onehot(first, I1), back_first, NT, preferred_element_type=F32)
     acc_three[...] += lax.dot_general(onehot(third, I3), back[...].astype(BF), NT, preferred_element_type=F32)
 
     @pl.when(k == groups - 1)
     def _():
-        one_ref[...] = (scale * acc_one[...]).astype(BF)
-        three_ref[...] = (scale * acc_three[...]).astype(BF)
+        if not last:
+            ends[0][...] = acc_one[...]
+            ends[1][...] = acc_three[...]
+            return
+        rest_ref = ends[0]
+        for r in range(reps):
+            blocks = []
+            for acc in (acc_one, acc_three):
+                rows = acc.shape[0] // reps
+                for b in range(acc.shape[1] // LANES):
+                    blocks.append(acc[r * rows : (r + 1) * rows, b * LANES : (b + 1) * LANES])
+            rest_ref[place(r)] = (scale * jnp.concatenate(blocks, axis=0)).astype(BF)
+
+
+SMEM = pl.BlockSpec(memory_space=pltpu.SMEM)
+VMEM = pl.BlockSpec(memory_space=pltpu.VMEM)
 
 
 def whole(shape):
@@ -211,16 +286,54 @@
     )(bottom_out, pooled.reshape(samples * tables, width), top_grad, top_weight)
 
 
-def gram(feat, top_grad, scale):
+def gram(where, feat, top_grad, scale, shape):
     count, width, samples = feat.shape
     pairs = count * (count - 1) // 2
     return pl.pallas_call(
         lambda *refs: gram_kernel(count, scale, *refs),
-        out_shape=jax.ShapeDtypeStruct((width + pairs, top_grad.shape[1]), F32),
-        scratch_shapes=[pltpu.VMEM((count, width, samples), F32), pltpu.VMEM((pairs, samples), F32)],
+        in_specs=[SMEM, VMEM, VMEM],
+        out_shape=(jax.ShapeDtypeStruct(shape, BF),) * 2,
+        scratch_shapes=[
+            pltpu.VMEM((count, width, samples), F32),
+            pltpu.VMEM((pairs, samples), F32),
+            pltpu.VMEM((width + pairs, top_grad.shape[1]), F32),
+        ],
         compiler_params=pltpu.CompilerParams(vmem_limit_bytes=48 << 20),
         name="gram",
-    )(feat, top_grad)
+    )(where, feat, top_grad)
+
+
+def join_core(keep, came):
+    return pl.pallas_call(
+        join_core_kernel, out_shape=(jax.ShapeDtypeStruct(keep.shape[1:], BF),) * 4, name="join_core"
+    )(keep, came)
+
+
+def join_x(where, *parts):
+    rows, lanes = parts[0].shape
+    return pl.pallas_call(
+        join_x_kernel,
+        in_specs=[SMEM] + [VMEM] * 4,
+        out_shape=(jax.ShapeDtypeStruct((rows // 4, lanes), BF),) * 4,
+        scratch_shapes=[pltpu.VMEM((rows, lanes), F32)],
+        name="join_x",
+    )(where, *parts)
+
+
+def join_y(*parts):
+    return pl.pallas_call(
+        join_y_kernel, out_shape=jax.ShapeDtypeStruct((LANES, LANES), BF), name="join_y"
+    )(*parts)
+
+
+def assemble(where, shape, *parts):
+    return pl.pallas_call(
+        assemble_kernel,
+        in_specs=[SMEM] + [VMEM] * 5,
+        out_shape=jax.ShapeDtypeStruct(shape, BF),
+        scratch_shapes=[pltpu.VMEM(shape, F32)],
+        name="assemble",
+    )(where, *parts)
 
 
 def before(order, first, last, core_one, core_two, core_three):
@@ -255,28 +368,34 @@
     return sorted_digits, links
 
 
-def after(received, order, sorted_digits, links, core_two, scale):
+def after(begin, end, received, order, sorted_digits, links, core_two, scale, reps, old):
+    rest = (I1 * D1 * R + I3 * D3 * R) // reps // LANES
     total, width = received.shape
     group = total // I2
     left, right, chained = links
-    return pl.pallas_call(
-        lambda *refs: after_kernel(scale, *refs),
+    last = end == I2
+    sums = (I1, D1 * R), (I3, D3 * R)
+    two_shape = I2, R * D2 * R // LANES, LANES
+    extra_in = [whole(sums[0]), whole(sums[1]), pl.BlockSpec(memory_space=pl.ANY)] if begin else []
+    ends = [((reps, rest, LANES), BF)] if last else [(one, F32) for one in sums]
+    return pl.pallas_call(
+        lambda *refs: after_kernel(scale, begin, reps if last else 0, *refs),
         grid_spec=pltpu.PrefetchScalarGridSpec(
             num_scalar_prefetch=1,
-            grid=(I2,),
+            grid=(end - begin,),
             in_specs=[
                 whole(sorted_digits.shape),
                 whole((total, width)),
-                pl.BlockSpec((D1 * R, group), lambda k, o: (0, k)),
-                pl.BlockSpec((D3 * R, group), lambda k, o: (0, k)),
-                pl.BlockSpec((D1 * D2 * R, group), lambda k, o: (0, k)),
-                pl.BlockSpec((1, R, D2 * R), lambda k, o: (k, 0, 0)),
-            ],
-            out_specs=(
-                whole((I1, D1 * R)),
-                pl.BlockSpec((1, R, D2 * R), lambda k, o: (k, 0, 0)),
-                whole((I3, D3 * R)),
-            ),
+                pl.BlockSpec((D1 * R, group), lambda k, o: (0, begin + k)),
+                pl.BlockSpec((D3 * R, group), lambda k, o: (0, begin + k)),
+                pl.BlockSpec((D1 * D2 * R, group), lambda k, o: (0, begin + k)),
+                pl.BlockSpec((1, R, D2 * R), lambda k, o: (begin + k, 0, 0)),
+            ]
+            + extra_in,
+            out_specs=[
+                pl.BlockSpec((1,) + two_shape[1:], lambda k, o: (place(begin + k), 0, 0)),
+            ]
+            + [whole(shape) for shape, kind in ends],
             scratch_shapes=[
                 pltpu.VMEM((total, width), F32),
                 pltpu.VMEM((2, group, width), F32),
@@ -289,18 +408,48 @@
                 pltpu.VMEM((D1 * D2 * R, group), F32),
             ],
         ),
-        out_shape=(
-            jax.ShapeDtypeStruct((I1, D1 * R), BF),
-            jax.ShapeDtypeStruct((I2, R, D2 * R), BF),
-            jax.ShapeDtypeStruct((I3, D3 * R), BF),
-        ),
+        out_shape=[jax.ShapeDtypeStruct(two_shape, BF)] + [jax.ShapeDtypeStruct(*one) for one in ends],
+        input_output_aliases={9: 0} if begin else {},
         compiler_params=pltpu.CompilerParams(vmem_limit_bytes=48 << 20),
         name="after",
-    )(order, sorted_digits, received, left, right, chained, core_two)
-
-
-def scatter_sum(array):
-    return lax.psum_scatter(array, "rep", scatter_dimension=0, tiled=True)
+    )(order, sorted_digits, received, left, right, chained, core_two, *old)
+
+
+CUTS = 5, 10
+AXES = {"x": 4, "z_hi": 2, "core": 2, "y": 4, "z_lo": 8}
+
+
+def groups_of(*names):
+    places = np.arange(int(np.prod(list(AXES.values())))).reshape(tuple(AXES.values()))
+    order = list(AXES)
+    moved = [order.index(n) for n in names]
+    kept = [i for i in range(len(order)) if i not in moved]
+    return places.transpose(kept + moved).reshape(-1, int(np.prod([AXES[n] for n in names]))).tolist()
+
+
+def swap(array, *names):
+    return lax.all_to_all(
+        array, ("rep", "tab"), 0, 0, axis_index_groups=groups_of(*names), tiled=True
+    )
+
+
+def add_up(array, *names):
+    return jnp.sum(swap(array, *names).astype(F32), axis=0)
+
+
+def shift(array, axis, by):
+    size = 4
+    step = 4 if axis == "rep" else 8
+    number = size * step
+    return lax.ppermute(array, axis, [(i, (i + by * step) % number) for i in range(number)])
+
+
+def swap_core(array):
+    return lax.ppermute(array, "rep", [(i, i ^ 1) for i in range(16)])
+
+
+def gather_up(array, size, *names):
+    return swap(jnp.broadcast_to(array[None], (size,) + array.shape), *names)
 
 
 def on_device(
@@ -321,25 +470,51 @@
     scale = float(np.float32(1.0 / np.sqrt(batch_all)))
     grad_rows, grad_bottom, feat = dense(bottom_out, pooled, top_grad, top_weight)
     received = lax.all_to_all(grad_rows, "tab", split_axis=0, concat_axis=0, tiled=True)
-    dense_term = gram(feat, top_grad, scale)
-    grad_top = lax.psum(dense_term, ("rep", "tab")).astype(BF)
-    order = grouped[0, 0]
+    rep, tab = lax.axis_index("rep"), lax.axis_index("tab")
+    where = jnp.stack([rep >> 2, rep & 1, tab >> 3]).astype(jnp.int32)
+    rows = top_weight.shape[0]
+    padded = -(-rows // 2 // 64) * 64
+    quarter = padded // 4
+    keep, send = gram(where, feat, top_grad, scale, (4, padded, LANES))
+    own, *others = join_core(keep, swap_core(send))
+    order, own, others = lax.optimization_barrier((grouped[0, 0], own, others))
     sorted_digits, links = before(
         order, digit_first[0], digit_last[0], core_first[0], core_mid[0], core_last[0]
     )
-    one, two, three = after(
-        received.reshape(-1, width), order, sorted_digits, links, core_mid[0], scale
-    )
-    parts = jnp.concatenate(
-        [one.reshape(reps, -1, LANES), two.reshape(reps, -1, LANES), three.reshape(reps, -1, LANES)],
-        axis=1,
-    )
-    share = scatter_sum(parts.reshape(-1, LANES)).astype(F32)
-    size_one = I1 * D1 * R // reps // LANES
-    size_two = I2 * R * D2 * R // reps // LANES
-    grad_one = share[:size_one].reshape(1, I1 // reps, D1 * R)
-    grad_two = share[size_one : size_one + size_two].reshape(1, I2 // reps, R, D2 * R)
-    grad_three = share[size_one + size_two :].reshape(1, I3 // reps, D3 * R)
+    own, *others = join_x(where, own, *[shift(one, "rep", 1 + n) for n, one in enumerate(others)])
+    partial = join_y(own, *[shift(one, "tab", 1 + n) for n, one in enumerate(others)])
+    received = received.reshape(-1, width)
+    links, partial = lax.optimization_barrier((links, partial))
+    received, partial = lax.optimization_barrier((received, partial))
+
+    def piece(begin, end, old):
+        return after(begin, end, received, order, sorted_digits, links, core_mid[0], scale, reps, old)
+
+    two, one, three = piece(0, CUTS[0], ())
+    summed = add_up(partial.reshape(16, SUB, LANES), "z_hi", "z_lo").astype(BF)
+    one, summed = lax.optimization_barrier((one, summed))
+    two, one, three = piece(CUTS[0], CUTS[1], (one, three, two))
+    summed = gather_up(summed, 16, "z_hi", "z_lo").reshape(LANES, LANES)[:quarter]
+    one, summed = lax.optimization_barrier((one, summed))
+    two, rest = piece(CUTS[1], I2, (one, three, two))
+    summed = gather_up(summed, 4, "y").reshape(padded, LANES)
+    rest, summed = lax.optimization_barrier((rest, summed))
+    mine = [summed] + [shift(summed, "rep", n) for n in (1, 2, 3)]
+    grad_top = assemble(where, (rows, top_grad.shape[1]), *mine, swap_core(jnp.stack(mine)))
+    parts = jnp.concatenate([two, rest], axis=1)
+    parts = add_up(parts.reshape(2, 8, -1, LANES), "core").astype(BF)
+    parts = add_up(parts.reshape(4, 2, -1, LANES), "x").astype(BF)
+    share = add_up(parts, "z_hi")
+    size_two = R * D2 * R // LANES
+    size_one = I1 // reps * D1 * R // LANES
+    widths = D2 * R // LANES, D1 * R // LANES, D3 * R // LANES
+
+    def lay(block, blocks):
+        return block.reshape(blocks, -1, LANES).swapaxes(0, 1).reshape(1, -1, blocks * LANES)
+
+    grad_two = lay(share[:size_two], widths[0])[:, None]
+    grad_one = lay(share[size_two : size_two + size_one], widths[1])
+    grad_three = lay(share[size_two + size_one :], widths[2])
     return (grad_one, grad_two, grad_three, grad_top, grad_bottom)
 
 

time: 262 us -> 228 us (0.87); the launches traced: 261 us -> 224 us
  blocking collectives: 115 us -> 7.4 us
  starting transfers between devices: 16.3 us -> 93.3 us
  waiting for transfers between devices: 34 us -> 12.4 us
  Pallas kernels: 66.6 us -> 80.3 us
  between operations: 14.1 us -> 1.12 us
  local copies, waits for them, and re-layouts: 13.9 us -> 26.4 us
    psum x1 -> x0, blocking collectives: 115 us -> none  [on_device(): grad_top = lax.psum(dense_term, ('rep', 'tab')).astype(BF)]
    all_to_all x0 -> x5, starting transfers between devices: none -> 39.2 us  [swap(): lax.all_to_all(array, ('rep', 'tab'), 0, 0, axis_index_groups=groups_of(*...]
    ppermute x0 -> x11, starting transfers between devices: none -> 37.8 us  [the longest x9 30.9 us: shift(): lax.ppermute(array, axis, [(i, (i + by * step) % number) for i in range(n...]
    all_to_all x1, waiting for transfers between devices: 34 us -> 0.01 us  [on_device(): lax.all_to_all(grad_rows, 'tab', split_axis=0, concat_axis=0, tiled=True)]
    unnamed x30 -> x84, local copies, waits for them, and re-layouts: 9.57 us -> 23.2 us
    pallas_call x2 -> x8, Pallas kernels: 44.4 us -> 57.4 us  [the longest x3 44.2 us: after(): pl.pallas_call(lambda *refs: after_kernel(scale, begin, reps if last else...]
    all_to_all x0 -> x5, waiting for transfers between devices: none -> 8.33 us  [swap(): lax.all_to_all(array, ('rep', 'tab'), 0, 0, axis_index_groups=groups_of(*...]
    all_to_all x0 -> x1, blocking collectives: none -> 7.4 us  [swap(): lax.all_to_all(array, ('rep', 'tab'), 0, 0, axis_index_groups=groups_of(*...]
  transfers between devices with their start and end apart: 2 -> 17, of which waited for: 1 -> 3; matrix products, arithmetic and copies ran while one was open for 0% -> 1% of each run, Pallas kernels for 7% -> 31%
where the time goes in v2:
time: 228 us; the launch traced here: 224 us
  starting transfers between devices  93.3 us (41%)
  Pallas kernels  80.3 us (35%)
  local copies, waits for them, and re-layouts  26.4 us (12%)
  waiting for transfers between devices  12.4 us (5%)
  blocking collectives  7.4 us (3%)
  other arithmetic  3.02 us (1%)
    pallas_call x3, Pallas kernels, after(): pl.pallas_call(lambda *refs: after_kernel(scale, begin, reps if last else...  44.2 us
    all_to_all x5, starting transfers between devices, swap(): lax.all_to_all(array, ('rep', 'tab'), 0, 0, axis_index_groups=groups_of(*...  39.2 us
    ppermute x9, starting transfers between devices, shift(): lax.ppermute(array, axis, [(i, (i + by * step) % number) for i in range(n...  30.9 us
    unnamed x84, local copies, waits for them, and re-layouts  23.2 us
    all_to_all x1, starting transfers between devices, on_device(): lax.all_to_all(grad_rows, 'tab', split_axis=0, concat_axis=0, tiled=True)  16.2 us
    pallas_call x1, Pallas kernels, before(): pl.pallas_call(before_kernel, grid=(I2,), in_specs=[whole(table), whole((...  12.3 us
    pallas_call x1, Pallas kernels, dense(): pl.pallas_call(lambda *refs: dense_kernel(count, *refs), out_shape=(jax.S...  8.81 us
    all_to_all x5, waiting for transfers between devices, swap(): lax.all_to_all(array, ('rep', 'tab'), 0, 0, axis_index_groups=groups_of(*...  8.33 us
  transfers between devices with their start and end apart: 17, of which 3 were waited for; matrix products, arithmetic and copies ran while one was open for 1% of the time, Pallas kernels for 31%

profile of v2, /device:TPU:1, one launch (start us, length us, event | category | flops | bytes accessed | tf_op | source)
XLA Modules:
  0.0 224.0 jit_solution(1245923350654194887)
XLA Ops:
  0.6 1.2 copy-done.9
  1.9 1.1 copy-done.10
  3.0 0.9 copy-done.11
  4.6 8.8 %dense.1 = (bf16[32,128,128]{2,1,0:T(8,128)(2,1)}, bf16[128,128]{1,0:T(8,128)(2,1)}, bf16[33,128,128]{2,1,0:T(8,128)(2,1)S(1)}) custom-call(bf16[128,128]{1,0:T(8,128)(2,1)S(1)} %copy-done.25, bf16[4096,128]{1,0:T(8,128)(2,1)S(1)} %bitcast.48, bf16[128,512]{1,0:T(8,128)(2,1)S(1)} %copy-done.11, bf16[656,512]{1,0:T(8,128)(2,1)S(1)} %copy-done.10), custom_call_target="tpu_custom_call" | custom-call | tf_op jit(solution)/shard_map/dense/pallas_call | solution.py:271
  13.4 16.2 %all-to-all-start = ((bf16[32,128,128]{2,1,0:T(8,128)(2,1)}), bf16[32,128,128]{2,1,0:T(8,128)(2,1)S(1)}, u32[]{:S(2)}, u32[]{:S(2)}) async-start(bf16[32,128,128]{2,1,0:T(8,128)(2,1)} %get-tuple-element.54), calls=%async_computation | async-start | bytes 2097152 | tf_op jit(solution)/shard_map/all_to_all | solution.py:472
  29.8 5.9 %gram.1 = (bf16[4,384,128]{2,1,0:T(8,128)(2,1)S(1)}, bf16[4,384,128]{2,1,0:T(8,128)(2,1)S(1)}) custom-call(s32[3]{0:T(128)S(1)} %pad_add_fusion.refs_0_.at_ref, bf16[33,128,128]{2,1,0:T(8,128)(2,1)S(1)} %get-tuple-element.46.refs_1_, bf16[128,512]{1,0:T(8,128)(2,1)S(1)} %copy-done.12), custom_call_target="tpu_custom_call" | custom-call | tf_op jit(solution)/shard_map/gram/pallas_call | solution.py:292
  36.4 3.0 %collective-permute-start = (bf16[4,384,128]{2,1,0:T(8,128)(2,1)S(1)}, bf16[4,384,128]{2,1,0:T(8,128)(2,1)S(1)}, u32[]{:S(2)}, u32[]{:S(2)}) collective-permute-start(bf16[4,384,128]{2,1,0:T(8,128)(2,1)S(1)} %get-tuple-element.48), channel_id=1, source_target_pairs={{0,32},{32,0},{64,96},{96,64},{128,160},{160,128},{192,224},{224,1... | collective-permute-start | bytes 1179656 | tf_op jit(solution)/shard_map/ppermute | solution.py:448
  39.4 1.3 collective-permute-done.came_ref
  41.5 1.9 join_core.1
  43.4 3.1 %collective-permute-start.1 = (bf16[384,128]{1,0:T(8,128)(2,1)}, bf16[384,128]{1,0:T(8,128)(2,1)S(1)}, u32[]{:S(2)}, u32[]{:S(2)}) collective-permute-start(bf16[384,128]{1,0:T(8,128)(2,1)} %get-tuple-element.59), channel_id=1, source_target_pairs={{0,128},{32,160},{64,192},{96,224},{128,256},{160,288},{192,320},{... | collective-permute-start | bytes 294920 | tf_op jit(solution)/shard_map/ppermute | solution.py:444
  46.5 4.4 %collective-permute-start.2 = (bf16[384,128]{1,0:T(8,128)(2,1)}, bf16[384,128]{1,0:T(8,128)(2,1)S(1)}, u32[]{:S(2)}, u32[]{:S(2)}) collective-permute-start(bf16[384,128]{1,0:T(8,128)(2,1)} %get-tuple-element.60), channel_id=1, source_target_pairs={{0,256},{32,288},{64,320},{96,352},{128,384},{160,416},{192,448},{... | collective-permute-start | bytes 294920 | tf_op jit(solution)/shard_map/ppermute | solution.py:444
  50.9 3.1 %collective-permute-start.3 = (bf16[384,128]{1,0:T(8,128)(2,1)}, bf16[384,128]{1,0:T(8,128)(2,1)S(1)}, u32[]{:S(2)}, u32[]{:S(2)}) collective-permute-start(bf16[384,128]{1,0:T(8,128)(2,1)} %get-tuple-element.61), channel_id=1, source_target_pairs={{0,384},{32,416},{64,448},{96,480},{128,0},{160,32},{192,64},{224,... | collective-permute-start | bytes 294920 | tf_op jit(solution)/shard_map/ppermute | solution.py:444
  54.0 2.8 %collective-permute-done.3.d = bf16[384,128]{1,0:T(8,128)(2,1)S(1)} collective-permute-done((bf16[384,128]{1,0:T(8,128)(2,1)}, bf16[384,128]{1,0:T(8,128)(2,1)S(1)}, u32[]{:S(2)}, u32[]{:S(2)}) %collective-permute-start.3) | collective-permute-done | bytes 98336 | tf_op jit(solution)/shard_map/ppermute | solution.py:444
  57.4 1.7 join_x.1
  59.1 3.4 %collective-permute-start.4 = (bf16[96,128]{1,0:T(8,128)(2,1)}, bf16[96,128]{1,0:T(8,128)(2,1)S(1)}, u32[]{:S(2)}, u32[]{:S(2)}) collective-permute-start(bf16[96,128]{1,0:T(8,128)(2,1)} %get-tuple-element.63), channel_id=1, source_target_pairs={{0,8},{1,9},{2,10},{3,11},{4,12},{5,13},{6,14},{7,15},{8,16},{9,17... | collective-permute-start | bytes 73736 | tf_op jit(solution)/shard_map/ppermute | solution.py:444
  62.5 4.3 %collective-permute-start.5 = (bf16[96,128]{1,0:T(8,128)(2,1)}, bf16[96,128]{1,0:T(8,128)(2,1)S(1)}, u32[]{:S(2)}, u32[]{:S(2)}) collective-permute-start(bf16[96,128]{1,0:T(8,128)(2,1)} %get-tuple-element.64), channel_id=1, source_target_pairs={{0,16},{1,17},{2,18},{3,19},{4,20},{5,21},{6,22},{7,23},{8,24},{9,... | collective-permute-start | bytes 73736 | tf_op jit(solution)/shard_map/ppermute | solution.py:444
  66.9 3.1 %collective-permute-start.6 = (bf16[96,128]{1,0:T(8,128)(2,1)}, bf16[96,128]{1,0:T(8,128)(2,1)S(1)}, u32[]{:S(2)}, u32[]{:S(2)}) collective-permute-start(bf16[96,128]{1,0:T(8,128)(2,1)} %get-tuple-element.65), channel_id=1, source_target_pairs={{0,24},{1,25},{2,26},{3,27},{4,28},{5,29},{6,30},{7,31},{8,0},{9,1... | collective-permute-start | bytes 73736 | tf_op jit(solution)/shard_map/ppermute | solution.py:444
  70.2 1.8 digits.1.sorted_ref.refs_1_
  72.0 1.0 copy-done
  73.8 12.3 %before.1 = (bf16[256,4096]{1,0:T(8,128)(2,1)S(1)}, bf16[512,4096]{1,0:T(8,128)(2,1)}, bf16[1024,4096]{1,0:T(8,128)(2,1)}) custom-call(s32[32,128]{1,0:T(8,128)S(1)} %copy-done.13, bf16[256,128]{1,0:T(8,128)(2,1)S(1)} %bitcast.50, bf16[16,64,256]{2,1,0:T(8,128)(2,1)S(1)} %bitcast.44, bf16[512,128]{1,0:T(8,128)(2,1)S(1)} %bitcast.49), custom_call_target="tpu_custom_call" | custom-call | tf_op jit(solution)/shard_map/before/pallas_call | solution.py:346
  86.7 1.4 join_y.1
  88.1 9.2 %all-to-all-start.1 = ((bf16[16,8,128]{2,1,0:T(8,128)(2,1)}), bf16[16,8,128]{2,1,0:T(8,128)(2,1)S(1)}, u32[]{:S(2)}, u32[]{:S(2)}) async-start(bf16[16,8,128]{2,1,0:T(8,128)(2,1)} %bitcast.65), calls=%async_computation.1 | async-start | bytes 65536 | tf_op jit(solution)/shard_map/all_to_all | solution.py:431
  97.3 1.0 copy-done.1
  99.1 13.9 %after.3 = (bf16[16,128,128]{2,1,0:T(8,128)(2,1)S(1)}, f32[128,256]{1,0:T(8,128)S(1)}, f32[128,512]{1,0:T(8,128)S(1)}) custom-call(s32[4096]{0:T(1024)S(1)} %bitcast.52, s32[32,128]{1,0:T(8,128)S(1)} %copy-done.14, bf16[4096,128]{1,0:T(8,128)(2,1)S(1)} %bitcast.41, bf16[256,4096]{1,0:T(8,128)(2,1)S(1)} %get-tuple-element.68.refs_3_, ...), custom_call_target="tpu_custom_call" | custom-call | tf_op jit(solution)/shard_map/after/pallas_call | solution.py:381
  113.0 0.8 copy-done.4
  115.8 11.5 %all-to-all-start.2 = ((bf16[16,8,128]{2,1,0:T(8,128)(2,1)}), bf16[16,8,128]{2,1,0:T(8,128)(2,1)S(1)}, u32[]{:S(2)}, u32[]{:S(2)}) async-start(bf16[16,8,128]{2,1,0:T(8,128)(2,1)} %broadcast_in_dim.4), calls=%async_computation.2 | async-start | bytes 65536 | tf_op jit(solution)/shard_map/all_to_all | solution.py:431
  127.3 1.0 copy-done.2
  128.3 1.0 copy-done.5
  129.4 0.9 copy-done.18
  130.3 0.9 copy-done.24
  131.2 14.0 %after.4 = (bf16[16,128,128]{2,1,0:T(8,128)(2,1)S(1)}, f32[128,256]{1,0:T(8,128)S(1)}, f32[128,512]{1,0:T(8,128)S(1)}) custom-call(s32[4096]{0:T(1024)S(1)} %bitcast.53, s32[32,128]{1,0:T(8,128)S(1)} %copy-done.15, bf16[4096,128]{1,0:T(8,128)(2,1)S(1)} %bitcast.42, bf16[256,4096]{1,0:T(8,128)(2,1)S(1)} %get-tuple-element.68.refs_3_, ...), custom_call_target="tpu_custom_call", output_to_operand_aliasing={{0}: (9, {})} | custom-call | tf_op jit(solution)/shard_map/after/pallas_call | solution.py:381
  145.2 0.8 copy-done.6
  147.3 3.3 %all-to-all-start.3 = ((bf16[4,96,128]{2,1,0:T(8,128)(2,1)}), bf16[4,96,128]{2,1,0:T(8,128)(2,1)S(1)}, u32[]{:S(2)}, u32[]{:S(2)}) async-start(bf16[4,96,128]{2,1,0:T(8,128)(2,1)} %broadcast_in_dim.5), calls=%async_computation.3 | async-start | bytes 196608 | tf_op jit(solution)/shard_map/all_to_all | solution.py:431
  150.6 1.0 copy-done.3
  151.7 1.0 copy-done.7
  152.7 0.9 copy-done.22
  153.6 16.3 %after.5 = (bf16[16,128,128]{2,1,0:T(8,128)(2,1)S(1)}, bf16[16,48,128]{2,1,0:T(8,128)(2,1)S(1)}) custom-call(s32[4096]{0:T(1024)S(1)} %bitcast.54, s32[32,128]{1,0:T(8,128)S(1)} %copy-done.15, bf16[4096,128]{1,0:T(8,128)(2,1)S(1)} %bitcast.43, bf16[256,4096]{1,0:T(8,128)(2,1)S(1)} %get-tuple-element.68.refs_3_, ...), custom_call_target="tpu_custom_call", output_to_operand_aliasing={{0}: (9, {})} | custom-call | tf_op jit(solution)/shard_map/after/pallas_call | solution.py:381
  171.4 1.2 pad_maximum_fusion
  172.6 7.4 %all_to_all.35 = bf16[2,8,176,128]{3,2,1,0:T(8,128)(2,1)S(1)} all-to-all(bf16[2,8,176,128]{3,2,1,0:T(8,128)(2,1)S(1)} %bitcast.55), channel_id=1, replica_groups={{0,32},{1,33},{2,34},{3,35},{4,36},{5,37},{6,38},{7,39},{8,40},{9,41},{..., dimensions={0} | all-to-all | bytes 1441792 | tf_op jit(solution)/shard_map/all_to_all | solution.py:431
  180.0 0.9 reduce_sum.46
  181.0 3.6 %all-to-all-start.5 = ((bf16[4,2,176,128]{3,2,1,0:T(8,128)(2,1)}), bf16[4,2,176,128]{3,2,1,0:T(8,128)(2,1)S(1)}, u32[]{:S(2)}, u32[]{:S(2)}) async-start(bf16[4,2,176,128]{3,2,1,0:T(8,128)(2,1)} %bitcast.18), calls=%async_computation.5 | async-start | bytes 720896 | tf_op jit(solution)/shard_map/all_to_all | solution.py:431
  184.6 4.6 %collective-permute-start.9 = (bf16[384,128]{1,0:T(8,128)(2,1)S(1)}, bf16[384,128]{1,0:T(8,128)(2,1)S(1)}, u32[]{:S(2)}, u32[]{:S(2)}) collective-permute-start(bf16[384,128]{1,0:T(8,128)(2,1)S(1)} %bitcast.56), channel_id=1, source_target_pairs={{0,384},{32,416},{64,448},{96,480},{128,0},{160,32},{192,64},{224,... | collective-permute-start | bytes 294920 | tf_op jit(solution)/shard_map/ppermute | solution.py:444
  189.2 2.5 %collective-permute-start.8 = (bf16[384,128]{1,0:T(8,128)(2,1)S(1)}, bf16[384,128]{1,0:T(8,128)(2,1)S(1)}, u32[]{:S(2)}, u32[]{:S(2)}) collective-permute-start(bf16[384,128]{1,0:T(8,128)(2,1)S(1)} %bitcast.57), channel_id=1, source_target_pairs={{0,256},{32,288},{64,320},{96,352},{128,384},{160,416},{192,448},{... | collective-permute-start | bytes 294920 | tf_op jit(solution)/shard_map/ppermute | solution.py:444
  191.7 2.5 %collective-permute-start.7 = (bf16[384,128]{1,0:T(8,128)(2,1)S(1)}, bf16[384,128]{1,0:T(8,128)(2,1)S(1)}, u32[]{:S(2)}, u32[]{:S(2)}) collective-permute-start(bf16[384,128]{1,0:T(8,128)(2,1)S(1)} %bitcast.58), channel_id=1, source_target_pairs={{0,128},{32,160},{64,192},{96,224},{128,256},{160,288},{192,320},{... | collective-permute-start | bytes 294920 | tf_op jit(solution)/shard_map/ppermute | solution.py:444
  194.9 11.6 %all-to-all-start.6 = ((bf16[2,176,128]{2,1,0:T(8,128)(2,1)}), bf16[2,176,128]{2,1,0:T(8,128)(2,1)S(1)}, u32[]{:S(2)}, u32[]{:S(2)}) async-start(bf16[2,176,128]{2,1,0:T(8,128)(2,1)} %reduce_sum.47), calls=%async_computation.6 | async-start | bytes 180224 | tf_op jit(solution)/shard_map/all_to_all | solution.py:431
  206.6 4.0 %collective-permute-start.10 = (bf16[4,384,128]{2,1,0:T(8,128)(2,1)S(1)}, bf16[4,384,128]{2,1,0:T(8,128)(2,1)S(1)}, u32[]{:S(2)}, u32[]{:S(2)}) collective-permute-start(bf16[4,384,128]{2,1,0:T(8,128)(2,1)S(1)} %pad_maximum_fusion.1), channel_id=1, source_target_pairs={{0,32},{32,0},{64,96},{96,64},{128,160},{160,128},{192,224},{224,1... | collective-permute-start | bytes 1179656 | tf_op jit(solution)/shard_map/ppermute | solution.py:448
  210.6 8.3 %all-to-all-done.6 = bf16[2,176,128]{2,1,0:T(8,128)(2,1)S(1)} async-done(((bf16[2,176,128]{2,1,0:T(8,128)(2,1)}), bf16[2,176,128]{2,1,0:T(8,128)(2,1)S(1)}, u32[]{:S(2)}, u32[]{:S(2)}) %all-to-all-start.6) | async-done | bytes 90144 | tf_op jit(solution)/shard_map/all_to_all | solution.py:431
  221.6 2.3 %assemble.1 = bf16[656,512]{1,0:T(8,128)(2,1)} custom-call(s32[3]{0:T(128)} %copy-done.26, bf16[384,128]{1,0:T(8,128)(2,1)} %bitcast.60, bf16[384,128]{1,0:T(8,128)(2,1)} %copy-done.32, bf16[384,128]{1,0:T(8,128)(2,1)} %copy-done.31, bf16[384,128]{1,0:T(8,128)(2,1)} %copy-done.30, bf16[4,384,128]{2,1,0:T(8,128)(2,1)} %copy-done.29), custom_call_target="tpu_custom_call" | custom-call | tf_op jit(solution)/shard_map/assemble/pallas_call | solution.py:330
  (97 shorter events, 13.5 us)
Async XLA Ops:
  0.6 1.2 copy-start.9
  1.9 1.1 copy-start.10
  3.0 0.9 copy-start.11
  3.9 0.8 copy-start.25
  13.4 16.4 %copy-start.12 = (bf16[128,512]{1,0:T(8,128)(2,1)S(1)}, bf16[128,512]{1,0:T(8,128)(2,1)}, u32[]{:S(2)}) copy-start(bf16[128,512]{1,0:T(8,128)(2,1)} %refs_2_.3) | copy-start | bytes 393220
  13.4 74.7 %all-to-all-start = ((bf16[32,128,128]{2,1,0:T(8,128)(2,1)}), bf16[32,128,128]{2,1,0:T(8,128)(2,1)S(1)}, u32[]{:S(2)}, u32[]{:S(2)}) async-start(bf16[32,128,128]{2,1,0:T(8,128)(2,1)} %get-tuple-element.54), calls=%async_computation | async-start | bytes 2097152 | tf_op jit(solution)/shard_map/all_to_all | solution.py:472
  29.7 40.3 %copy-start.37 = (bf16[1,128,256]{2,1,0:T(8,128)(2,1)S(1)}, bf16[1,128,256]{2,1,0:T(8,128)(2,1)}, u32[]{:S(2)}) copy-start(bf16[1,128,256]{2,1,0:T(8,128)(2,1)} %param.14) | copy-start | bytes 196612
  29.7 40.4 %copy-start.33 = (bf16[1,128,512]{2,1,0:T(8,128)(2,1)S(1)}, bf16[1,128,512]{2,1,0:T(8,128)(2,1)}, u32[]{:S(2)}) copy-start(bf16[1,128,512]{2,1,0:T(8,128)(2,1)} %param.16) | copy-start | bytes 393220
  29.8 27.0 %copy-start.26 = (s32[3]{0:T(128)}, s32[3]{0:T(128)S(1)}, u32[]{:S(2)}) copy-start(s32[3]{0:T(128)S(1)} %pad_add_fusion.refs_0_.at_ref) | copy-start | bytes 40
  35.6 0.7 copy-start.16
  36.4 60.9 %copy-start.19 = (s32[1,1,4096]{2,1,0:T(1,128)S(1)}, s32[1,1,4096]{2,1,0:T(1,128)}, u32[]{:S(2)}) copy-start(s32[1,1,4096]{2,1,0:T(1,128)} %param.19) | copy-start | bytes 49156
  36.4 4.3 %collective-permute-start = (bf16[4,384,128]{2,1,0:T(8,128)(2,1)S(1)}, bf16[4,384,128]{2,1,0:T(8,128)(2,1)S(1)}, u32[]{:S(2)}, u32[]{:S(2)}) collective-permute-start(bf16[4,384,128]{2,1,0:T(8,128)(2,1)S(1)} %get-tuple-element.48), channel_id=1, source_target_pairs={{0,32},{32,0},{64,96},{96,64},{128,160},{160,128},{192,224},{224,1... | collective-permute-start | bytes 1179656 | tf_op jit(solution)/shard_map/ppermute | solution.py:448
  40.7 0.7 copy-start.28
  43.4 10.6 %collective-permute-start.1 = (bf16[384,128]{1,0:T(8,128)(2,1)}, bf16[384,128]{1,0:T(8,128)(2,1)S(1)}, u32[]{:S(2)}, u32[]{:S(2)}) collective-permute-start(bf16[384,128]{1,0:T(8,128)(2,1)} %get-tuple-element.59), channel_id=1, source_target_pairs={{0,128},{32,160},{64,192},{96,224},{128,256},{160,288},{192,320},{... | collective-permute-start | bytes 294920 | tf_op jit(solution)/shard_map/ppermute | solution.py:444
  46.5 7.5 %collective-permute-start.2 = (bf16[384,128]{1,0:T(8,128)(2,1)}, bf16[384,128]{1,0:T(8,128)(2,1)S(1)}, u32[]{:S(2)}, u32[]{:S(2)}) collective-permute-start(bf16[384,128]{1,0:T(8,128)(2,1)} %get-tuple-element.60), channel_id=1, source_target_pairs={{0,256},{32,288},{64,320},{96,352},{128,384},{160,416},{192,448},{... | collective-permute-start | bytes 294920 | tf_op jit(solution)/shard_map/ppermute | solution.py:444
  50.9 5.9 %collective-permute-start.3 = (bf16[384,128]{1,0:T(8,128)(2,1)}, bf16[384,128]{1,0:T(8,128)(2,1)S(1)}, u32[]{:S(2)}, u32[]{:S(2)}) collective-permute-start(bf16[384,128]{1,0:T(8,128)(2,1)} %get-tuple-element.61), channel_id=1, source_target_pairs={{0,384},{32,416},{64,448},{96,480},{128,0},{160,32},{192,64},{224,... | collective-permute-start | bytes 294920 | tf_op jit(solution)/shard_map/ppermute | solution.py:444
  53.9 2.8 %copy-start.34 = (bf16[384,128]{1,0:T(8,128)(2,1)}, bf16[384,128]{1,0:T(8,128)(2,1)S(1)}, u32[]{:S(2)}) copy-start(bf16[384,128]{1,0:T(8,128)(2,1)S(1)} %collective-permute-done.1.b) | copy-start | bytes 294916
  54.0 2.8 %copy-start.35 = (bf16[384,128]{1,0:T(8,128)(2,1)}, bf16[384,128]{1,0:T(8,128)(2,1)S(1)}, u32[]{:S(2)}) copy-start(bf16[384,128]{1,0:T(8,128)(2,1)S(1)} %collective-permute-done.2.c) | copy-start | bytes 294916
  59.1 26.9 %collective-permute-start.4 = (bf16[96,128]{1,0:T(8,128)(2,1)}, bf16[96,128]{1,0:T(8,128)(2,1)S(1)}, u32[]{:S(2)}, u32[]{:S(2)}) collective-permute-start(bf16[96,128]{1,0:T(8,128)(2,1)} %get-tuple-element.63), channel_id=1, source_target_pairs={{0,8},{1,9},{2,10},{3,11},{4,12},{5,13},{6,14},{7,15},{8,16},{9,17... | collective-permute-start | bytes 73736 | tf_op jit(solution)/shard_map/ppermute | solution.py:444
  62.5 23.5 %collective-permute-start.5 = (bf16[96,128]{1,0:T(8,128)(2,1)}, bf16[96,128]{1,0:T(8,128)(2,1)S(1)}, u32[]{:S(2)}, u32[]{:S(2)}) collective-permute-start(bf16[96,128]{1,0:T(8,128)(2,1)} %get-tuple-element.64), channel_id=1, source_target_pairs={{0,16},{1,17},{2,18},{3,19},{4,20},{5,21},{6,22},{7,23},{8,24},{9,... | collective-permute-start | bytes 73736 | tf_op jit(solution)/shard_map/ppermute | solution.py:444
  66.9 19.2 %collective-permute-start.6 = (bf16[96,128]{1,0:T(8,128)(2,1)}, bf16[96,128]{1,0:T(8,128)(2,1)S(1)}, u32[]{:S(2)}, u32[]{:S(2)}) collective-permute-start(bf16[96,128]{1,0:T(8,128)(2,1)} %get-tuple-element.65), channel_id=1, source_target_pairs={{0,24},{1,25},{2,26},{3,27},{4,28},{5,29},{6,30},{7,31},{8,0},{9,1... | collective-permute-start | bytes 73736 | tf_op jit(solution)/shard_map/ppermute | solution.py:444
  72.0 1.0 copy-start
  88.1 27.1 %all-to-all-start.1 = ((bf16[16,8,128]{2,1,0:T(8,128)(2,1)}), bf16[16,8,128]{2,1,0:T(8,128)(2,1)S(1)}, u32[]{:S(2)}, u32[]{:S(2)}) async-start(bf16[16,8,128]{2,1,0:T(8,128)(2,1)} %bitcast.65), calls=%async_computation.1 | async-start | bytes 65536 | tf_op jit(solution)/shard_map/all_to_all | solution.py:431
  97.3 1.0 copy-start.1
  99.1 28.2 %copy-start.15 = (s32[32,128]{1,0:T(8,128)S(1)}, s32[32,128]{1,0:T(8,128)}, u32[]{:S(2)}) copy-start(s32[32,128]{1,0:T(8,128)} %digits.1.sorted_ref.refs_1_) | copy-start | bytes 49156
  113.0 0.8 copy-start.4
  115.8 30.8 %all-to-all-start.2 = ((bf16[16,8,128]{2,1,0:T(8,128)(2,1)}), bf16[16,8,128]{2,1,0:T(8,128)(2,1)S(1)}, u32[]{:S(2)}, u32[]{:S(2)}) async-start(bf16[16,8,128]{2,1,0:T(8,128)(2,1)} %broadcast_in_dim.4), calls=%async_computation.2 | async-start | bytes 65536 | tf_op jit(solution)/shard_map/all_to_all | solution.py:431
  127.3 1.0 copy-start.2
  128.3 1.0 copy-start.5
  129.4 0.9 copy-start.18
  130.3 0.9 copy-start.24
  145.2 0.8 copy-start.6
  147.3 24.1 %all-to-all-start.3 = ((bf16[4,96,128]{2,1,0:T(8,128)(2,1)}), bf16[4,96,128]{2,1,0:T(8,128)(2,1)S(1)}, u32[]{:S(2)}, u32[]{:S(2)}) async-start(bf16[4,96,128]{2,1,0:T(8,128)(2,1)} %broadcast_in_dim.5), calls=%async_computation.3 | async-start | bytes 196608 | tf_op jit(solution)/shard_map/all_to_all | solution.py:431
  150.6 1.0 copy-start.3
  151.7 1.0 copy-start.7
  152.7 0.9 copy-start.22
  169.9 0.8 copy-start.8
  171.4 35.1 %copy-start.27 = (bf16[4,96,128]{2,1,0:T(8,128)(2,1)}, bf16[4,96,128]{2,1,0:T(8,128)(2,1)S(1)}, u32[]{:S(2)}) copy-start(bf16[4,96,128]{2,1,0:T(8,128)(2,1)S(1)} %all-to-all-done.3) | copy-start | bytes 294916
  181.0 13.2 %all-to-all-start.5 = ((bf16[4,2,176,128]{3,2,1,0:T(8,128)(2,1)}), bf16[4,2,176,128]{3,2,1,0:T(8,128)(2,1)S(1)}, u32[]{:S(2)}, u32[]{:S(2)}) async-start(bf16[4,2,176,128]{3,2,1,0:T(8,128)(2,1)} %bitcast.18), calls=%async_computation.5 | async-start | bytes 720896 | tf_op jit(solution)/shard_map/all_to_all | solution.py:431
  184.6 21.9 %collective-permute-start.9 = (bf16[384,128]{1,0:T(8,128)(2,1)S(1)}, bf16[384,128]{1,0:T(8,128)(2,1)S(1)}, u32[]{:S(2)}, u32[]{:S(2)}) collective-permute-start(bf16[384,128]{1,0:T(8,128)(2,1)S(1)} %bitcast.56), channel_id=1, source_target_pairs={{0,384},{32,416},{64,448},{96,480},{128,0},{160,32},{192,64},{224,... | collective-permute-start | bytes 294920 | tf_op jit(solution)/shard_map/ppermute | solution.py:444
  189.2 17.3 %collective-permute-start.8 = (bf16[384,128]{1,0:T(8,128)(2,1)S(1)}, bf16[384,128]{1,0:T(8,128)(2,1)S(1)}, u32[]{:S(2)}, u32[]{:S(2)}) collective-permute-start(bf16[384,128]{1,0:T(8,128)(2,1)S(1)} %bitcast.57), channel_id=1, source_target_pairs={{0,256},{32,288},{64,320},{96,352},{128,384},{160,416},{192,448},{... | collective-permute-start | bytes 294920 | tf_op jit(solution)/shard_map/ppermute | solution.py:444
  191.7 14.8 %collective-permute-start.7 = (bf16[384,128]{1,0:T(8,128)(2,1)S(1)}, bf16[384,128]{1,0:T(8,128)(2,1)S(1)}, u32[]{:S(2)}, u32[]{:S(2)}) collective-permute-start(bf16[384,128]{1,0:T(8,128)(2,1)S(1)} %bitcast.58), channel_id=1, source_target_pairs={{0,128},{32,160},{64,192},{96,224},{128,256},{160,288},{192,320},{... | collective-permute-start | bytes 294920 | tf_op jit(solution)/shard_map/ppermute | solution.py:444
  194.9 24.0 %all-to-all-start.6 = ((bf16[2,176,128]{2,1,0:T(8,128)(2,1)}), bf16[2,176,128]{2,1,0:T(8,128)(2,1)S(1)}, u32[]{:S(2)}, u32[]{:S(2)}) async-start(bf16[2,176,128]{2,1,0:T(8,128)(2,1)} %reduce_sum.47), calls=%async_computation.6 | async-start | bytes 180224 | tf_op jit(solution)/shard_map/all_to_all | solution.py:431
  206.5 14.4 %copy-start.30 = (bf16[384,128]{1,0:T(8,128)(2,1)}, bf16[384,128]{1,0:T(8,128)(2,1)S(1)}, u32[]{:S(2)}) copy-start(bf16[384,128]{1,0:T(8,128)(2,1)S(1)} %collective-permute-done.9.d) | copy-start | bytes 294916
  206.5 14.4 %copy-start.31 = (bf16[384,128]{1,0:T(8,128)(2,1)}, bf16[384,128]{1,0:T(8,128)(2,1)S(1)}, u32[]{:S(2)}) copy-start(bf16[384,128]{1,0:T(8,128)(2,1)S(1)} %collective-permute-done.8.c) | copy-start | bytes 294916
  206.5 14.4 %copy-start.32 = (bf16[384,128]{1,0:T(8,128)(2,1)}, bf16[384,128]{1,0:T(8,128)(2,1)S(1)}, u32[]{:S(2)}) copy-start(bf16[384,128]{1,0:T(8,128)(2,1)S(1)} %collective-permute-done.7.b) | copy-start | bytes 294916
  206.6 14.3 %collective-permute-start.10 = (bf16[4,384,128]{2,1,0:T(8,128)(2,1)S(1)}, bf16[4,384,128]{2,1,0:T(8,128)(2,1)S(1)}, u32[]{:S(2)}, u32[]{:S(2)}) collective-permute-start(bf16[4,384,128]{2,1,0:T(8,128)(2,1)S(1)} %pad_maximum_fusion.1), channel_id=1, source_target_pairs={{0,32},{32,0},{64,96},{96,64},{128,160},{160,128},{192,224},{224,1... | collective-permute-start | bytes 1179656 | tf_op jit(solution)/shard_map/ppermute | solution.py:448
  220.9 0.8 copy-start.29
  (10 other events, 6.6 us)

commit v3 on v2

--- a/solution.py
+++ b/solution.py
@@ -109,20 +109,17 @@
 
 
 def join_y_kernel(a, b, c, d, out):
-    total = total_of((a, b, c, d))
-    fill = jnp.zeros((out.shape[0] - total.shape[0], total.shape[1]), F32)
-    out[...] = jnp.concatenate([total, fill], axis=0).astype(BF)
-
-
-def assemble_kernel(at_ref, a, b, c, d, other_ref, out, wide):
-    x, core = at_ref[0], at_ref[1]
+    out[...] = total_of((a, b, c, d)).astype(BF)
+
+
+def assemble_kernel(at_ref, mine_ref, other_ref, out, wide):
+    core = at_ref[1]
     rows = out.shape[0] // 2
-    for n, mine in enumerate((a, b, c, d)):
-        own, other = mine[...].astype(F32), other_ref[n].astype(F32)
+    for n in range(mine_ref.shape[0]):
+        own, other = mine_ref[n].astype(F32), other_ref[n].astype(F32)
         low = jnp.where(core == 0, own, other)[:rows]
         high = jnp.where(core == 0, other, own)[:rows]
-        column = pl.ds(pl.multiple_of((x + 4 - n) % 4 * LANES, LANES), LANES)
-        wide[:, column] = jnp.concatenate([low, high], axis=0)
+        wide[:, n * LANES : (n + 1) * LANES] = jnp.concatenate([low, high], axis=0)
     out[...] = wide[...].astype(BF)
 
 
@@ -322,14 +319,14 @@
 
 def join_y(*parts):
     return pl.pallas_call(
-        join_y_kernel, out_shape=jax.ShapeDtypeStruct((LANES, LANES), BF), name="join_y"
+        join_y_kernel, out_shape=jax.ShapeDtypeStruct(parts[0].shape, BF), name="join_y"
     )(*parts)
 
 
 def assemble(where, shape, *parts):
     return pl.pallas_call(
         assemble_kernel,
-        in_specs=[SMEM] + [VMEM] * 5,
+        in_specs=[SMEM, VMEM, VMEM],
         out_shape=jax.ShapeDtypeStruct(shape, BF),
         scratch_shapes=[pltpu.VMEM(shape, F32)],
         name="assemble",
@@ -415,7 +412,7 @@
     )(order, sorted_digits, received, left, right, chained, core_two, *old)
 
 
-CUTS = 5, 10
+CUT = 8
 AXES = {"x": 4, "z_hi": 2, "core": 2, "y": 4, "z_lo": 8}
 
 
@@ -490,21 +487,23 @@
     def piece(begin, end, old):
         return after(begin, end, received, order, sorted_digits, links, core_mid[0], scale, reps, old)
 
-    two, one, three = piece(0, CUTS[0], ())
-    summed = add_up(partial.reshape(16, SUB, LANES), "z_hi", "z_lo").astype(BF)
+    two, one, three = piece(0, CUT, ())
+    copies = gather_up(partial, 16, "z_hi", "z_lo")
+    summed = jnp.sum(copies.astype(F32), axis=0).astype(BF)
     one, summed = lax.optimization_barrier((one, summed))
-    two, one, three = piece(CUTS[0], CUTS[1], (one, three, two))
-    summed = gather_up(summed, 16, "z_hi", "z_lo").reshape(LANES, LANES)[:quarter]
-    one, summed = lax.optimization_barrier((one, summed))
-    two, rest = piece(CUTS[1], I2, (one, three, two))
-    summed = gather_up(summed, 4, "y").reshape(padded, LANES)
-    rest, summed = lax.optimization_barrier((rest, summed))
-    mine = [summed] + [shift(summed, "rep", n) for n in (1, 2, 3)]
-    grad_top = assemble(where, (rows, top_grad.shape[1]), *mine, swap_core(jnp.stack(mine)))
+    two, rest = piece(CUT, I2, (one, three, two))
+    mine = gather_up(summed, 16, "x", "y").reshape(4, padded, LANES)
+    rest, mine = lax.optimization_barrier((rest, mine))
     parts = jnp.concatenate([two, rest], axis=1)
     parts = add_up(parts.reshape(2, 8, -1, LANES), "core").astype(BF)
-    parts = add_up(parts.reshape(4, 2, -1, LANES), "x").astype(BF)
-    share = add_up(parts, "z_hi")
+    parts = add_up(parts.reshape(4, 2, -1, LANES), "x")
+    other_z = lax.ppermute(
+        lax.dynamic_index_in_dim(parts, 1 - (rep >> 1 & 1), 0, False).astype(BF),
+        "rep",
+        [(i, i ^ 2) for i in range(16)],
+    )
+    share = lax.dynamic_index_in_dim(parts, rep >> 1 & 1, 0, False) + other_z.astype(F32)
+    grad_top = assemble(where, (rows, top_grad.shape[1]), mine, swap_core(mine))
     size_two = R * D2 * R // LANES
     size_one = I1 // reps * D1 * R // LANES
     widths = D2 * R // LANES, D1 * R // LANES, D3 * R // LANES

time: 228 us -> 197 us (0.86)
  starting transfers between devices: 93.3 us -> 74.5 us
  local copies, waits for them, and re-layouts: 26.4 us -> 20.7 us
  Pallas kernels: 80.3 us -> 77.8 us
    all_to_all x5 -> x3, starting transfers between devices: 39.2 us -> 17.7 us  [swap(): lax.all_to_all(array, ('rep', 'tab'), 0, 0, axis_index_groups=groups_of(*...]
    ppermute x0 -> x1, starting transfers between devices: none -> 12.2 us  [on_device(): lax.ppermute(lax.dynamic_index_in_dim(parts, 1 - (rep >> 1 & 1), 0, False...]
    ppermute x9 -> x6, starting transfers between devices: 30.9 us -> 21.5 us  [shift(): lax.ppermute(array, axis, [(i, (i + by * step) % number) for i in range(n...]
    unnamed x84 -> x60, local copies, waits for them, and re-layouts: 23.2 us -> 16.4 us
    pallas_call x3 -> x2, Pallas kernels: 44.2 us -> 41.9 us  [after(): pl.pallas_call(lambda *refs: after_kernel(scale, begin, reps if last else...]
    all_to_all x5 -> x3, waiting for transfers between devices: 8.33 us -> 6.87 us  [swap(): lax.all_to_all(array, ('rep', 'tab'), 0, 0, axis_index_groups=groups_of(*...]
  transfers between devices with their start and end apart: 17 -> 13, of which waited for: 3 -> 3; matrix products, arithmetic and copies ran while one was open for 1% -> 1% of each run, Pallas kernels for 31% -> 34%
where the time goes in v3:
time: 197 us; the launch traced here: 195 us
  Pallas kernels  77.8 us (39%)
  starting transfers between devices  74.5 us (38%)
  local copies, waits for them, and re-layouts  20.7 us (11%)
  waiting for transfers between devices  11 us (6%)
  blocking collectives  6.84 us (3%)
  other arithmetic  3.33 us (2%)
    pallas_call x2, Pallas kernels, after(): pl.pallas_call(lambda *refs: after_kernel(scale, begin, reps if last else...  41.9 us
    ppermute x6, starting transfers between devices, shift(): lax.ppermute(array, axis, [(i, (i + by * step) % number) for i in range(n...  21.5 us
    all_to_all x3, starting transfers between devices, swap(): lax.all_to_all(array, ('rep', 'tab'), 0, 0, axis_index_groups=groups_of(*...  17.7 us
    unnamed x60, local copies, waits for them, and re-layouts  16.4 us
    all_to_all x1, starting transfers between devices, on_device(): lax.all_to_all(grad_rows, 'tab', split_axis=0, concat_axis=0, tiled=True)  16.2 us
    pallas_call x1, Pallas kernels, before(): pl.pallas_call(before_kernel, grid=(I2,), in_specs=[whole(table), whole((...  12.3 us
    ppermute x1, starting transfers between devices, on_device(): lax.ppermute(lax.dynamic_index_in_dim(parts, 1 - (rep >> 1 & 1), 0, False...  12.2 us
    pallas_call x1, Pallas kernels, dense(): pl.pallas_call(lambda *refs: dense_kernel(count, *refs), out_shape=(jax.S...  8.79 us
  transfers between devices with their start and end apart: 13, of which 3 were waited for; matrix products, arithmetic and copies ran while one was open for 1% of the time, Pallas kernels for 34%

profile of v3, /device:TPU:1, one launch (start us, length us, event | category | flops | bytes accessed | tf_op | source)
XLA Modules:
  0.0 195.2 jit_solution(16579606767522923559)
XLA Ops:
  0.6 1.2 copy-done.6
  1.9 1.1 copy-done.7
  3.0 0.9 copy-done.8
  3.9 0.8 copy-done.17
  4.6 8.8 %dense.1 = (bf16[32,128,128]{2,1,0:T(8,128)(2,1)}, bf16[128,128]{1,0:T(8,128)(2,1)}, bf16[33,128,128]{2,1,0:T(8,128)(2,1)S(1)}) custom-call(bf16[128,128]{1,0:T(8,128)(2,1)S(1)} %copy-done.17, bf16[4096,128]{1,0:T(8,128)(2,1)S(1)} %bitcast.43, bf16[128,512]{1,0:T(8,128)(2,1)S(1)} %copy-done.8, bf16[656,512]{1,0:T(8,128)(2,1)S(1)} %copy-done.7), custom_call_target="tpu_custom_call" | custom-call | tf_op jit(solution)/shard_map/dense/pallas_call | solution.py:268
  13.4 16.2 %all-to-all-start = ((bf16[32,128,128]{2,1,0:T(8,128)(2,1)}), bf16[32,128,128]{2,1,0:T(8,128)(2,1)S(1)}, u32[]{:S(2)}, u32[]{:S(2)}) async-start(bf16[32,128,128]{2,1,0:T(8,128)(2,1)} %get-tuple-element.49), calls=%async_computation | async-start | bytes 2097152 | tf_op jit(solution)/shard_map/all_to_all | solution.py:469
  29.8 5.9 %gram.1 = (bf16[4,384,128]{2,1,0:T(8,128)(2,1)S(1)}, bf16[4,384,128]{2,1,0:T(8,128)(2,1)S(1)}) custom-call(s32[3]{0:T(128)S(1)} %pad_add_fusion.refs_0_.at_ref, bf16[33,128,128]{2,1,0:T(8,128)(2,1)S(1)} %get-tuple-element.41.refs_1_, bf16[128,512]{1,0:T(8,128)(2,1)S(1)} %copy-done.9), custom_call_target="tpu_custom_call" | custom-call | tf_op jit(solution)/shard_map/gram/pallas_call | solution.py:289
  35.6 0.7 copy-done.10
  36.4 2.9 %collective-permute-start = (bf16[4,384,128]{2,1,0:T(8,128)(2,1)S(1)}, bf16[4,384,128]{2,1,0:T(8,128)(2,1)S(1)}, u32[]{:S(2)}, u32[]{:S(2)}) collective-permute-start(bf16[4,384,128]{2,1,0:T(8,128)(2,1)S(1)} %get-tuple-element.43), channel_id=1, source_target_pairs={{0,32},{32,0},{64,96},{96,64},{128,160},{160,128},{192,224},{224,1... | collective-permute-start | bytes 1179656 | tf_op jit(solution)/shard_map/ppermute | solution.py:445
  39.2 1.3 collective-permute-done.came_ref
  40.6 0.7 copy-done.19
  41.3 1.9 join_core.1
  43.2 3.2 %collective-permute-start.1 = (bf16[384,128]{1,0:T(8,128)(2,1)}, bf16[384,128]{1,0:T(8,128)(2,1)S(1)}, u32[]{:S(2)}, u32[]{:S(2)}) collective-permute-start(bf16[384,128]{1,0:T(8,128)(2,1)} %get-tuple-element.54), channel_id=1, source_target_pairs={{0,128},{32,160},{64,192},{96,224},{128,256},{160,288},{192,320},{... | collective-permute-start | bytes 294920 | tf_op jit(solution)/shard_map/ppermute | solution.py:441
  46.5 4.4 %collective-permute-start.2 = (bf16[384,128]{1,0:T(8,128)(2,1)}, bf16[384,128]{1,0:T(8,128)(2,1)S(1)}, u32[]{:S(2)}, u32[]{:S(2)}) collective-permute-start(bf16[384,128]{1,0:T(8,128)(2,1)} %get-tuple-element.55), channel_id=1, source_target_pairs={{0,256},{32,288},{64,320},{96,352},{128,384},{160,416},{192,448},{... | collective-permute-start | bytes 294920 | tf_op jit(solution)/shard_map/ppermute | solution.py:441
  50.8 3.1 %collective-permute-start.3 = (bf16[384,128]{1,0:T(8,128)(2,1)}, bf16[384,128]{1,0:T(8,128)(2,1)S(1)}, u32[]{:S(2)}, u32[]{:S(2)}) collective-permute-start(bf16[384,128]{1,0:T(8,128)(2,1)} %get-tuple-element.56), channel_id=1, source_target_pairs={{0,384},{32,416},{64,448},{96,480},{128,0},{160,32},{192,64},{224,... | collective-permute-start | bytes 294920 | tf_op jit(solution)/shard_map/ppermute | solution.py:441
  53.9 2.8 %collective-permute-done.3.d = bf16[384,128]{1,0:T(8,128)(2,1)S(1)} collective-permute-done((bf16[384,128]{1,0:T(8,128)(2,1)}, bf16[384,128]{1,0:T(8,128)(2,1)S(1)}, u32[]{:S(2)}, u32[]{:S(2)}) %collective-permute-start.3) | collective-permute-done | bytes 98336 | tf_op jit(solution)/shard_map/ppermute | solution.py:441
  57.4 1.7 join_x.1
  59.1 3.4 %collective-permute-start.4 = (bf16[96,128]{1,0:T(8,128)(2,1)}, bf16[96,128]{1,0:T(8,128)(2,1)S(1)}, u32[]{:S(2)}, u32[]{:S(2)}) collective-permute-start(bf16[96,128]{1,0:T(8,128)(2,1)} %get-tuple-element.58), channel_id=1, source_target_pairs={{0,8},{1,9},{2,10},{3,11},{4,12},{5,13},{6,14},{7,15},{8,16},{9,17... | collective-permute-start | bytes 73736 | tf_op jit(solution)/shard_map/ppermute | solution.py:441
  62.5 4.3 %collective-permute-start.5 = (bf16[96,128]{1,0:T(8,128)(2,1)}, bf16[96,128]{1,0:T(8,128)(2,1)S(1)}, u32[]{:S(2)}, u32[]{:S(2)}) collective-permute-start(bf16[96,128]{1,0:T(8,128)(2,1)} %get-tuple-element.59), channel_id=1, source_target_pairs={{0,16},{1,17},{2,18},{3,19},{4,20},{5,21},{6,22},{7,23},{8,24},{9,... | collective-permute-start | bytes 73736 | tf_op jit(solution)/shard_map/ppermute | solution.py:441
  66.9 3.1 %collective-permute-start.6 = (bf16[96,128]{1,0:T(8,128)(2,1)}, bf16[96,128]{1,0:T(8,128)(2,1)S(1)}, u32[]{:S(2)}, u32[]{:S(2)}) collective-permute-start(bf16[96,128]{1,0:T(8,128)(2,1)} %get-tuple-element.60), channel_id=1, source_target_pairs={{0,24},{1,25},{2,26},{3,27},{4,28},{5,29},{6,30},{7,31},{8,0},{9,1... | collective-permute-start | bytes 73736 | tf_op jit(solution)/shard_map/ppermute | solution.py:441
  70.2 1.8 digits.1.sorted_ref.refs_1_
  72.0 1.0 copy-done
  73.0 0.7 copy-done.11
  73.7 12.3 %before.1 = (bf16[256,4096]{1,0:T(8,128)(2,1)S(1)}, bf16[512,4096]{1,0:T(8,128)(2,1)}, bf16[1024,4096]{1,0:T(8,128)(2,1)}) custom-call(s32[32,128]{1,0:T(8,128)S(1)} %copy-done.11, bf16[256,128]{1,0:T(8,128)(2,1)S(1)} %bitcast.45, bf16[16,64,256]{2,1,0:T(8,128)(2,1)S(1)} %bitcast.40, bf16[512,128]{1,0:T(8,128)(2,1)S(1)} %bitcast.44), custom_call_target="tpu_custom_call" | custom-call | tf_op jit(solution)/shard_map/before/pallas_call | solution.py:343
  86.7 1.4 join_y.1
  88.1 1.6 broadcast_in_dim.4
  89.7 9.2 %all-to-all-start.1 = ((bf16[16,96,128]{2,1,0:T(8,128)(2,1)}), bf16[16,96,128]{2,1,0:T(8,128)(2,1)}, u32[]{:S(2)}, u32[]{:S(2)}) async-start(bf16[16,96,128]{2,1,0:T(8,128)(2,1)} %broadcast_in_dim.4), calls=%async_computation.1 | async-start | bytes 786432 | tf_op jit(solution)/shard_map/all_to_all | solution.py:428
  99.0 1.0 copy-done.1
  100.0 20.9 %after.2 = (bf16[16,128,128]{2,1,0:T(8,128)(2,1)S(1)}, f32[128,256]{1,0:T(8,128)S(1)}, f32[128,512]{1,0:T(8,128)S(1)}) custom-call(s32[4096]{0:T(1024)S(1)} %bitcast.47, s32[32,128]{1,0:T(8,128)S(1)} %copy-done.12, bf16[4096,128]{1,0:T(8,128)(2,1)S(1)} %bitcast.38, bf16[256,4096]{1,0:T(8,128)(2,1)S(1)} %get-tuple-element.63.refs_3_, ...), custom_call_target="tpu_custom_call" | custom-call | tf_op jit(solution)/shard_map/after/pallas_call | solution.py:378
  121.0 0.8 copy-done.3
  122.4 1.1 reduce_sum.33
  123.5 0.8 broadcast_in_dim.5
  124.3 4.2 %all-to-all-start.2 = ((bf16[16,96,128]{2,1,0:T(8,128)(2,1)}), bf16[16,96,128]{2,1,0:T(8,128)(2,1)}, u32[]{:S(2)}, u32[]{:S(2)}) async-start(bf16[16,96,128]{2,1,0:T(8,128)(2,1)} %broadcast_in_dim.5), calls=%async_computation.2 | async-start | bytes 786432 | tf_op jit(solution)/shard_map/all_to_all | solution.py:428
  128.5 1.0 copy-done.2
  129.5 1.0 copy-done.4
  130.6 0.9 copy-done.16
  131.5 20.9 %after.3 = (bf16[16,128,128]{2,1,0:T(8,128)(2,1)S(1)}, bf16[16,48,128]{2,1,0:T(8,128)(2,1)S(1)}) custom-call(s32[4096]{0:T(1024)S(1)} %bitcast.48, s32[32,128]{1,0:T(8,128)S(1)} %copy-done.12, bf16[4096,128]{1,0:T(8,128)(2,1)S(1)} %bitcast.39, bf16[256,4096]{1,0:T(8,128)(2,1)S(1)} %get-tuple-element.63.refs_3_, ...), custom_call_target="tpu_custom_call", output_to_operand_aliasing={{0}: (9, {})} | custom-call | tf_op jit(solution)/shard_map/after/pallas_call | solution.py:378
  152.4 0.8 copy-done.5
  153.9 1.2 pad_maximum_fusion
  155.1 6.8 %all_to_all.25 = bf16[2,8,176,128]{3,2,1,0:T(8,128)(2,1)S(1)} all-to-all(bf16[2,8,176,128]{3,2,1,0:T(8,128)(2,1)S(1)} %bitcast.49), channel_id=1, replica_groups={{0,32},{1,33},{2,34},{3,35},{4,36},{5,37},{6,38},{7,39},{8,40},{9,41},{..., dimensions={0} | all-to-all | bytes 1441792 | tf_op jit(solution)/shard_map/all_to_all | solution.py:428
  161.9 0.9 reduce_sum.34
  162.9 4.3 %all-to-all-start.4 = ((bf16[4,2,176,128]{3,2,1,0:T(8,128)(2,1)}), bf16[4,2,176,128]{3,2,1,0:T(8,128)(2,1)S(1)}, u32[]{:S(2)}, u32[]{:S(2)}) async-start(bf16[4,2,176,128]{3,2,1,0:T(8,128)(2,1)} %bitcast.16), calls=%async_computation.4 | async-start | bytes 720896 | tf_op jit(solution)/shard_map/all_to_all | solution.py:428
  167.2 6.9 %all-to-all-done.4 = bf16[4,2,176,128]{3,2,1,0:T(8,128)(2,1)S(1)} async-done(((bf16[4,2,176,128]{3,2,1,0:T(8,128)(2,1)}), bf16[4,2,176,128]{3,2,1,0:T(8,128)(2,1)S(1)}, u32[]{:S(2)}, u32[]{:S(2)}) %all-to-all-start.4) | async-done | bytes 360480 | tf_op jit(solution)/shard_map/all_to_all | solution.py:428
  174.1 12.2 %collective-permute-start.7 = (bf16[176,128]{1,0:T(8,128)(2,1)S(1)}, bf16[176,128]{1,0:T(8,128)(2,1)S(1)}, u32[]{:S(2)}, u32[]{:S(2)}) collective-permute-start(bf16[176,128]{1,0:T(8,128)(2,1)S(1)} %fusion), channel_id=1, source_target_pairs={{0,64},{32,96},{64,0},{96,32},{128,192},{160,224},{192,128},{224,1... | collective-permute-start | bytes 135176 | tf_op jit(solution)/shard_map/ppermute | solution.py:500
  186.3 4.0 %collective-permute-start.8 = (bf16[4,384,128]{2,1,0:T(8,128)(2,1)}, bf16[4,384,128]{2,1,0:T(8,128)(2,1)S(1)}, u32[]{:S(2)}, u32[]{:S(2)}) collective-permute-start(bf16[4,384,128]{2,1,0:T(8,128)(2,1)} %bitcast.14.mine_ref), channel_id=1, source_target_pairs={{0,32},{32,0},{64,96},{96,64},{128,160},{160,128},{192,224},{224,1... | collective-permute-start | bytes 1179656 | tf_op jit(solution)/shard_map/ppermute | solution.py:445
  190.5 0.7 broadcast_in_dim_reshape.3
  192.4 0.7 copy-done.20
  193.1 2.1 %assemble.1 = bf16[656,512]{1,0:T(8,128)(2,1)} custom-call(s32[3]{0:T(128)} %copy-done.18, bf16[4,384,128]{2,1,0:T(8,128)(2,1)} %bitcast.14.mine_ref, bf16[4,384,128]{2,1,0:T(8,128)(2,1)} %copy-done.20), custom_call_target="tpu_custom_call" | custom-call | tf_op jit(solution)/shard_map/assemble/pallas_call | solution.py:327
  (63 shorter events, 4.3 us)
Async XLA Ops:
  0.6 1.2 copy-start.6
  1.9 1.1 copy-start.7
  3.0 0.9 copy-start.8
  3.9 0.8 copy-start.17
  13.4 16.4 %copy-start.9 = (bf16[128,512]{1,0:T(8,128)(2,1)S(1)}, bf16[128,512]{1,0:T(8,128)(2,1)}, u32[]{:S(2)}) copy-start(bf16[128,512]{1,0:T(8,128)(2,1)} %refs_2_.3) | copy-start | bytes 393220
  13.4 74.7 %all-to-all-start = ((bf16[32,128,128]{2,1,0:T(8,128)(2,1)}), bf16[32,128,128]{2,1,0:T(8,128)(2,1)S(1)}, u32[]{:S(2)}, u32[]{:S(2)}) async-start(bf16[32,128,128]{2,1,0:T(8,128)(2,1)} %get-tuple-element.49), calls=%async_computation | async-start | bytes 2097152 | tf_op jit(solution)/shard_map/all_to_all | solution.py:469
  29.6 40.3 %copy-start.25 = (bf16[1,128,256]{2,1,0:T(8,128)(2,1)S(1)}, bf16[1,128,256]{2,1,0:T(8,128)(2,1)}, u32[]{:S(2)}) copy-start(bf16[1,128,256]{2,1,0:T(8,128)(2,1)} %param.14) | copy-start | bytes 196612
  29.7 40.4 %copy-start.21 = (bf16[1,128,512]{2,1,0:T(8,128)(2,1)S(1)}, bf16[1,128,512]{2,1,0:T(8,128)(2,1)}, u32[]{:S(2)}) copy-start(bf16[1,128,512]{2,1,0:T(8,128)(2,1)} %param.16) | copy-start | bytes 393220
  29.8 26.9 %copy-start.18 = (s32[3]{0:T(128)}, s32[3]{0:T(128)S(1)}, u32[]{:S(2)}) copy-start(s32[3]{0:T(128)S(1)} %pad_add_fusion.refs_0_.at_ref) | copy-start | bytes 40
  35.6 0.7 copy-start.10
  36.4 4.2 %collective-permute-start = (bf16[4,384,128]{2,1,0:T(8,128)(2,1)S(1)}, bf16[4,384,128]{2,1,0:T(8,128)(2,1)S(1)}, u32[]{:S(2)}, u32[]{:S(2)}) collective-permute-start(bf16[4,384,128]{2,1,0:T(8,128)(2,1)S(1)} %get-tuple-element.43), channel_id=1, source_target_pairs={{0,32},{32,0},{64,96},{96,64},{128,160},{160,128},{192,224},{224,1... | collective-permute-start | bytes 1179656 | tf_op jit(solution)/shard_map/ppermute | solution.py:445
  40.6 0.7 copy-start.19
  43.2 55.7 %copy-start.14 = (s32[1,1,4096]{2,1,0:T(1,128)S(1)}, s32[1,1,4096]{2,1,0:T(1,128)}, u32[]{:S(2)}) copy-start(s32[1,1,4096]{2,1,0:T(1,128)} %param.19) | copy-start | bytes 49156
  43.2 10.7 %collective-permute-start.1 = (bf16[384,128]{1,0:T(8,128)(2,1)}, bf16[384,128]{1,0:T(8,128)(2,1)S(1)}, u32[]{:S(2)}, u32[]{:S(2)}) collective-permute-start(bf16[384,128]{1,0:T(8,128)(2,1)} %get-tuple-element.54), channel_id=1, source_target_pairs={{0,128},{32,160},{64,192},{96,224},{128,256},{160,288},{192,320},{... | collective-permute-start | bytes 294920 | tf_op jit(solution)/shard_map/ppermute | solution.py:441
  46.5 7.5 %collective-permute-start.2 = (bf16[384,128]{1,0:T(8,128)(2,1)}, bf16[384,128]{1,0:T(8,128)(2,1)S(1)}, u32[]{:S(2)}, u32[]{:S(2)}) collective-permute-start(bf16[384,128]{1,0:T(8,128)(2,1)} %get-tuple-element.55), channel_id=1, source_target_pairs={{0,256},{32,288},{64,320},{96,352},{128,384},{160,416},{192,448},{... | collective-permute-start | bytes 294920 | tf_op jit(solution)/shard_map/ppermute | solution.py:441
  50.8 5.9 %collective-permute-start.3 = (bf16[384,128]{1,0:T(8,128)(2,1)}, bf16[384,128]{1,0:T(8,128)(2,1)S(1)}, u32[]{:S(2)}, u32[]{:S(2)}) collective-permute-start(bf16[384,128]{1,0:T(8,128)(2,1)} %get-tuple-element.56), channel_id=1, source_target_pairs={{0,384},{32,416},{64,448},{96,480},{128,0},{160,32},{192,64},{224,... | collective-permute-start | bytes 294920 | tf_op jit(solution)/shard_map/ppermute | solution.py:441
  53.9 2.8 %copy-start.22 = (bf16[384,128]{1,0:T(8,128)(2,1)}, bf16[384,128]{1,0:T(8,128)(2,1)S(1)}, u32[]{:S(2)}) copy-start(bf16[384,128]{1,0:T(8,128)(2,1)S(1)} %collective-permute-done.1.b) | copy-start | bytes 294916
  53.9 2.8 %copy-start.23 = (bf16[384,128]{1,0:T(8,128)(2,1)}, bf16[384,128]{1,0:T(8,128)(2,1)S(1)}, u32[]{:S(2)}) copy-start(bf16[384,128]{1,0:T(8,128)(2,1)S(1)} %collective-permute-done.2.c) | copy-start | bytes 294916
  56.7 0.6 copy-start.24
  59.1 27.0 %collective-permute-start.4 = (bf16[96,128]{1,0:T(8,128)(2,1)}, bf16[96,128]{1,0:T(8,128)(2,1)S(1)}, u32[]{:S(2)}, u32[]{:S(2)}) collective-permute-start(bf16[96,128]{1,0:T(8,128)(2,1)} %get-tuple-element.58), channel_id=1, source_target_pairs={{0,8},{1,9},{2,10},{3,11},{4,12},{5,13},{6,14},{7,15},{8,16},{9,17... | collective-permute-start | bytes 73736 | tf_op jit(solution)/shard_map/ppermute | solution.py:441
  62.5 23.6 %collective-permute-start.5 = (bf16[96,128]{1,0:T(8,128)(2,1)}, bf16[96,128]{1,0:T(8,128)(2,1)S(1)}, u32[]{:S(2)}, u32[]{:S(2)}) collective-permute-start(bf16[96,128]{1,0:T(8,128)(2,1)} %get-tuple-element.59), channel_id=1, source_target_pairs={{0,16},{1,17},{2,18},{3,19},{4,20},{5,21},{6,22},{7,23},{8,24},{9,... | collective-permute-start | bytes 73736 | tf_op jit(solution)/shard_map/ppermute | solution.py:441
  66.9 19.2 %collective-permute-start.6 = (bf16[96,128]{1,0:T(8,128)(2,1)}, bf16[96,128]{1,0:T(8,128)(2,1)S(1)}, u32[]{:S(2)}, u32[]{:S(2)}) collective-permute-start(bf16[96,128]{1,0:T(8,128)(2,1)} %get-tuple-element.60), channel_id=1, source_target_pairs={{0,24},{1,25},{2,26},{3,27},{4,28},{5,29},{6,30},{7,31},{8,0},{9,1... | collective-permute-start | bytes 73736 | tf_op jit(solution)/shard_map/ppermute | solution.py:441
  72.0 1.0 copy-start
  73.0 0.7 copy-start.11
  73.7 25.2 %copy-start.12 = (s32[32,128]{1,0:T(8,128)S(1)}, s32[32,128]{1,0:T(8,128)}, u32[]{:S(2)}) copy-start(s32[32,128]{1,0:T(8,128)} %digits.1.sorted_ref.refs_1_) | copy-start | bytes 49156
  86.1 0.6 copy-start.26
  86.1 0.6 copy-start.27
  86.1 0.6 copy-start.28
  89.7 32.7 %all-to-all-start.1 = ((bf16[16,96,128]{2,1,0:T(8,128)(2,1)}), bf16[16,96,128]{2,1,0:T(8,128)(2,1)}, u32[]{:S(2)}, u32[]{:S(2)}) async-start(bf16[16,96,128]{2,1,0:T(8,128)(2,1)} %broadcast_in_dim.4), calls=%async_computation.1 | async-start | bytes 786432 | tf_op jit(solution)/shard_map/all_to_all | solution.py:428
  99.0 1.0 copy-start.1
  120.9 0.8 copy-start.3
  121.7 0.7 copy-start.15
  124.3 29.6 %all-to-all-start.2 = ((bf16[16,96,128]{2,1,0:T(8,128)(2,1)}), bf16[16,96,128]{2,1,0:T(8,128)(2,1)}, u32[]{:S(2)}, u32[]{:S(2)}) async-start(bf16[16,96,128]{2,1,0:T(8,128)(2,1)} %broadcast_in_dim.5), calls=%async_computation.2 | async-start | bytes 786432 | tf_op jit(solution)/shard_map/all_to_all | solution.py:428
  128.5 1.0 copy-start.2
  129.5 1.0 copy-start.4
  130.6 0.9 copy-start.16
  152.4 0.8 copy-start.5
  153.2 0.7 copy-start.13
  162.9 11.1 %all-to-all-start.4 = ((bf16[4,2,176,128]{3,2,1,0:T(8,128)(2,1)}), bf16[4,2,176,128]{3,2,1,0:T(8,128)(2,1)S(1)}, u32[]{:S(2)}, u32[]{:S(2)}) async-start(bf16[4,2,176,128]{3,2,1,0:T(8,128)(2,1)} %bitcast.16), calls=%async_computation.4 | async-start | bytes 720896 | tf_op jit(solution)/shard_map/all_to_all | solution.py:428
  174.1 16.3 %collective-permute-start.7 = (bf16[176,128]{1,0:T(8,128)(2,1)S(1)}, bf16[176,128]{1,0:T(8,128)(2,1)S(1)}, u32[]{:S(2)}, u32[]{:S(2)}) collective-permute-start(bf16[176,128]{1,0:T(8,128)(2,1)S(1)} %fusion), channel_id=1, source_target_pairs={{0,64},{32,96},{64,0},{96,32},{128,192},{160,224},{192,128},{224,1... | collective-permute-start | bytes 135176 | tf_op jit(solution)/shard_map/ppermute | solution.py:500
  186.3 6.0 %collective-permute-start.8 = (bf16[4,384,128]{2,1,0:T(8,128)(2,1)}, bf16[4,384,128]{2,1,0:T(8,128)(2,1)S(1)}, u32[]{:S(2)}, u32[]{:S(2)}) collective-permute-start(bf16[4,384,128]{2,1,0:T(8,128)(2,1)} %bitcast.14.mine_ref), channel_id=1, source_target_pairs={{0,32},{32,0},{64,96},{96,64},{128,160},{160,128},{192,224},{224,1... | collective-permute-start | bytes 1179656 | tf_op jit(solution)/shard_map/ppermute | solution.py:445
  192.4 0.7 copy-start.20

commit v4 on v3

--- a/solution.py
+++ b/solution.py
@@ -15,6 +15,7 @@
 I3 = 128
 LANES = 128
 SUB = 8
+TALL = 16
 BF = jnp.bfloat16
 F32 = jnp.float32
 NT = (((1,), (1,)), ((), ()))
@@ -109,7 +110,25 @@
 
 
 def join_y_kernel(a, b, c, d, out):
-    out[...] = total_of((a, b, c, d)).astype(BF)
+    out[...] = jnp.broadcast_to(total_of((a, b, c, d)).astype(BF)[None], out.shape)
+
+
+def join_z_kernel(copies_ref, out):
+    total = copies_ref[0].astype(F32)
+    for n in range(1, copies_ref.shape[0]):
+        total += copies_ref[n].astype(F32)
+    out[...] = jnp.broadcast_to(total.astype(BF)[None], out.shape)
+
+
+def last_kernel(at_ref, parts_ref, other_ref, one_ref, two_ref, three_ref):
+    own = jnp.where(at_ref[3] == 0, parts_ref[0], parts_ref[1])
+    share = own + other_ref[...].astype(F32)
+    begin = 0
+    for out in (two_ref, one_ref, three_ref):
+        rows = out.shape[0]
+        for b in range(out.shape[1] // LANES):
+            out[:, b * LANES : (b + 1) * LANES] = share[begin : begin + rows]
+            begin += rows
 
 
 def assemble_kernel(at_ref, mine_ref, other_ref, out, wide):
@@ -166,14 +185,14 @@
 ):
     last = reps > 0
     if start:
-        old_one_ref, old_three_ref, unused = refs[:3]
+        old_one_ref, old_three_ref, old_two_ref = refs[:3]
         refs = refs[3:]
-    two_ref, *ends = refs[: 2 if last else 3]
-    wide, picked, gt, inner, back, acc_one, acc_three, right_wide, chained_wide = refs[2 if last else 3 :]
+    two_ref, *ends = refs[: 1 if last else 3]
+    wide, picked, gt, inner, back, acc_one, acc_three = refs[1 if last else 3 :]
     k = pl.program_id(0)
     groups = pl.num_programs(0)
     group = left_ref.shape[1]
-    steps = (R // SUB) * (group // LANES)
+    steps = (R // TALL) * (group // LANES)
     share = group // steps
 
     def fetch(slot, base, begin, number):
@@ -186,6 +205,9 @@
         acc_one[...] = old_one_ref[...] if start else jnp.zeros_like(acc_one)
         acc_three[...] = old_three_ref[...] if start else jnp.zeros_like(acc_three)
 
+        for r in range(start):
+            two_ref[place(r), : R * D2 * R // LANES] = old_two_ref[r]
+
         def one(step, carry):
             fetch(0, start * group, step * share, share)
             return carry
@@ -195,47 +217,45 @@
     slot = k % 2
     later = (start + jnp.minimum(k + 1, groups - 1)) * group
     gt[...] = picked[slot].T
-    right_wide[...] = right_ref[...].astype(F32)
-    chained_wide[...] = chained_ref[...].astype(F32)
 
     def chunk(step, carry):
         fetch(1 - slot, later, step * share, share)
-        half = step // (R // SUB)
-        lanes = pl.ds(pl.multiple_of(half * LANES, LANES), LANES)
-        low = (step % (R // SUB)) * SUB
-        rights = [right_wide[pl.ds(pl.multiple_of(c * R + low, SUB), SUB), lanes] for c in range(D3)]
+        lanes = pl.ds(pl.multiple_of(step // (R // TALL) * LANES, LANES), LANES)
+        low = step % (R // TALL) * TALL
+        rights = [right_ref[pl.ds(pl.multiple_of(c * R + low, TALL), TALL), lanes].astype(F32) for c in range(D3)]
         totals = [None] * D3
         for j in range(D1 * D2):
-            at = pl.ds(pl.multiple_of(j * R + low, SUB), SUB)
-            link = chained_wide[at, lanes]
+            at = pl.ds(pl.multiple_of(j * R + low, TALL), TALL)
+            link = chained_ref[at, lanes].astype(F32)
             total = None
             for c in range(D3):
-                g = jnp.broadcast_to(gt[pl.ds(j * D3 + c, 1), lanes], (SUB, LANES))
+                g = jnp.broadcast_to(gt[pl.ds(j * D3 + c, 1), lanes], (TALL, LANES))
                 term = g * rights[c]
                 total = term if total is None else total + term
                 term = g * link
                 totals[c] = term if totals[c] is None else totals[c] + term
-            inner[at, lanes] = total
+            inner[at, lanes] = total.astype(BF)
         for c in range(D3):
-            back[pl.ds(pl.multiple_of(c * R + low, SUB), SUB), lanes] = totals[c]
+            back[pl.ds(pl.multiple_of(c * R + low, TALL), TALL), lanes] = totals[c].astype(BF)
         return carry
 
     lax.fori_loop(0, steps, chunk, 0)
     first, third = digits_of(sorted_ref, group, start + k)
-    inner_all = inner[...].astype(BF)
+    inner_all = inner[...]
     two = None
     firsts = []
     for a in range(D1):
         part = inner_all[a * D2 * R : (a + 1) * D2 * R]
-        term = lax.dot_general(left_ref[a * R : (a + 1) * R], part, NT, preferred_element_type=F32)
+        term = lax.dot_general(part, left_ref[a * R : (a + 1) * R], NT, preferred_element_type=F32)
         two = term if two is None else two + term
         firsts.append(lax.dot_general(mid_ref[0], part, NN, preferred_element_type=F32).astype(BF))
-    two = (scale * two).astype(BF)
+    two = (scale * two.T).astype(BF)
+    into = place(start + k) if last else k
     for b in range(D2 * R // LANES):
-        two_ref[0, b * R : (b + 1) * R] = two[:, b * LANES : (b + 1) * LANES]
+        two_ref[into, b * R : (b + 1) * R] = two[:, b * LANES : (b + 1) * LANES]
     back_first = jnp.concatenate(firsts, axis=0)
-    acc_one[...] += lax.dot_general(onehot(first, I1), back_first, NT, preferred_element_type=F32)
-    acc_three[...] += lax.dot_general(onehot(third, I3), back[...].astype(BF), NT, preferred_element_type=F32)
+    acc_one[...] += lax.dot_general(back_first, onehot(first, I1), NT, preferred_element_type=F32)
+    acc_three[...] += lax.dot_general(back[...], onehot(third, I3), NT, preferred_element_type=F32)
 
     @pl.when(k == groups - 1)
     def _():
@@ -243,14 +263,14 @@
             ends[0][...] = acc_one[...]
             ends[1][...] = acc_three[...]
             return
-        rest_ref = ends[0]
+        sums = acc_one[...].T, acc_three[...].T
         for r in range(reps):
             blocks = []
-            for acc in (acc_one, acc_three):
+            for acc in sums:
                 rows = acc.shape[0] // reps
                 for b in range(acc.shape[1] // LANES):
                     blocks.append(acc[r * rows : (r + 1) * rows, b * LANES : (b + 1) * LANES])
-            rest_ref[place(r)] = (scale * jnp.concatenate(blocks, axis=0)).astype(BF)
+            two_ref[place(r), R * D2 * R // LANES :] = (scale * jnp.concatenate(blocks, axis=0)).astype(BF)
 
 
 SMEM = pl.BlockSpec(memory_space=pltpu.SMEM)
@@ -319,8 +339,24 @@
 
 def join_y(*parts):
     return pl.pallas_call(
-        join_y_kernel, out_shape=jax.ShapeDtypeStruct(parts[0].shape, BF), name="join_y"
+        join_y_kernel, out_shape=jax.ShapeDtypeStruct((16,) + parts[0].shape, BF), name="join_y"
     )(*parts)
+
+
+def join_z(copies):
+    return pl.pallas_call(
+        join_z_kernel, out_shape=jax.ShapeDtypeStruct(copies.shape, BF), name="join_z"
+    )(copies)
+
+
+def last_sum(where, parts, other, reps):
+    shapes = (I1 // reps, D1 * R), (R, D2 * R), (I3 // reps, D3 * R)
+    return pl.pallas_call(
+        last_kernel,
+        in_specs=[SMEM, VMEM, VMEM],
+        out_shape=[jax.ShapeDtypeStruct(shape, F32) for shape in shapes],
+        name="last_sum",
+    )(where, parts, other)
 
 
 def assemble(where, shape, *parts):
@@ -371,10 +407,13 @@
     group = total // I2
     left, right, chained = links
     last = end == I2
-    sums = (I1, D1 * R), (I3, D3 * R)
-    two_shape = I2, R * D2 * R // LANES, LANES
-    extra_in = [whole(sums[0]), whole(sums[1]), pl.BlockSpec(memory_space=pl.ANY)] if begin else []
-    ends = [((reps, rest, LANES), BF)] if last else [(one, F32) for one in sums]
+    sums = (D1 * R, I1), (D3 * R, I3)
+    size_two = R * D2 * R // LANES
+    extra_in = [whole(sums[0]), whole(sums[1]), whole((begin, size_two, LANES))] if begin else []
+    if last:
+        outs = [((reps, size_two + rest, LANES), BF)]
+    else:
+        outs = [((end - begin, size_two, LANES), BF)] + [(one, F32) for one in sums]
     return pl.pallas_call(
         lambda *refs: after_kernel(scale, begin, reps if last else 0, *refs),
         grid_spec=pltpu.PrefetchScalarGridSpec(
@@ -389,24 +428,18 @@
                 pl.BlockSpec((1, R, D2 * R), lambda k, o: (begin + k, 0, 0)),
             ]
             + extra_in,
-            out_specs=[
-                pl.BlockSpec((1,) + two_shape[1:], lambda k, o: (place(begin + k), 0, 0)),
-            ]
-            + [whole(shape) for shape, kind in ends],
+            out_specs=[whole(shape) for shape, kind in outs],
             scratch_shapes=[
                 pltpu.VMEM((total, width), F32),
                 pltpu.VMEM((2, group, width), F32),
                 pltpu.VMEM((width, group), F32),
-                pltpu.VMEM((D1 * D2 * R, group), F32),
-                pltpu.VMEM((D3 * R, group), F32),
-                pltpu.VMEM((I1, D1 * R), F32),
-                pltpu.VMEM((I3, D3 * R), F32),
-                pltpu.VMEM((D3 * R, group), F32),
-                pltpu.VMEM((D1 * D2 * R, group), F32),
+                pltpu.VMEM((D1 * D2 * R, group), BF),
+                pltpu.VMEM((D3 * R, group), BF),
+                pltpu.VMEM((D1 * R, I1), F32),
+                pltpu.VMEM((D3 * R, I3), F32),
             ],
         ),
-        out_shape=[jax.ShapeDtypeStruct(two_shape, BF)] + [jax.ShapeDtypeStruct(*one) for one in ends],
-        input_output_aliases={9: 0} if begin else {},
+        out_shape=[jax.ShapeDtypeStruct(*one) for one in outs],
         compiler_params=pltpu.CompilerParams(vmem_limit_bytes=48 << 20),
         name="after",
     )(order, sorted_digits, received, left, right, chained, core_two, *old)
@@ -468,7 +501,7 @@
     grad_rows, grad_bottom, feat = dense(bottom_out, pooled, top_grad, top_weight)
     received = lax.all_to_all(grad_rows, "tab", split_axis=0, concat_axis=0, tiled=True)
     rep, tab = lax.axis_index("rep"), lax.axis_index("tab")
-    where = jnp.stack([rep >> 2, rep & 1, tab >> 3]).astype(jnp.int32)
+    where = jnp.stack([rep >> 2, rep & 1, tab >> 3, rep >> 1 & 1]).astype(jnp.int32)
     rows = top_weight.shape[0]
     padded = -(-rows // 2 // 64) * 64
     quarter = padded // 4
@@ -488,32 +521,19 @@
         return after(begin, end, received, order, sorted_digits, links, core_mid[0], scale, reps, old)
 
     two, one, three = piece(0, CUT, ())
-    copies = gather_up(partial, 16, "z_hi", "z_lo")
-    summed = jnp.sum(copies.astype(F32), axis=0).astype(BF)
+    summed = join_z(swap(partial, "z_hi", "z_lo"))
     one, summed = lax.optimization_barrier((one, summed))
-    two, rest = piece(CUT, I2, (one, three, two))
-    mine = gather_up(summed, 16, "x", "y").reshape(4, padded, LANES)
-    rest, mine = lax.optimization_barrier((rest, mine))
-    parts = jnp.concatenate([two, rest], axis=1)
+    (parts,) = piece(CUT, I2, (one, three, two))
+    mine = swap(summed, "x", "y").reshape(4, padded, LANES)
+    parts, mine = lax.optimization_barrier((parts, mine))
     parts = add_up(parts.reshape(2, 8, -1, LANES), "core").astype(BF)
     parts = add_up(parts.reshape(4, 2, -1, LANES), "x")
-    other_z = lax.ppermute(
-        lax.dynamic_index_in_dim(parts, 1 - (rep >> 1 & 1), 0, False).astype(BF),
-        "rep",
-        [(i, i ^ 2) for i in range(16)],
-    )
-    share = lax.dynamic_index_in_dim(parts, rep >> 1 & 1, 0, False) + other_z.astype(F32)
     grad_top = assemble(where, (rows, top_grad.shape[1]), mine, swap_core(mine))
-    size_two = R * D2 * R // LANES
-    size_one = I1 // reps * D1 * R // LANES
-    widths = D2 * R // LANES, D1 * R // LANES, D3 * R // LANES
-
-    def lay(block, blocks):
-        return block.reshape(blocks, -1, LANES).swapaxes(0, 1).reshape(1, -1, blocks * LANES)
-
-    grad_two = lay(share[:size_two], widths[0])[:, None]
-    grad_one = lay(share[size_two : size_two + size_one], widths[1])
-    grad_three = lay(share[size_two + size_one :], widths[2])
+    parts, grad_top = lax.optimization_barrier((parts, grad_top))
+    sent = jnp.where(where[3] == 0, parts[1], parts[0]).astype(BF)
+    other = lax.ppermute(sent, "rep", [(i, i ^ 2) for i in range(16)])
+    grad_one, grad_two, grad_three = last_sum(where, parts, other, reps)
+    grad_one, grad_two, grad_three = grad_one[None], grad_two[None, None], grad_three[None]
     return (grad_one, grad_two, grad_three, grad_top, grad_bottom)
 
 

time: 197 us -> 191 us (0.970); the launches traced: 195 us -> 187 us
  local copies, waits for them, and re-layouts: 20.7 us -> 17.9 us
  other arithmetic: 3.33 us -> 1.07 us
    pallas_call x2, Pallas kernels: 41.9 us -> 37 us  [after(): pl.pallas_call(lambda *refs: after_kernel(scale, begin, reps if last else...]
    pallas_call x1 -> x3, Pallas kernels: 1.42 us -> 4.94 us  [the longest x1 1.8 us: join_z(): pl.pallas_call(join_z_kernel, out_shape=jax.ShapeDtypeStruct(copies.shape...]
    all_to_all x3, waiting for transfers between devices: 6.87 us -> 4.3 us  [swap(): lax.all_to_all(array, ('rep', 'tab'), 0, 0, axis_index_groups=groups_of(*...]
    broadcast_in_dim x2 -> x0, local copies, waits for them, and re-layouts: 2.36 us -> none  [gather_up(): return swap(jnp.broadcast_to(array[None], (size,) + array.shape), *names)]
    unnamed x60 -> x64, local copies, waits for them, and re-layouts: 16.4 us -> 17.9 us
  transfers between devices with their start and end apart: 13 -> 13, of which waited for: 3 -> 4; matrix products, arithmetic and copies ran while one was open for 1% -> 0% of each run, Pallas kernels for 34% -> 33%
where the time goes in v4:
time: 191 us; the launch traced here: 187 us
  Pallas kernels  76.5 us (40%)
  starting transfers between devices  72.8 us (38%)
  local copies, waits for them, and re-layouts  17.9 us (9%)
  waiting for transfers between devices  9.87 us (5%)
  blocking collectives  7.93 us (4%)
    pallas_call x2, Pallas kernels, after(): pl.pallas_call(lambda *refs: after_kernel(scale, begin, reps if last else...  37 us
    ppermute x6, starting transfers between devices, shift(): lax.ppermute(array, axis, [(i, (i + by * step) % number) for i in range(n...  21.3 us
    unnamed x64, local copies, waits for them, and re-layouts  17.9 us
    all_to_all x3, starting transfers between devices, swap(): lax.all_to_all(array, ('rep', 'tab'), 0, 0, axis_index_groups=groups_of(*...  17.7 us
    all_to_all x1, starting transfers between devices, on_device(): lax.all_to_all(grad_rows, 'tab', split_axis=0, concat_axis=0, tiled=True)  16.1 us
    pallas_call x1, Pallas kernels, before(): pl.pallas_call(before_kernel, grid=(I2,), in_specs=[whole(table), whole((...  12.3 us
    ppermute x1, starting transfers between devices, on_device(): other = lax.ppermute(sent, 'rep', [(i, i ^ 2) for i in range(16)])  12.2 us
    pallas_call x1, Pallas kernels, dense(): pl.pallas_call(lambda *refs: dense_kernel(count, *refs), out_shape=(jax.S...  8.81 us
  transfers between devices with their start and end apart: 13, of which 4 were waited for; matrix products, arithmetic and copies ran while one was open for 0% of the time, Pallas kernels for 33%

profile of v4, /device:TPU:1, one launch (start us, length us, event | category | flops | bytes accessed | tf_op | source)
XLA Modules:
  0.0 187.0 jit_solution(16105828208114734681)
XLA Ops:
  0.6 1.2 copy-done.4
  1.9 1.1 copy-done.5
  3.0 0.9 copy-done.6
  3.9 0.8 copy-done.17
  4.6 8.8 %dense.1 = (bf16[32,128,128]{2,1,0:T(8,128)(2,1)}, bf16[128,128]{1,0:T(8,128)(2,1)}, bf16[33,128,128]{2,1,0:T(8,128)(2,1)S(1)}) custom-call(bf16[128,128]{1,0:T(8,128)(2,1)S(1)} %copy-done.17, bf16[4096,128]{1,0:T(8,128)(2,1)S(1)} %bitcast.31, bf16[128,512]{1,0:T(8,128)(2,1)S(1)} %copy-done.6, bf16[656,512]{1,0:T(8,128)(2,1)S(1)} %copy-done.5), custom_call_target="tpu_custom_call" | custom-call | tf_op jit(solution)/shard_map/dense/pallas_call | solution.py:288
  13.4 16.1 %all-to-all-start = ((bf16[32,128,128]{2,1,0:T(8,128)(2,1)}), bf16[32,128,128]{2,1,0:T(8,128)(2,1)S(1)}, u32[]{:S(2)}, u32[]{:S(2)}) async-start(bf16[32,128,128]{2,1,0:T(8,128)(2,1)} %get-tuple-element.52), calls=%async_computation | async-start | bytes 2097152 | tf_op jit(solution)/shard_map/all_to_all | solution.py:502
  29.6 0.9 copy-done.7
  30.5 5.9 %gram.1 = (bf16[4,384,128]{2,1,0:T(8,128)(2,1)S(1)}, bf16[4,384,128]{2,1,0:T(8,128)(2,1)S(1)}) custom-call(s32[4]{0:T(128)S(1)} %pad_add_fusion.refs_0_.at_ref, bf16[33,128,128]{2,1,0:T(8,128)(2,1)S(1)} %get-tuple-element.44.refs_1_, bf16[128,512]{1,0:T(8,128)(2,1)S(1)} %copy-done.7), custom_call_target="tpu_custom_call" | custom-call | tf_op jit(solution)/shard_map/gram/pallas_call | solution.py:309
  36.4 0.7 copy-done.8
  37.2 2.9 %collective-permute-start = (bf16[4,384,128]{2,1,0:T(8,128)(2,1)S(1)}, bf16[4,384,128]{2,1,0:T(8,128)(2,1)S(1)}, u32[]{:S(2)}, u32[]{:S(2)}) collective-permute-start(bf16[4,384,128]{2,1,0:T(8,128)(2,1)S(1)} %get-tuple-element.46), channel_id=1, source_target_pairs={{0,32},{32,0},{64,96},{96,64},{128,160},{160,128},{192,224},{224,1... | collective-permute-start | bytes 1179656 | tf_op jit(solution)/shard_map/ppermute | solution.py:478
  40.0 1.3 collective-permute-done.came_ref
  41.3 0.7 copy-done.20
  42.1 1.9 %join_core.1 = (bf16[384,128]{1,0:T(8,128)(2,1)}, bf16[384,128]{1,0:T(8,128)(2,1)}, bf16[384,128]{1,0:T(8,128)(2,1)}, bf16[384,128]{1,0:T(8,128)(2,1)}) custom-call(bf16[4,384,128]{2,1,0:T(8,128)(2,1)} %copy-done.8, bf16[4,384,128]{2,1,0:T(8,128)(2,1)} %copy-done.20), custom_call_target="tpu_custom_call" | custom-call | tf_op jit(solution)/shard_map/join_core/pallas_call | solution.py:324
  44.0 3.1 %collective-permute-start.1 = (bf16[384,128]{1,0:T(8,128)(2,1)}, bf16[384,128]{1,0:T(8,128)(2,1)S(1)}, u32[]{:S(2)}, u32[]{:S(2)}) collective-permute-start(bf16[384,128]{1,0:T(8,128)(2,1)} %get-tuple-element.57), channel_id=1, source_target_pairs={{0,128},{32,160},{64,192},{96,224},{128,256},{160,288},{192,320},{... | collective-permute-start | bytes 294920 | tf_op jit(solution)/shard_map/ppermute | solution.py:474
  47.1 4.4 %collective-permute-start.2 = (bf16[384,128]{1,0:T(8,128)(2,1)}, bf16[384,128]{1,0:T(8,128)(2,1)S(1)}, u32[]{:S(2)}, u32[]{:S(2)}) collective-permute-start(bf16[384,128]{1,0:T(8,128)(2,1)} %get-tuple-element.58), channel_id=1, source_target_pairs={{0,256},{32,288},{64,320},{96,352},{128,384},{160,416},{192,448},{... | collective-permute-start | bytes 294920 | tf_op jit(solution)/shard_map/ppermute | solution.py:474
  51.5 3.1 %collective-permute-start.3 = (bf16[384,128]{1,0:T(8,128)(2,1)}, bf16[384,128]{1,0:T(8,128)(2,1)S(1)}, u32[]{:S(2)}, u32[]{:S(2)}) collective-permute-start(bf16[384,128]{1,0:T(8,128)(2,1)} %get-tuple-element.59), channel_id=1, source_target_pairs={{0,384},{32,416},{64,448},{96,480},{128,0},{160,32},{192,64},{224,... | collective-permute-start | bytes 294920 | tf_op jit(solution)/shard_map/ppermute | solution.py:474
  54.6 2.8 %collective-permute-done.3.d = bf16[384,128]{1,0:T(8,128)(2,1)S(1)} collective-permute-done((bf16[384,128]{1,0:T(8,128)(2,1)}, bf16[384,128]{1,0:T(8,128)(2,1)S(1)}, u32[]{:S(2)}, u32[]{:S(2)}) %collective-permute-start.3) | collective-permute-done | bytes 98336 | tf_op jit(solution)/shard_map/ppermute | solution.py:474
  58.0 1.7 join_x.1
  59.7 3.4 %collective-permute-start.4 = (bf16[96,128]{1,0:T(8,128)(2,1)}, bf16[96,128]{1,0:T(8,128)(2,1)S(1)}, u32[]{:S(2)}, u32[]{:S(2)}) collective-permute-start(bf16[96,128]{1,0:T(8,128)(2,1)} %get-tuple-element.61), channel_id=1, source_target_pairs={{0,8},{1,9},{2,10},{3,11},{4,12},{5,13},{6,14},{7,15},{8,16},{9,17... | collective-permute-start | bytes 73736 | tf_op jit(solution)/shard_map/ppermute | solution.py:474
  63.1 4.3 %collective-permute-start.5 = (bf16[96,128]{1,0:T(8,128)(2,1)}, bf16[96,128]{1,0:T(8,128)(2,1)S(1)}, u32[]{:S(2)}, u32[]{:S(2)}) collective-permute-start(bf16[96,128]{1,0:T(8,128)(2,1)} %get-tuple-element.62), channel_id=1, source_target_pairs={{0,16},{1,17},{2,18},{3,19},{4,20},{5,21},{6,22},{7,23},{8,24},{9,... | collective-permute-start | bytes 73736 | tf_op jit(solution)/shard_map/ppermute | solution.py:474
  67.5 3.1 %collective-permute-start.6 = (bf16[96,128]{1,0:T(8,128)(2,1)}, bf16[96,128]{1,0:T(8,128)(2,1)S(1)}, u32[]{:S(2)}, u32[]{:S(2)}) collective-permute-start(bf16[96,128]{1,0:T(8,128)(2,1)} %get-tuple-element.63), channel_id=1, source_target_pairs={{0,24},{1,25},{2,26},{3,27},{4,28},{5,29},{6,30},{7,31},{8,0},{9,1... | collective-permute-start | bytes 73736 | tf_op jit(solution)/shard_map/ppermute | solution.py:474
  70.8 1.8 digits.1.sorted_ref.refs_1_
  72.6 1.0 copy-done
  73.6 0.7 copy-done.11
  74.4 12.3 %before.1 = (bf16[256,4096]{1,0:T(8,128)(2,1)S(1)}, bf16[512,4096]{1,0:T(8,128)(2,1)}, bf16[1024,4096]{1,0:T(8,128)(2,1)}) custom-call(s32[32,128]{1,0:T(8,128)S(1)} %copy-done.11, bf16[256,128]{1,0:T(8,128)(2,1)S(1)} %bitcast.33, bf16[16,64,256]{2,1,0:T(8,128)(2,1)S(1)} %bitcast.27, bf16[512,128]{1,0:T(8,128)(2,1)S(1)} %bitcast.32), custom_call_target="tpu_custom_call" | custom-call | tf_op jit(solution)/shard_map/before/pallas_call | solution.py:379
  87.3 1.6 join_y.1
  88.9 9.2 %all-to-all-start.1 = ((bf16[16,96,128]{2,1,0:T(8,128)(2,1)}), bf16[16,96,128]{2,1,0:T(8,128)(2,1)}, u32[]{:S(2)}, u32[]{:S(2)}) async-start(bf16[16,96,128]{2,1,0:T(8,128)(2,1)} %join_y.1), calls=%async_computation.1 | async-start | bytes 786432 | tf_op jit(solution)/shard_map/all_to_all | solution.py:461
  98.2 1.0 copy-done.1
  99.2 0.7 copy-done.12
  99.9 18.4 %after.2 = (bf16[8,128,128]{2,1,0:T(8,128)(2,1)S(1)}, f32[256,128]{1,0:T(8,128)S(1)}, f32[512,128]{1,0:T(8,128)S(1)}) custom-call(s32[4096]{0:T(1024)S(1)} %bitcast.35, s32[32,128]{1,0:T(8,128)S(1)} %copy-done.12, bf16[4096,128]{1,0:T(8,128)(2,1)S(1)} %bitcast.25, bf16[256,4096]{1,0:T(8,128)(2,1)S(1)} %get-tuple-element.66.refs_3_, ...), custom_call_target="tpu_custom_call" | custom-call | tf_op jit(solution)/shard_map/after/pallas_call | solution.py:417
  118.4 0.7 copy-done.9
  119.7 1.8 join_z.1
  121.5 4.2 %all-to-all-start.2 = ((bf16[16,96,128]{2,1,0:T(8,128)(2,1)}), bf16[16,96,128]{2,1,0:T(8,128)(2,1)}, u32[]{:S(2)}, u32[]{:S(2)}) async-start(bf16[16,96,128]{2,1,0:T(8,128)(2,1)} %join_z.1), calls=%async_computation.2 | async-start | bytes 786432 | tf_op jit(solution)/shard_map/all_to_all | solution.py:461
  125.8 1.0 copy-done.2
  126.8 0.9 copy-done.10
  127.7 0.9 copy-done.16
  128.7 18.6 %after.3 = bf16[16,176,128]{2,1,0:T(8,128)(2,1)S(1)} custom-call(s32[4096]{0:T(1024)S(1)} %bitcast.36, s32[32,128]{1,0:T(8,128)S(1)} %copy-done.13, bf16[4096,128]{1,0:T(8,128)(2,1)S(1)} %bitcast.26, bf16[256,4096]{1,0:T(8,128)(2,1)S(1)} %get-tuple-element.66.refs_3_, bf16[512,4096]{1,0:T(8,128)(2,1)} %get-tuple-element.67.refs_4_, ...), custom_call_target="tpu_custom_call" | custom-call | tf_op jit(solution)/shard_map/after/pallas_call | solution.py:417
  147.2 0.9 copy-done.3
  148.1 7.9 %all_to_all.25 = bf16[2,8,176,128]{3,2,1,0:T(8,128)(2,1)S(1)} all-to-all(bf16[2,8,176,128]{3,2,1,0:T(8,128)(2,1)} %bitcast.30), channel_id=1, replica_groups={{0,32},{1,33},{2,34},{3,35},{4,36},{5,37},{6,38},{7,39},{8,40},{9,41},{..., dimensions={0} | all-to-all | bytes 1441792 | tf_op jit(solution)/shard_map/all_to_all | solution.py:461
  156.0 0.9 reduce_sum.21
  157.0 4.3 %all-to-all-start.4 = ((bf16[4,2,176,128]{3,2,1,0:T(8,128)(2,1)}), bf16[4,2,176,128]{3,2,1,0:T(8,128)(2,1)S(1)}, u32[]{:S(2)}, u32[]{:S(2)}) async-start(bf16[4,2,176,128]{3,2,1,0:T(8,128)(2,1)} %bitcast.17), calls=%async_computation.4 | async-start | bytes 720896 | tf_op jit(solution)/shard_map/all_to_all | solution.py:461
  161.3 2.5 %collective-permute-start.7 = (bf16[4,384,128]{2,1,0:T(8,128)(2,1)}, bf16[4,384,128]{2,1,0:T(8,128)(2,1)S(1)}, u32[]{:S(2)}, u32[]{:S(2)}) collective-permute-start(bf16[4,384,128]{2,1,0:T(8,128)(2,1)} %bitcast.15.mine_ref), channel_id=1, source_target_pairs={{0,32},{32,0},{64,96},{96,64},{128,160},{160,128},{192,224},{224,1... | collective-permute-start | bytes 1179656 | tf_op jit(solution)/shard_map/ppermute | solution.py:478
  163.8 4.3 %all-to-all-done.4 = bf16[4,2,176,128]{3,2,1,0:T(8,128)(2,1)S(1)} async-done(((bf16[4,2,176,128]{3,2,1,0:T(8,128)(2,1)}), bf16[4,2,176,128]{3,2,1,0:T(8,128)(2,1)S(1)}, u32[]{:S(2)}, u32[]{:S(2)}) %all-to-all-start.4) | async-done | bytes 360480 | tf_op jit(solution)/shard_map/all_to_all | solution.py:461
  168.2 0.8 copy-done.21
  169.0 2.1 %assemble.1 = bf16[656,512]{1,0:T(8,128)(2,1)} custom-call(s32[4]{0:T(128)} %copy-done.18, bf16[4,384,128]{2,1,0:T(8,128)(2,1)} %bitcast.15.mine_ref, bf16[4,384,128]{2,1,0:T(8,128)(2,1)} %copy-done.21), custom_call_target="tpu_custom_call" | custom-call | tf_op jit(solution)/shard_map/assemble/pallas_call | solution.py:363
  171.1 12.2 %collective-permute-start.8 = (bf16[176,128]{1,0:T(8,128)(2,1)S(1)}, bf16[176,128]{1,0:T(8,128)(2,1)S(1)}, u32[]{:S(2)}, u32[]{:S(2)}) collective-permute-start(bf16[176,128]{1,0:T(8,128)(2,1)S(1)} %fusion), channel_id=1, source_target_pairs={{0,64},{32,96},{64,0},{96,32},{128,192},{160,224},{192,128},{224,1... | collective-permute-start | bytes 135176 | tf_op jit(solution)/shard_map/ppermute | solution.py:534
  183.4 1.5 collective-permute-done.8.other_ref
  185.5 1.6 last_sum.1
  (59 shorter events, 2.9 us)
Async XLA Ops:
  0.6 1.2 copy-start.4
  1.9 1.1 copy-start.5
  3.0 0.9 copy-start.6
  3.9 0.8 copy-start.17
  4.6 65.9 %copy-start.26 = (bf16[1,128,256]{2,1,0:T(8,128)(2,1)S(1)}, bf16[1,128,256]{2,1,0:T(8,128)(2,1)}, u32[]{:S(2)}) copy-start(bf16[1,128,256]{2,1,0:T(8,128)(2,1)} %param.14) | copy-start | bytes 196612
  4.6 66.1 %copy-start.22 = (bf16[1,128,512]{2,1,0:T(8,128)(2,1)S(1)}, bf16[1,128,512]{2,1,0:T(8,128)(2,1)}, u32[]{:S(2)}) copy-start(bf16[1,128,512]{2,1,0:T(8,128)(2,1)} %param.16) | copy-start | bytes 393220
  4.6 93.5 %copy-start.14 = (s32[1,1,4096]{2,1,0:T(1,128)S(1)}, s32[1,1,4096]{2,1,0:T(1,128)}, u32[]{:S(2)}) copy-start(s32[1,1,4096]{2,1,0:T(1,128)} %param.19) | copy-start | bytes 49156
  13.4 75.5 %all-to-all-start = ((bf16[32,128,128]{2,1,0:T(8,128)(2,1)}), bf16[32,128,128]{2,1,0:T(8,128)(2,1)S(1)}, u32[]{:S(2)}, u32[]{:S(2)}) async-start(bf16[32,128,128]{2,1,0:T(8,128)(2,1)} %get-tuple-element.52), calls=%async_computation | async-start | bytes 2097152 | tf_op jit(solution)/shard_map/all_to_all | solution.py:502
  29.6 27.7 %copy-start.18 = (s32[4]{0:T(128)}, s32[4]{0:T(128)S(1)}, u32[]{:S(2)}) copy-start(s32[4]{0:T(128)S(1)} %pad_add_fusion.refs_0_.at_ref) | copy-start | bytes 52
  29.6 0.9 copy-start.7
  36.4 0.7 copy-start.8
  37.2 4.2 %collective-permute-start = (bf16[4,384,128]{2,1,0:T(8,128)(2,1)S(1)}, bf16[4,384,128]{2,1,0:T(8,128)(2,1)S(1)}, u32[]{:S(2)}, u32[]{:S(2)}) collective-permute-start(bf16[4,384,128]{2,1,0:T(8,128)(2,1)S(1)} %get-tuple-element.46), channel_id=1, source_target_pairs={{0,32},{32,0},{64,96},{96,64},{128,160},{160,128},{192,224},{224,1... | collective-permute-start | bytes 1179656 | tf_op jit(solution)/shard_map/ppermute | solution.py:478
  41.3 0.7 copy-start.20
  44.0 10.5 %collective-permute-start.1 = (bf16[384,128]{1,0:T(8,128)(2,1)}, bf16[384,128]{1,0:T(8,128)(2,1)S(1)}, u32[]{:S(2)}, u32[]{:S(2)}) collective-permute-start(bf16[384,128]{1,0:T(8,128)(2,1)} %get-tuple-element.57), channel_id=1, source_target_pairs={{0,128},{32,160},{64,192},{96,224},{128,256},{160,288},{192,320},{... | collective-permute-start | bytes 294920 | tf_op jit(solution)/shard_map/ppermute | solution.py:474
  47.1 7.5 %collective-permute-start.2 = (bf16[384,128]{1,0:T(8,128)(2,1)}, bf16[384,128]{1,0:T(8,128)(2,1)S(1)}, u32[]{:S(2)}, u32[]{:S(2)}) collective-permute-start(bf16[384,128]{1,0:T(8,128)(2,1)} %get-tuple-element.58), channel_id=1, source_target_pairs={{0,256},{32,288},{64,320},{96,352},{128,384},{160,416},{192,448},{... | collective-permute-start | bytes 294920 | tf_op jit(solution)/shard_map/ppermute | solution.py:474
  51.5 5.9 %collective-permute-start.3 = (bf16[384,128]{1,0:T(8,128)(2,1)}, bf16[384,128]{1,0:T(8,128)(2,1)S(1)}, u32[]{:S(2)}, u32[]{:S(2)}) collective-permute-start(bf16[384,128]{1,0:T(8,128)(2,1)} %get-tuple-element.59), channel_id=1, source_target_pairs={{0,384},{32,416},{64,448},{96,480},{128,0},{160,32},{192,64},{224,... | collective-permute-start | bytes 294920 | tf_op jit(solution)/shard_map/ppermute | solution.py:474
  54.5 2.8 %copy-start.23 = (bf16[384,128]{1,0:T(8,128)(2,1)}, bf16[384,128]{1,0:T(8,128)(2,1)S(1)}, u32[]{:S(2)}) copy-start(bf16[384,128]{1,0:T(8,128)(2,1)S(1)} %collective-permute-done.1.b) | copy-start | bytes 294916
  54.6 2.8 %copy-start.24 = (bf16[384,128]{1,0:T(8,128)(2,1)}, bf16[384,128]{1,0:T(8,128)(2,1)S(1)}, u32[]{:S(2)}) copy-start(bf16[384,128]{1,0:T(8,128)(2,1)S(1)} %collective-permute-done.2.c) | copy-start | bytes 294916
  57.3 0.6 copy-start.25
  59.7 27.0 %collective-permute-start.4 = (bf16[96,128]{1,0:T(8,128)(2,1)}, bf16[96,128]{1,0:T(8,128)(2,1)S(1)}, u32[]{:S(2)}, u32[]{:S(2)}) collective-permute-start(bf16[96,128]{1,0:T(8,128)(2,1)} %get-tuple-element.61), channel_id=1, source_target_pairs={{0,8},{1,9},{2,10},{3,11},{4,12},{5,13},{6,14},{7,15},{8,16},{9,17... | collective-permute-start | bytes 73736 | tf_op jit(solution)/shard_map/ppermute | solution.py:474
  63.1 23.6 %collective-permute-start.5 = (bf16[96,128]{1,0:T(8,128)(2,1)}, bf16[96,128]{1,0:T(8,128)(2,1)S(1)}, u32[]{:S(2)}, u32[]{:S(2)}) collective-permute-start(bf16[96,128]{1,0:T(8,128)(2,1)} %get-tuple-element.62), channel_id=1, source_target_pairs={{0,16},{1,17},{2,18},{3,19},{4,20},{5,21},{6,22},{7,23},{8,24},{9,... | collective-permute-start | bytes 73736 | tf_op jit(solution)/shard_map/ppermute | solution.py:474
  67.5 19.2 %collective-permute-start.6 = (bf16[96,128]{1,0:T(8,128)(2,1)}, bf16[96,128]{1,0:T(8,128)(2,1)S(1)}, u32[]{:S(2)}, u32[]{:S(2)}) collective-permute-start(bf16[96,128]{1,0:T(8,128)(2,1)} %get-tuple-element.63), channel_id=1, source_target_pairs={{0,24},{1,25},{2,26},{3,27},{4,28},{5,29},{6,30},{7,31},{8,0},{9,1... | collective-permute-start | bytes 73736 | tf_op jit(solution)/shard_map/ppermute | solution.py:474
  72.6 1.0 copy-start
  73.6 0.7 copy-start.11
  86.7 0.6 copy-start.28
  86.7 0.6 copy-start.29
  86.7 0.6 copy-start.30
  88.9 30.8 %all-to-all-start.1 = ((bf16[16,96,128]{2,1,0:T(8,128)(2,1)}), bf16[16,96,128]{2,1,0:T(8,128)(2,1)}, u32[]{:S(2)}, u32[]{:S(2)}) async-start(bf16[16,96,128]{2,1,0:T(8,128)(2,1)} %join_y.1), calls=%async_computation.1 | async-start | bytes 786432 | tf_op jit(solution)/shard_map/all_to_all | solution.py:461
  98.2 1.0 copy-start.1
  99.2 0.7 copy-start.12
  99.9 25.8 %copy-start.13 = (s32[32,128]{1,0:T(8,128)S(1)}, s32[32,128]{1,0:T(8,128)}, u32[]{:S(2)}) copy-start(s32[32,128]{1,0:T(8,128)} %digits.1.sorted_ref.refs_1_) | copy-start | bytes 49156
  118.4 0.7 copy-start.9
  119.1 0.6 copy-start.15
  121.5 26.6 %all-to-all-start.2 = ((bf16[16,96,128]{2,1,0:T(8,128)(2,1)}), bf16[16,96,128]{2,1,0:T(8,128)(2,1)}, u32[]{:S(2)}, u32[]{:S(2)}) async-start(bf16[16,96,128]{2,1,0:T(8,128)(2,1)} %join_z.1), calls=%async_computation.2 | async-start | bytes 786432 | tf_op jit(solution)/shard_map/all_to_all | solution.py:461
  125.8 1.0 copy-start.2
  126.8 0.9 copy-start.10
  127.7 0.9 copy-start.16
  147.2 0.9 copy-start.3
  157.0 11.1 %all-to-all-start.4 = ((bf16[4,2,176,128]{3,2,1,0:T(8,128)(2,1)}), bf16[4,2,176,128]{3,2,1,0:T(8,128)(2,1)S(1)}, u32[]{:S(2)}, u32[]{:S(2)}) async-start(bf16[4,2,176,128]{3,2,1,0:T(8,128)(2,1)} %bitcast.17), calls=%async_computation.4 | async-start | bytes 720896 | tf_op jit(solution)/shard_map/all_to_all | solution.py:461
  161.3 6.9 %collective-permute-start.7 = (bf16[4,384,128]{2,1,0:T(8,128)(2,1)}, bf16[4,384,128]{2,1,0:T(8,128)(2,1)S(1)}, u32[]{:S(2)}, u32[]{:S(2)}) collective-permute-start(bf16[4,384,128]{2,1,0:T(8,128)(2,1)} %bitcast.15.mine_ref), channel_id=1, source_target_pairs={{0,32},{32,0},{64,96},{96,64},{128,160},{160,128},{192,224},{224,1... | collective-permute-start | bytes 1179656 | tf_op jit(solution)/shard_map/ppermute | solution.py:478
  168.2 16.7 %copy-start.19 = (f32[2,176,128]{2,1,0:T(8,128)}, f32[2,176,128]{2,1,0:T(8,128)S(1)}, u32[]{:S(2)}) copy-start(f32[2,176,128]{2,1,0:T(8,128)S(1)} %convert_reduce_fusion.parts_ref) | copy-start | bytes 540676
  168.2 0.8 copy-start.21
  171.1 13.7 %collective-permute-start.8 = (bf16[176,128]{1,0:T(8,128)(2,1)S(1)}, bf16[176,128]{1,0:T(8,128)(2,1)S(1)}, u32[]{:S(2)}, u32[]{:S(2)}) collective-permute-start(bf16[176,128]{1,0:T(8,128)(2,1)S(1)} %fusion), channel_id=1, source_target_pairs={{0,64},{32,96},{64,0},{96,32},{128,192},{160,224},{192,128},{224,1... | collective-permute-start | bytes 135176 | tf_op jit(solution)/shard_map/ppermute | solution.py:534
  184.8 0.6 copy-start.27

commit v5 on v4

--- a/solution.py
+++ b/solution.py
@@ -528,10 +528,11 @@
     parts, mine = lax.optimization_barrier((parts, mine))
     parts = add_up(parts.reshape(2, 8, -1, LANES), "core").astype(BF)
     parts = add_up(parts.reshape(4, 2, -1, LANES), "x")
-    grad_top = assemble(where, (rows, top_grad.shape[1]), mine, swap_core(mine))
-    parts, grad_top = lax.optimization_barrier((parts, grad_top))
+    other_mine = swap_core(mine)
+    parts, other_mine = lax.optimization_barrier((parts, other_mine))
     sent = jnp.where(where[3] == 0, parts[1], parts[0]).astype(BF)
     other = lax.ppermute(sent, "rep", [(i, i ^ 2) for i in range(16)])
+    grad_top = assemble(where, (rows, top_grad.shape[1]), mine, other_mine)
     grad_one, grad_two, grad_three = last_sum(where, parts, other, reps)
     grad_one, grad_two, grad_three = grad_one[None], grad_two[None, None], grad_three[None]
     return (grad_one, grad_two, grad_three, grad_top, grad_bottom)

time: 191 us -> 188 us (0.984)
  transfers between devices with their start and end apart: 13 -> 13, of which waited for: 4 -> 3; matrix products, arithmetic and copies ran while one was open for 0% -> 0% of each run, Pallas kernels for 33% -> 35%
where the time goes in v5:
time: 188 us; the launch traced here: 185 us
  Pallas kernels  76.5 us (41%)
  starting transfers between devices  72.8 us (39%)
  local copies, waits for them, and re-layouts  17.1 us (9%)
  waiting for transfers between devices  8.4 us (4%)
  blocking collectives  7.94 us (4%)
    pallas_call x2, Pallas kernels, after(): pl.pallas_call(lambda *refs: after_kernel(scale, begin, reps if last else...  37 us
    ppermute x6, starting transfers between devices, shift(): lax.ppermute(array, axis, [(i, (i + by * step) % number) for i in range(n...  21.3 us
    all_to_all x3, starting transfers between devices, swap(): lax.all_to_all(array, ('rep', 'tab'), 0, 0, axis_index_groups=groups_of(*...  17.7 us
    unnamed x64, local copies, waits for them, and re-layouts  17.1 us
    all_to_all x1, starting transfers between devices, on_device(): lax.all_to_all(grad_rows, 'tab', split_axis=0, concat_axis=0, tiled=True)  16.1 us
    pallas_call x1, Pallas kernels, before(): pl.pallas_call(before_kernel, grid=(I2,), in_specs=[whole(table), whole((...  12.3 us
    ppermute x1, starting transfers between devices, on_device(): other = lax.ppermute(sent, 'rep', [(i, i ^ 2) for i in range(16)])  12.2 us
    pallas_call x1, Pallas kernels, dense(): pl.pallas_call(lambda *refs: dense_kernel(count, *refs), out_shape=(jax.S...  8.81 us
  transfers between devices with their start and end apart: 13, of which 3 were waited for; matrix products, arithmetic and copies ran while one was open for 0% of the time, Pallas kernels for 35%

profile of v5, /device:TPU:1, one launch (start us, length us, event | category | flops | bytes accessed | tf_op | source)
XLA Modules:
  0.0 184.8 jit_solution(6046120740875301046)
XLA Ops:
  0.6 1.2 copy-done.4
  1.9 1.1 copy-done.5
  3.0 0.9 copy-done.6
  3.9 0.8 copy-done.17
  4.6 8.8 %dense.1 = (bf16[32,128,128]{2,1,0:T(8,128)(2,1)}, bf16[128,128]{1,0:T(8,128)(2,1)}, bf16[33,128,128]{2,1,0:T(8,128)(2,1)S(1)}) custom-call(bf16[128,128]{1,0:T(8,128)(2,1)S(1)} %copy-done.17, bf16[4096,128]{1,0:T(8,128)(2,1)S(1)} %bitcast.31, bf16[128,512]{1,0:T(8,128)(2,1)S(1)} %copy-done.6, bf16[656,512]{1,0:T(8,128)(2,1)S(1)} %copy-done.5), custom_call_target="tpu_custom_call" | custom-call | tf_op jit(solution)/shard_map/dense/pallas_call | solution.py:288
  13.4 16.1 %all-to-all-start = ((bf16[32,128,128]{2,1,0:T(8,128)(2,1)}), bf16[32,128,128]{2,1,0:T(8,128)(2,1)S(1)}, u32[]{:S(2)}, u32[]{:S(2)}) async-start(bf16[32,128,128]{2,1,0:T(8,128)(2,1)} %get-tuple-element.52), calls=%async_computation | async-start | bytes 2097152 | tf_op jit(solution)/shard_map/all_to_all | solution.py:502
  29.6 0.9 copy-done.7
  30.5 5.9 %gram.1 = (bf16[4,384,128]{2,1,0:T(8,128)(2,1)S(1)}, bf16[4,384,128]{2,1,0:T(8,128)(2,1)S(1)}) custom-call(s32[4]{0:T(128)S(1)} %pad_add_fusion.refs_0_.at_ref, bf16[33,128,128]{2,1,0:T(8,128)(2,1)S(1)} %get-tuple-element.44.refs_1_, bf16[128,512]{1,0:T(8,128)(2,1)S(1)} %copy-done.7), custom_call_target="tpu_custom_call" | custom-call | tf_op jit(solution)/shard_map/gram/pallas_call | solution.py:309
  36.4 0.7 copy-done.8
  37.2 2.9 %collective-permute-start = (bf16[4,384,128]{2,1,0:T(8,128)(2,1)S(1)}, bf16[4,384,128]{2,1,0:T(8,128)(2,1)S(1)}, u32[]{:S(2)}, u32[]{:S(2)}) collective-permute-start(bf16[4,384,128]{2,1,0:T(8,128)(2,1)S(1)} %get-tuple-element.46), channel_id=1, source_target_pairs={{0,32},{32,0},{64,96},{96,64},{128,160},{160,128},{192,224},{224,1... | collective-permute-start | bytes 1179656 | tf_op jit(solution)/shard_map/ppermute | solution.py:478
  40.0 1.3 collective-permute-done.came_ref
  41.3 0.7 copy-done.20
  42.1 1.9 %join_core.1 = (bf16[384,128]{1,0:T(8,128)(2,1)}, bf16[384,128]{1,0:T(8,128)(2,1)}, bf16[384,128]{1,0:T(8,128)(2,1)}, bf16[384,128]{1,0:T(8,128)(2,1)}) custom-call(bf16[4,384,128]{2,1,0:T(8,128)(2,1)} %copy-done.8, bf16[4,384,128]{2,1,0:T(8,128)(2,1)} %copy-done.20), custom_call_target="tpu_custom_call" | custom-call | tf_op jit(solution)/shard_map/join_core/pallas_call | solution.py:324
  44.0 3.1 %collective-permute-start.1 = (bf16[384,128]{1,0:T(8,128)(2,1)}, bf16[384,128]{1,0:T(8,128)(2,1)S(1)}, u32[]{:S(2)}, u32[]{:S(2)}) collective-permute-start(bf16[384,128]{1,0:T(8,128)(2,1)} %get-tuple-element.57), channel_id=1, source_target_pairs={{0,128},{32,160},{64,192},{96,224},{128,256},{160,288},{192,320},{... | collective-permute-start | bytes 294920 | tf_op jit(solution)/shard_map/ppermute | solution.py:474
  47.1 4.4 %collective-permute-start.2 = (bf16[384,128]{1,0:T(8,128)(2,1)}, bf16[384,128]{1,0:T(8,128)(2,1)S(1)}, u32[]{:S(2)}, u32[]{:S(2)}) collective-permute-start(bf16[384,128]{1,0:T(8,128)(2,1)} %get-tuple-element.58), channel_id=1, source_target_pairs={{0,256},{32,288},{64,320},{96,352},{128,384},{160,416},{192,448},{... | collective-permute-start | bytes 294920 | tf_op jit(solution)/shard_map/ppermute | solution.py:474
  51.5 3.1 %collective-permute-start.3 = (bf16[384,128]{1,0:T(8,128)(2,1)}, bf16[384,128]{1,0:T(8,128)(2,1)S(1)}, u32[]{:S(2)}, u32[]{:S(2)}) collective-permute-start(bf16[384,128]{1,0:T(8,128)(2,1)} %get-tuple-element.59), channel_id=1, source_target_pairs={{0,384},{32,416},{64,448},{96,480},{128,0},{160,32},{192,64},{224,... | collective-permute-start | bytes 294920 | tf_op jit(solution)/shard_map/ppermute | solution.py:474
  54.6 2.8 %collective-permute-done.3.d = bf16[384,128]{1,0:T(8,128)(2,1)S(1)} collective-permute-done((bf16[384,128]{1,0:T(8,128)(2,1)}, bf16[384,128]{1,0:T(8,128)(2,1)S(1)}, u32[]{:S(2)}, u32[]{:S(2)}) %collective-permute-start.3) | collective-permute-done | bytes 98336 | tf_op jit(solution)/shard_map/ppermute | solution.py:474
  57.3 0.6 copy-done.25
  58.0 1.7 join_x.1
  59.7 3.4 %collective-permute-start.4 = (bf16[96,128]{1,0:T(8,128)(2,1)}, bf16[96,128]{1,0:T(8,128)(2,1)S(1)}, u32[]{:S(2)}, u32[]{:S(2)}) collective-permute-start(bf16[96,128]{1,0:T(8,128)(2,1)} %get-tuple-element.61), channel_id=1, source_target_pairs={{0,8},{1,9},{2,10},{3,11},{4,12},{5,13},{6,14},{7,15},{8,16},{9,17... | collective-permute-start | bytes 73736 | tf_op jit(solution)/shard_map/ppermute | solution.py:474
  63.1 4.3 %collective-permute-start.5 = (bf16[96,128]{1,0:T(8,128)(2,1)}, bf16[96,128]{1,0:T(8,128)(2,1)S(1)}, u32[]{:S(2)}, u32[]{:S(2)}) collective-permute-start(bf16[96,128]{1,0:T(8,128)(2,1)} %get-tuple-element.62), channel_id=1, source_target_pairs={{0,16},{1,17},{2,18},{3,19},{4,20},{5,21},{6,22},{7,23},{8,24},{9,... | collective-permute-start | bytes 73736 | tf_op jit(solution)/shard_map/ppermute | solution.py:474
  67.5 3.1 %collective-permute-start.6 = (bf16[96,128]{1,0:T(8,128)(2,1)}, bf16[96,128]{1,0:T(8,128)(2,1)S(1)}, u32[]{:S(2)}, u32[]{:S(2)}) collective-permute-start(bf16[96,128]{1,0:T(8,128)(2,1)} %get-tuple-element.63), channel_id=1, source_target_pairs={{0,24},{1,25},{2,26},{3,27},{4,28},{5,29},{6,30},{7,31},{8,0},{9,1... | collective-permute-start | bytes 73736 | tf_op jit(solution)/shard_map/ppermute | solution.py:474
  70.8 1.8 digits.1.sorted_ref.refs_1_
  72.6 1.0 copy-done
  73.6 0.7 copy-done.11
  74.4 12.3 %before.1 = (bf16[256,4096]{1,0:T(8,128)(2,1)S(1)}, bf16[512,4096]{1,0:T(8,128)(2,1)}, bf16[1024,4096]{1,0:T(8,128)(2,1)}) custom-call(s32[32,128]{1,0:T(8,128)S(1)} %copy-done.11, bf16[256,128]{1,0:T(8,128)(2,1)S(1)} %bitcast.33, bf16[16,64,256]{2,1,0:T(8,128)(2,1)S(1)} %bitcast.27, bf16[512,128]{1,0:T(8,128)(2,1)S(1)} %bitcast.32), custom_call_target="tpu_custom_call" | custom-call | tf_op jit(solution)/shard_map/before/pallas_call | solution.py:379
  87.3 1.6 join_y.1
  88.9 9.2 %all-to-all-start.1 = ((bf16[16,96,128]{2,1,0:T(8,128)(2,1)}), bf16[16,96,128]{2,1,0:T(8,128)(2,1)}, u32[]{:S(2)}, u32[]{:S(2)}) async-start(bf16[16,96,128]{2,1,0:T(8,128)(2,1)} %join_y.1), calls=%async_computation.1 | async-start | bytes 786432 | tf_op jit(solution)/shard_map/all_to_all | solution.py:461
  98.2 1.0 copy-done.1
  99.2 0.7 copy-done.12
  99.9 18.4 %after.2 = (bf16[8,128,128]{2,1,0:T(8,128)(2,1)S(1)}, f32[256,128]{1,0:T(8,128)S(1)}, f32[512,128]{1,0:T(8,128)S(1)}) custom-call(s32[4096]{0:T(1024)S(1)} %bitcast.35, s32[32,128]{1,0:T(8,128)S(1)} %copy-done.12, bf16[4096,128]{1,0:T(8,128)(2,1)S(1)} %bitcast.25, bf16[256,4096]{1,0:T(8,128)(2,1)S(1)} %get-tuple-element.66.refs_3_, ...), custom_call_target="tpu_custom_call" | custom-call | tf_op jit(solution)/shard_map/after/pallas_call | solution.py:417
  118.4 0.7 copy-done.9
  119.1 0.6 copy-done.15
  119.7 1.8 join_z.1
  121.5 4.2 %all-to-all-start.2 = ((bf16[16,96,128]{2,1,0:T(8,128)(2,1)}), bf16[16,96,128]{2,1,0:T(8,128)(2,1)}, u32[]{:S(2)}, u32[]{:S(2)}) async-start(bf16[16,96,128]{2,1,0:T(8,128)(2,1)} %join_z.1), calls=%async_computation.2 | async-start | bytes 786432 | tf_op jit(solution)/shard_map/all_to_all | solution.py:461
  125.8 1.0 copy-done.2
  126.8 0.9 copy-done.10
  127.8 0.9 copy-done.16
  128.7 18.6 %after.3 = bf16[16,176,128]{2,1,0:T(8,128)(2,1)S(1)} custom-call(s32[4096]{0:T(1024)S(1)} %bitcast.36, s32[32,128]{1,0:T(8,128)S(1)} %copy-done.13, bf16[4096,128]{1,0:T(8,128)(2,1)S(1)} %bitcast.26, bf16[256,4096]{1,0:T(8,128)(2,1)S(1)} %get-tuple-element.66.refs_3_, bf16[512,4096]{1,0:T(8,128)(2,1)} %get-tuple-element.67.refs_4_, ...), custom_call_target="tpu_custom_call" | custom-call | tf_op jit(solution)/shard_map/after/pallas_call | solution.py:417
  147.3 0.9 copy-done.3
  148.1 7.9 %all_to_all.25 = bf16[2,8,176,128]{3,2,1,0:T(8,128)(2,1)S(1)} all-to-all(bf16[2,8,176,128]{3,2,1,0:T(8,128)(2,1)} %bitcast.30), channel_id=1, replica_groups={{0,32},{1,33},{2,34},{3,35},{4,36},{5,37},{6,38},{7,39},{8,40},{9,41},{..., dimensions={0} | all-to-all | bytes 1441792 | tf_op jit(solution)/shard_map/all_to_all | solution.py:461
  156.1 0.9 reduce_sum.21
  157.0 4.3 %all-to-all-start.4 = ((bf16[4,2,176,128]{3,2,1,0:T(8,128)(2,1)}), bf16[4,2,176,128]{3,2,1,0:T(8,128)(2,1)S(1)}, u32[]{:S(2)}, u32[]{:S(2)}) async-start(bf16[4,2,176,128]{3,2,1,0:T(8,128)(2,1)} %bitcast.17), calls=%async_computation.4 | async-start | bytes 720896 | tf_op jit(solution)/shard_map/all_to_all | solution.py:461
  161.3 2.5 %collective-permute-start.7 = (bf16[4,384,128]{2,1,0:T(8,128)(2,1)}, bf16[4,384,128]{2,1,0:T(8,128)(2,1)S(1)}, u32[]{:S(2)}, u32[]{:S(2)}) collective-permute-start(bf16[4,384,128]{2,1,0:T(8,128)(2,1)} %bitcast.15.mine_ref), channel_id=1, source_target_pairs={{0,32},{32,0},{64,96},{96,64},{128,160},{160,128},{192,224},{224,1... | collective-permute-start | bytes 1179656 | tf_op jit(solution)/shard_map/ppermute | solution.py:478
  163.8 4.3 %all-to-all-done.4 = bf16[4,2,176,128]{3,2,1,0:T(8,128)(2,1)S(1)} async-done(((bf16[4,2,176,128]{3,2,1,0:T(8,128)(2,1)}), bf16[4,2,176,128]{3,2,1,0:T(8,128)(2,1)S(1)}, u32[]{:S(2)}, u32[]{:S(2)}) %all-to-all-start.4) | async-done | bytes 360480 | tf_op jit(solution)/shard_map/all_to_all | solution.py:461
  168.2 12.2 %collective-permute-start.8 = (bf16[176,128]{1,0:T(8,128)(2,1)S(1)}, bf16[176,128]{1,0:T(8,128)(2,1)S(1)}, u32[]{:S(2)}, u32[]{:S(2)}) collective-permute-start(bf16[176,128]{1,0:T(8,128)(2,1)S(1)} %fusion), channel_id=1, source_target_pairs={{0,64},{32,96},{64,0},{96,32},{128,192},{160,224},{192,128},{224,1... | collective-permute-start | bytes 135176 | tf_op jit(solution)/shard_map/ppermute | solution.py:534
  180.5 2.1 %assemble.1 = bf16[656,512]{1,0:T(8,128)(2,1)} custom-call(s32[4]{0:T(128)} %copy-done.18, bf16[4,384,128]{2,1,0:T(8,128)(2,1)} %bitcast.15.mine_ref, bf16[4,384,128]{2,1,0:T(8,128)(2,1)} %copy-done.21), custom_call_target="tpu_custom_call" | custom-call | tf_op jit(solution)/shard_map/assemble/pallas_call | solution.py:363
  183.2 1.6 last_sum.1
  (59 shorter events, 1.7 us)
Async XLA Ops:
  0.6 1.2 copy-start.4
  1.9 1.1 copy-start.5
  3.0 0.9 copy-start.6
  3.9 0.8 copy-start.17
  4.6 65.9 %copy-start.26 = (bf16[1,128,256]{2,1,0:T(8,128)(2,1)S(1)}, bf16[1,128,256]{2,1,0:T(8,128)(2,1)}, u32[]{:S(2)}) copy-start(bf16[1,128,256]{2,1,0:T(8,128)(2,1)} %param.14) | copy-start | bytes 196612
  4.6 66.1 %copy-start.22 = (bf16[1,128,512]{2,1,0:T(8,128)(2,1)S(1)}, bf16[1,128,512]{2,1,0:T(8,128)(2,1)}, u32[]{:S(2)}) copy-start(bf16[1,128,512]{2,1,0:T(8,128)(2,1)} %param.16) | copy-start | bytes 393220
  4.6 93.5 %copy-start.14 = (s32[1,1,4096]{2,1,0:T(1,128)S(1)}, s32[1,1,4096]{2,1,0:T(1,128)}, u32[]{:S(2)}) copy-start(s32[1,1,4096]{2,1,0:T(1,128)} %param.19) | copy-start | bytes 49156
  13.4 75.5 %all-to-all-start = ((bf16[32,128,128]{2,1,0:T(8,128)(2,1)}), bf16[32,128,128]{2,1,0:T(8,128)(2,1)S(1)}, u32[]{:S(2)}, u32[]{:S(2)}) async-start(bf16[32,128,128]{2,1,0:T(8,128)(2,1)} %get-tuple-element.52), calls=%async_computation | async-start | bytes 2097152 | tf_op jit(solution)/shard_map/all_to_all | solution.py:502
  29.6 27.7 %copy-start.18 = (s32[4]{0:T(128)}, s32[4]{0:T(128)S(1)}, u32[]{:S(2)}) copy-start(s32[4]{0:T(128)S(1)} %pad_add_fusion.refs_0_.at_ref) | copy-start | bytes 52
  29.6 0.9 copy-start.7
  36.4 0.7 copy-start.8
  37.2 4.2 %collective-permute-start = (bf16[4,384,128]{2,1,0:T(8,128)(2,1)S(1)}, bf16[4,384,128]{2,1,0:T(8,128)(2,1)S(1)}, u32[]{:S(2)}, u32[]{:S(2)}) collective-permute-start(bf16[4,384,128]{2,1,0:T(8,128)(2,1)S(1)} %get-tuple-element.46), channel_id=1, source_target_pairs={{0,32},{32,0},{64,96},{96,64},{128,160},{160,128},{192,224},{224,1... | collective-permute-start | bytes 1179656 | tf_op jit(solution)/shard_map/ppermute | solution.py:478
  41.3 0.7 copy-start.20
  44.0 10.5 %collective-permute-start.1 = (bf16[384,128]{1,0:T(8,128)(2,1)}, bf16[384,128]{1,0:T(8,128)(2,1)S(1)}, u32[]{:S(2)}, u32[]{:S(2)}) collective-permute-start(bf16[384,128]{1,0:T(8,128)(2,1)} %get-tuple-element.57), channel_id=1, source_target_pairs={{0,128},{32,160},{64,192},{96,224},{128,256},{160,288},{192,320},{... | collective-permute-start | bytes 294920 | tf_op jit(solution)/shard_map/ppermute | solution.py:474
  47.1 7.5 %collective-permute-start.2 = (bf16[384,128]{1,0:T(8,128)(2,1)}, bf16[384,128]{1,0:T(8,128)(2,1)S(1)}, u32[]{:S(2)}, u32[]{:S(2)}) collective-permute-start(bf16[384,128]{1,0:T(8,128)(2,1)} %get-tuple-element.58), channel_id=1, source_target_pairs={{0,256},{32,288},{64,320},{96,352},{128,384},{160,416},{192,448},{... | collective-permute-start | bytes 294920 | tf_op jit(solution)/shard_map/ppermute | solution.py:474
  51.5 5.9 %collective-permute-start.3 = (bf16[384,128]{1,0:T(8,128)(2,1)}, bf16[384,128]{1,0:T(8,128)(2,1)S(1)}, u32[]{:S(2)}, u32[]{:S(2)}) collective-permute-start(bf16[384,128]{1,0:T(8,128)(2,1)} %get-tuple-element.59), channel_id=1, source_target_pairs={{0,384},{32,416},{64,448},{96,480},{128,0},{160,32},{192,64},{224,... | collective-permute-start | bytes 294920 | tf_op jit(solution)/shard_map/ppermute | solution.py:474
  54.5 2.8 %copy-start.23 = (bf16[384,128]{1,0:T(8,128)(2,1)}, bf16[384,128]{1,0:T(8,128)(2,1)S(1)}, u32[]{:S(2)}) copy-start(bf16[384,128]{1,0:T(8,128)(2,1)S(1)} %collective-permute-done.1.b) | copy-start | bytes 294916
  54.6 2.8 %copy-start.24 = (bf16[384,128]{1,0:T(8,128)(2,1)}, bf16[384,128]{1,0:T(8,128)(2,1)S(1)}, u32[]{:S(2)}) copy-start(bf16[384,128]{1,0:T(8,128)(2,1)S(1)} %collective-permute-done.2.c) | copy-start | bytes 294916
  57.3 0.6 copy-start.25
  59.7 27.0 %collective-permute-start.4 = (bf16[96,128]{1,0:T(8,128)(2,1)}, bf16[96,128]{1,0:T(8,128)(2,1)S(1)}, u32[]{:S(2)}, u32[]{:S(2)}) collective-permute-start(bf16[96,128]{1,0:T(8,128)(2,1)} %get-tuple-element.61), channel_id=1, source_target_pairs={{0,8},{1,9},{2,10},{3,11},{4,12},{5,13},{6,14},{7,15},{8,16},{9,17... | collective-permute-start | bytes 73736 | tf_op jit(solution)/shard_map/ppermute | solution.py:474
  63.1 23.6 %collective-permute-start.5 = (bf16[96,128]{1,0:T(8,128)(2,1)}, bf16[96,128]{1,0:T(8,128)(2,1)S(1)}, u32[]{:S(2)}, u32[]{:S(2)}) collective-permute-start(bf16[96,128]{1,0:T(8,128)(2,1)} %get-tuple-element.62), channel_id=1, source_target_pairs={{0,16},{1,17},{2,18},{3,19},{4,20},{5,21},{6,22},{7,23},{8,24},{9,... | collective-permute-start | bytes 73736 | tf_op jit(solution)/shard_map/ppermute | solution.py:474
  67.5 19.2 %collective-permute-start.6 = (bf16[96,128]{1,0:T(8,128)(2,1)}, bf16[96,128]{1,0:T(8,128)(2,1)S(1)}, u32[]{:S(2)}, u32[]{:S(2)}) collective-permute-start(bf16[96,128]{1,0:T(8,128)(2,1)} %get-tuple-element.63), channel_id=1, source_target_pairs={{0,24},{1,25},{2,26},{3,27},{4,28},{5,29},{6,30},{7,31},{8,0},{9,1... | collective-permute-start | bytes 73736 | tf_op jit(solution)/shard_map/ppermute | solution.py:474
  72.6 1.0 copy-start
  73.6 0.7 copy-start.11
  86.7 0.6 copy-start.28
  86.7 0.6 copy-start.29
  86.7 0.6 copy-start.30
  88.9 30.8 %all-to-all-start.1 = ((bf16[16,96,128]{2,1,0:T(8,128)(2,1)}), bf16[16,96,128]{2,1,0:T(8,128)(2,1)}, u32[]{:S(2)}, u32[]{:S(2)}) async-start(bf16[16,96,128]{2,1,0:T(8,128)(2,1)} %join_y.1), calls=%async_computation.1 | async-start | bytes 786432 | tf_op jit(solution)/shard_map/all_to_all | solution.py:461
  98.2 1.0 copy-start.1
  99.2 0.7 copy-start.12
  99.9 25.8 %copy-start.13 = (s32[32,128]{1,0:T(8,128)S(1)}, s32[32,128]{1,0:T(8,128)}, u32[]{:S(2)}) copy-start(s32[32,128]{1,0:T(8,128)} %digits.1.sorted_ref.refs_1_) | copy-start | bytes 49156
  118.4 0.7 copy-start.9
  119.1 0.6 copy-start.15
  121.5 26.6 %all-to-all-start.2 = ((bf16[16,96,128]{2,1,0:T(8,128)(2,1)}), bf16[16,96,128]{2,1,0:T(8,128)(2,1)}, u32[]{:S(2)}, u32[]{:S(2)}) async-start(bf16[16,96,128]{2,1,0:T(8,128)(2,1)} %join_z.1), calls=%async_computation.2 | async-start | bytes 786432 | tf_op jit(solution)/shard_map/all_to_all | solution.py:461
  125.8 1.0 copy-start.2
  126.8 0.9 copy-start.10
  127.7 0.9 copy-start.16
  147.2 0.9 copy-start.3
  157.0 11.1 %all-to-all-start.4 = ((bf16[4,2,176,128]{3,2,1,0:T(8,128)(2,1)}), bf16[4,2,176,128]{3,2,1,0:T(8,128)(2,1)S(1)}, u32[]{:S(2)}, u32[]{:S(2)}) async-start(bf16[4,2,176,128]{3,2,1,0:T(8,128)(2,1)} %bitcast.17), calls=%async_computation.4 | async-start | bytes 720896 | tf_op jit(solution)/shard_map/all_to_all | solution.py:461
  161.3 6.9 %collective-permute-start.7 = (bf16[4,384,128]{2,1,0:T(8,128)(2,1)}, bf16[4,384,128]{2,1,0:T(8,128)(2,1)S(1)}, u32[]{:S(2)}, u32[]{:S(2)}) collective-permute-start(bf16[4,384,128]{2,1,0:T(8,128)(2,1)} %bitcast.15.mine_ref), channel_id=1, source_target_pairs={{0,32},{32,0},{64,96},{96,64},{128,160},{160,128},{192,224},{224,1... | collective-permute-start | bytes 1179656 | tf_op jit(solution)/shard_map/ppermute | solution.py:478
  168.2 14.4 %copy-start.19 = (f32[2,176,128]{2,1,0:T(8,128)}, f32[2,176,128]{2,1,0:T(8,128)S(1)}, u32[]{:S(2)}) copy-start(f32[2,176,128]{2,1,0:T(8,128)S(1)} %convert_reduce_fusion.parts_ref) | copy-start | bytes 540676
  168.2 12.3 %copy-start.21 = (bf16[4,384,128]{2,1,0:T(8,128)(2,1)}, bf16[4,384,128]{2,1,0:T(8,128)(2,1)S(1)}, u32[]{:S(2)}) copy-start(bf16[4,384,128]{2,1,0:T(8,128)(2,1)S(1)} %collective-permute-done.7.other_ref) | copy-start | bytes 1179652
  168.2 14.4 %collective-permute-start.8 = (bf16[176,128]{1,0:T(8,128)(2,1)S(1)}, bf16[176,128]{1,0:T(8,128)(2,1)S(1)}, u32[]{:S(2)}, u32[]{:S(2)}) collective-permute-start(bf16[176,128]{1,0:T(8,128)(2,1)S(1)} %fusion), channel_id=1, source_target_pairs={{0,64},{32,96},{64,0},{96,32},{128,192},{160,224},{192,128},{224,1... | collective-permute-start | bytes 135176 | tf_op jit(solution)/shard_map/ppermute | solution.py:534
  182.6 0.6 copy-start.27
